TPU v7x, 32 devices: a whole 2x2x4 slice. The times are simulated.
32 devices in a mesh: grp: 2 (over y), tp: 4 (over z), req: 2 (over x), kv: 2 (over core).
Axes of the slice: x: 2, y: 2, z: 4, core: 2. Of those that a mesh axis runs over, the one named last changes fastest.
Arguments:
- tokens: bfloat16 [8, 128, 8192], P(('grp', 'req', 'kv'), 'tp'), parts along dimension 0, may hold values from -6 to 6
- norm_gain: bfloat16 [8192], replicated, may hold values from 0.3984375 to 1.59375
- w_query: bfloat16 [8192, 8192], P(('req', 'kv'), 'tp'), may hold values from -0.0625 to 0.0625
- w_key: bfloat16 [8192, 1024], P(('req', 'kv'), 'tp'), may hold values from -0.125 to 0.125
- w_value: bfloat16 [8192, 1024], P(('req', 'kv'), 'tp'), may hold values from -0.0625 to 0.0625
- w_out: bfloat16 [8192, 8192], P('tp', ('req', 'kv')), may hold values from -0.0625 to 0.0625
- cache_keys: bfloat16 [64, 64, 1024], P(('grp', 'req', 'kv')), parts along dimension 0, may hold values from -240 to 240
- cache_values: bfloat16 [64, 64, 1024], P(('grp', 'req', 'kv')), parts along dimension 0, may hold values from -6 to 6
- seg_ids: int32 [8, 128], P('grp'), parts along dimension 0, may hold values from 0 to 1, never falling along the last dimension, each value on 1 to 96 neighbouring positions
- block_ids: int32 [8, 2, 8], P('grp'), parts along dimension 0, may hold values from -1 to 31, as said below
Outputs:
- scored: bfloat16 [8, 128, 8192], P(('grp', 'req', 'kv'), 'tp'), parts along dimension 0
There are 2 independent parts, one for each index of `grp`. A program takes and returns all parts, laid end to end along the dimension named above; an argument that names none is the same for every part. Nothing has to cross between parts.
Inputs may be any that keep to these rules, and one draw needn't show every extreme that they name: `block_ids`: slots 0 to 3 of every step hold blocks 0 to 3; the next slots hold the first 1 to 4 blocks of one branch l, ids 4 + l * 4 + j in order of j; the rest are -1. The first step of every group holds 8 blocks.
All inputs are finite; a program needn't handle non-finite values.
Results may differ from a plain program's by a relative error of at most 0.03.
Values may be sent and summed in bfloat16 or wider, within the bound.
No kernel may reach another device: no remote copies, remote signals or barrier semaphores. Data moves between devices by JAX's collectives and lax.ppermute only.
A program may use at most 192 MiB of HBM per device.

v0:
```python
import jax
import jax.numpy as jnp
from jax import lax
from jax.sharding import PartitionSpec as P

HQ = 64
KVH = 8
HD = 128


EPS = 1e-06


def swapped(block, axis, distance):
    count = lax.axis_size(axis)
    route = []
    for low in range(count):
        high = low | 1 << distance
        if high != low and high < count:
            route += [(low, high), (high, low)]
    return lax.ppermute(block, axis, route)


def combined_all(shard, axis, join):
    gathered = jax.tree.map(
        lambda a, kind: lax.all_gather(a.astype(kind), axis),
        shard,
        jax.tree.map(lambda a: jnp.bfloat16 if a.dtype == jnp.float32 else a.dtype, shard),
    )

    def take(source):
        return jax.tree.map(
            lambda a, own: lax.dynamic_index_in_dim(a, source, 0, False).astype(own.dtype),
            gathered,
            shard,
        )

    return lax.fori_loop(
        1, lax.axis_size(axis), lambda source, state: join(state, take(source)), take(0)
    )


def partial_attend(heads, keys, values, allowed, scale):
    scores = jnp.einsum("rkgd,nkd->rkgn", heads, keys, preferred_element_type=jnp.float32) * scale
    wide_mask = allowed[:, None, None, :]
    scores = jnp.where(wide_mask, scores, -1e30)
    top = jnp.max(scores, axis=-1)
    weights = jnp.where(wide_mask, jnp.exp(scores - top[..., None]), 0.0)
    total = jnp.sum(weights, axis=-1)
    summed = jnp.einsum(
        "rkgn,nkd->rkgd", weights.astype(jnp.bfloat16), values, preferred_element_type=jnp.float32
    )
    return (top, total, summed)


def combine(first, second):
    top = jnp.maximum(first[0], second[0])
    left = jnp.exp(first[0] - top)
    right = jnp.exp(second[0] - top)
    return (
        top,
        first[1] * left + second[1] * right,
        first[2] * left[..., None] + second[2] * right[..., None],
    )


def on_device(
    tokens, norm_gain, w_query, w_key, w_value, w_out, cache_keys, cache_values, seg_ids, block_ids
):
    groups = seg_ids.shape[0]
    rows = seg_ids.shape[1]
    steps = block_ids.shape[1]
    group = lax.axis_index(("req", "kv"))
    tp_index = lax.axis_index("tp")
    head_dim = HD
    gsize = HQ // KVH
    local_heads = w_query.shape[1] // head_dim
    per_kv = min(gsize, local_heads)
    kv_count = local_heads // per_kv
    first_kv = tp_index * local_heads // gsize
    scale = head_dim ** (-0.5)
    blocks_here = cache_keys.shape[0]
    block_len = cache_keys.shape[1]
    blocks_all = blocks_here * groups
    wide = tokens[0].astype(jnp.float32)
    normed = (
        wide
        * lax.rsqrt(jnp.mean(wide * wide, axis=-1, keepdims=True) + EPS)
        * norm_gain.astype(jnp.float32)
    ).astype(jnp.bfloat16)
    whole = lax.all_gather(normed, "tp", axis=0, tiled=True)
    pieces = (
        lax.all_gather(w_query, ("req", "kv"), axis=0, tiled=True),
        lax.all_gather(w_key, ("req", "kv"), axis=0, tiled=True),
        lax.all_gather(w_value, ("req", "kv"), axis=0, tiled=True),
    )
    query_acc, key_acc, value_acc = tuple(
        (jnp.dot(whole, piece, preferred_element_type=jnp.float32) for piece in pieces)
    )
    queries = query_acc.astype(jnp.bfloat16)
    span = max(1, gsize // local_heads)
    stacked = jnp.stack((key_acc.astype(jnp.bfloat16), value_acc.astype(jnp.bfloat16)))
    for bit in range(span.bit_length() - 1):
        partner = swapped(stacked, "tp", bit)
        upper = tp_index // (1 << bit) % 2 == 1
        stacked = jnp.where(
            upper, jnp.concatenate((partner, stacked), 2), jnp.concatenate((stacked, partner), 2)
        )
    own_keys = stacked[0].reshape(rows, kv_count, head_dim)
    own_values = stacked[1].reshape(rows, kv_count, head_dim)
    heads = queries.reshape(rows, kv_count, per_kv, head_dim)
    member = jnp.any(
        block_ids[..., None] == jnp.arange(blocks_all, dtype=jnp.int32), axis=-2
    ).astype(jnp.float32)
    onehot = (seg_ids[..., None] == jnp.arange(steps, dtype=jnp.int32)).astype(jnp.float32)
    block_mask = jnp.einsum("grs,gsb->grb", onehot, member) > 0.5
    seg_here = lax.dynamic_index_in_dim(seg_ids, group, 0, keepdims=False)
    places = jnp.arange(rows, dtype=jnp.int32)
    own_mask = (seg_here[:, None] == seg_here[None, :]) & (places[:, None] >= places[None, :])
    own_part = partial_attend(heads, own_keys, own_values, own_mask, scale)
    gathered = lax.all_gather(queries[None], ("req", "kv"), axis=0, tiled=True)
    all_heads = gathered.reshape(groups * rows, kv_count, per_kv, head_dim)
    local_keys = lax.dynamic_slice_in_dim(
        cache_keys, first_kv * head_dim, kv_count * head_dim, 2
    ).reshape(blocks_here * block_len, kv_count, head_dim)
    local_values = lax.dynamic_slice_in_dim(
        cache_values, first_kv * head_dim, kv_count * head_dim, 2
    ).reshape(blocks_here * block_len, kv_count, head_dim)
    local_blocks = lax.dynamic_slice_in_dim(
        block_mask, group * blocks_here, blocks_here, 2
    ).reshape(groups * rows, blocks_here)
    local_mask = jnp.repeat(local_blocks, block_len, axis=1)
    cache_part = partial_attend(all_heads, local_keys, local_values, local_mask, scale)
    merged = combined_all(cache_part, ("req", "kv"), combine)
    mine = tuple((lax.dynamic_slice_in_dim(item, group * rows, rows, 0) for item in merged))
    top, total, summed = combine(mine, own_part)
    attended = (
        (summed / total[..., None]).astype(jnp.bfloat16).reshape(rows, local_heads * head_dim)
    )
    out_full = lax.all_gather(w_out, ("req", "kv"), axis=1, tiled=True)
    branch = lax.psum_scatter(
        jnp.dot(attended, out_full, preferred_element_type=jnp.float32).astype(jnp.bfloat16),
        "tp",
        scatter_dimension=0,
        tiled=True,
    )
    return branch[None]


def solution(mesh):
    placed = (
        P(("grp", "req", "kv"), "tp", None),
        P(),
        P(("req", "kv"), "tp"),
        P(("req", "kv"), "tp"),
        P(("req", "kv"), "tp"),
        P("tp", ("req", "kv")),
        P(("grp", "req", "kv"), None, None),
        P(("grp", "req", "kv"), None, None),
        P("grp", None),
        P("grp", None, None),
    )
    return jax.shard_map(
        on_device,
        mesh=mesh,
        in_specs=placed,
        out_specs=P(("grp", "req", "kv"), "tp", None),
        check_vma=False,
    )
```

profile of v0, /device:TPU:0, one launch (start us, length us, event | category | flops | bytes accessed | tf_op | source)
XLA Modules:
  0.0 703.1 jit_solution(2923378047686696902)
XLA Ops:
  11.4 48.0 %all-gather.12.cloned.1.call-done = bf16[128,8192]{1,0:T(8,128)(2,1)} async-done(((bf16[32,8192]{1,0:T(8,128)(2,1)}), bf16[128,8192]{1,0:T(8,128)(2,1)}) %all-gather.12.cloned.1.call-update) | async-done | bytes 2097168 | tf_op jit(solution)/shard_map/all_gather | solution.py:91
  59.4 201.8 %all-gather.14.cloned.1.call-done = bf16[8192,2048]{1,0:T(8,128)(2,1)} async-done(((bf16[2048,2048]{1,0:T(8,128)(2,1)}), bf16[8192,2048]{1,0:T(8,128)(2,1)}) %all-gather.14.cloned.1.call-update) | async-done | bytes 33554448 | tf_op jit(solution)/shard_map/all_gather | solution.py:93
  261.2 16.5 %convolution_convert_fusion.1 = bf16[128,2048]{1,0:T(8,128)(2,1)} fusion(bf16[128,8192]{1,0:T(8,128)(2,1)} %all-gather.12.cloned.1.call-done, bf16[8192,2048]{1,0:T(8,128)(2,1)} %all-gather.14.cloned.1.call-done), kind=kOutput, calls=%fused_computation.16 | convolution fusion | flops 4295229440 | bytes 36175872 | tf_op jit(solution)/shard_map/dot_general | solution.py:98
  280.5 19.9 %all-gather.22.cloned.1.call-done = bf16[512,2048]{1,0:T(8,128)(2,1)} async-done(((bf16[128,2048]{1,0:T(8,128)(2,1)}), bf16[512,2048]{1,0:T(8,128)(2,1)}) %all-gather.22.cloned.1.call-update) | async-done | bytes 2097168 | tf_op jit(solution)/shard_map/all_gather | solution.py:121
  302.7 3.8 fusion.3
  306.5 6.9 copy-done
  313.5 5.7 convert_bitcast_fusion
  320.3 16.1 %all-gather.18.cloned.1.call-done = bf16[8192,256]{1,0:T(8,128)(2,1)} async-done(((bf16[2048,256]{1,0:T(8,128)(2,1)}), bf16[8192,256]{1,0:T(8,128)(2,1)}) %all-gather.18.cloned.1.call-update) | async-done | bytes 4194320 | tf_op jit(solution)/shard_map/all_gather | solution.py:95
  339.4 32.9 %all-gather.16.cloned.1.call-done = bf16[8192,256]{1,0:T(8,128)(2,1)} async-done(((bf16[2048,256]{1,0:T(8,128)(2,1)}), bf16[8192,256]{1,0:T(8,128)(2,1)}) %all-gather.16.cloned.1.call-update) | async-done | bytes 4194320 | tf_op jit(solution)/shard_map/all_gather | solution.py:94
  375.9 5.2 all-gather.1
  381.2 9.4 %fusion.5 = bf16[512,2,8]{0,2,1:T(8,128)(2,1)S(1)} fusion(f32[2,512,512,8]{2,1,3,0:T(8,128)} %copy-done, f32[512,2,8]{0,2,1:T(8,128)S(1)} %get-tuple-element.228, pred[512,512]{0,1:T(8,128)(4,1)S(1)} %bitcast.94), kind=kLoop, calls=%fused_computation.12 | loop fusion | flops 20963328 | bytes 17088512 | tf_op jit(solution)/shard_map/reduce_sum | solution.py:49
  390.6 5.6 all-gather.2
  396.1 36.2 %all-gather.24.cloned.1.call-done = bf16[2048,2,8,128]{0,3,2,1:T(8,128)(2,1)} async-done(((bf16[512,2,8,128]{0,3,2,1:T(8,128)(2,1)}), bf16[2048,2,8,128]{0,3,2,1:T(8,128)(2,1)}) %all-gather.24.cloned.1.call-update) | async-done | bytes 8388624 | tf_op jit(solution)/shard_map/all_gather | solution.py:26
  432.4 4.1 slice_convert_fusion
  436.5 5.7 copy.44
  442.1 14.4 %copy.63 = bf16[2048,2,8,128]{3,2,1,0:T(8,128)(2,1)} copy(bf16[2048,2,8,128]{0,3,2,1:T(8,128)(2,1)} %all-gather.24.cloned.1.call-done) | data formatting | bytes 16777216 | tf_op jit(solution)/shard_map/while | solution.py:38
  456.5 24.3 %while.19 = (s32[]{:T(128)}, f32[512,2,8]{0,2,1:T(8,128)S(1)}, f32[512,2,8]{0,2,1:T(8,128)S(1)}, f32[512,2,8,128]{3,2,1,0:T(8,128)}, bf16[4,512,2,8]{1,3,2,0:T(8...) while((s32[]{:T(128)}, f32[512,2,8]{0,2,1:T(8,128)S(1)}, ...), condition=%wide.region_5.6_spmd, body=%wide.region_4.5_spmd.sunk | while | flops 4259845 | bytes 10911895 | solution.py:38
  457.0 7.8 %fusion.63 = f32[512,2,8,128]{3,2,1,0:T(8,128)} fusion(f32[512,2,8,128]{3,2,1,0:T(8,128)} %get-tuple-element.298, f32[512,2,8]{2,1,0:T(2,128)S(1)} %copy.95, bf16[4,512,2,8,128]{4,3,2,1,0:T(8,128)(2,1)} %get-tuple-element.311, s32[]{:T(128)S(6)} %select_n.89, f32[512,2,8]{2,1,0:T(2,128)S(1)} %copy.96), kind=kLoop, calls=%fused_computation.1.clone.1 | loop fusion | flops 4194304 | bytes 10551300 | tf_op jit(solution)/shard_map/while/body/eval_jaxpr/add | solution.py:63
  465.3 7.5 %fusion.63 = f32[512,2,8,128]{3,2,1,0:T(8,128)} fusion(f32[512,2,8,128]{3,2,1,0:T(8,128)} %get-tuple-element.298, f32[512,2,8]{2,1,0:T(2,128)S(1)} %copy.95, bf16[4,512,2,8,128]{4,3,2,1,0:T(8,128)(2,1)} %get-tuple-element.311, s32[]{:T(128)S(6)} %select_n.89, f32[512,2,8]{2,1,0:T(2,128)S(1)} %copy.96), kind=kLoop, calls=%fused_computation.1.clone.1 | loop fusion | flops 4194304 | bytes 10551300 | tf_op jit(solution)/shard_map/while/body/eval_jaxpr/add | solution.py:63
  473.3 7.5 %fusion.63 = f32[512,2,8,128]{3,2,1,0:T(8,128)} fusion(f32[512,2,8,128]{3,2,1,0:T(8,128)} %get-tuple-element.298, f32[512,2,8]{2,1,0:T(2,128)S(1)} %copy.95, bf16[4,512,2,8,128]{4,3,2,1,0:T(8,128)(2,1)} %get-tuple-element.311, s32[]{:T(128)S(6)} %select_n.89, f32[512,2,8]{2,1,0:T(2,128)S(1)} %copy.96), kind=kLoop, calls=%fused_computation.1.clone.1 | loop fusion | flops 4194304 | bytes 10551300 | tf_op jit(solution)/shard_map/while/body/eval_jaxpr/add | solution.py:63
  480.8 5.4 copy.48
  487.8 147.7 %all-gather.20.cloned.1.call-done = bf16[2048,8192]{1,0:T(8,128)(2,1)} async-done(((bf16[2048,2048]{1,0:T(8,128)(2,1)}), bf16[2048,8192]{1,0:T(8,128)(2,1)}) %all-gather.20.cloned.1.call-update) | async-done | bytes 33554448 | tf_op jit(solution)/shard_map/all_gather | solution.py:140
  635.5 16.7 %convolution_convert_fusion = bf16[128,8192]{1,0:T(8,128)(2,1)} fusion(bf16[128,2048]{0,1:T(8,128)(2,1)S(1)} %bitcast.98, bf16[2048,8192]{1,0:T(8,128)(2,1)} %all-gather.20.cloned.1.call-done), kind=kOutput, calls=%fused_computation.13 | convolution fusion | flops 4296015872 | bytes 36175872 | tf_op jit(solution)/shard_map/dot_general | solution.py:142
  652.2 44.0 %reduce-scatter.2.cloned.1.call-done = bf16[32,8192]{1,0:T(8,128)(2,1)} async-done(((bf16[128,8192]{1,0:T(8,128)(2,1)}), bf16[32,8192]{1,0:T(8,128)(2,1)}) %reduce-scatter.2.cloned.1.call-update) | async-done | bytes 524304 | tf_op jit(solution)/shard_map/reduce_scatter | solution.py:141
  (62 shorter events, 20.6 us)
Async XLA Ops:
  6.5 52.8 %all-gather.12.cloned.1.call-start = ((), (), s32[]{:S(2)}) async-start(), calls=%async_computation.1 | async-start | bytes 2621440 | tf_op jit(solution)/shard_map/all_gather | solution.py:91
  10.6 250.6 %all-gather.14.cloned.1.call-start = ((), (), s32[]{:S(2)}) async-start(), calls=%async_computation.2 | async-start | bytes 41943040 | tf_op jit(solution)/shard_map/all_gather | solution.py:93
  11.3 289.1 %all-gather.22.cloned.1.call-start = ((), (), s32[]{:S(2)}) async-start(), calls=%async_computation.7 | async-start | bytes 2621440 | tf_op jit(solution)/shard_map/all_gather | solution.py:121
  277.7 2.5 copy-start.3
  277.7 2.6 copy-start.4
  277.7 58.7 %all-gather.18.cloned.1.call-start = ((), (), s32[]{:S(2)}) async-start(), calls=%async_computation.4 | async-start | bytes 5242880 | tf_op jit(solution)/shard_map/all_gather | solution.py:95
  278.3 94.0 %all-gather.16.cloned.1.call-start = ((), (), s32[]{:S(2)}) async-start(), calls=%async_computation.3 | async-start | bytes 5242880 | tf_op jit(solution)/shard_map/all_gather | solution.py:94
  278.9 153.5 %all-gather.24.cloned.1.call-start = ((), (), s32[]{:S(2)}) async-start(), calls=%async_computation.8 | async-start | bytes 10485760 | tf_op jit(solution)/shard_map/all_gather | solution.py:26
  306.5 7.0 copy-start
  319.2 17.2 %copy-start.1 = (bf16[128,8192]{1,0:T(8,128)(2,1)S(1)}, bf16[128,8192]{1,0:T(8,128)(2,1)}, u32[]{:S(2)}) copy-start(bf16[128,8192]{1,0:T(8,128)(2,1)} %all-gather.12.cloned.1.call-done) | copy-start | bytes 6291460
  319.2 316.3 %all-gather.20.cloned.1.call-start = ((), (), s32[]{:S(2)}) async-start(), calls=%async_computation.5 | async-start | bytes 41943040 | tf_op jit(solution)/shard_map/all_gather | solution.py:140
  319.9 376.3 %reduce-scatter.2.cloned.1.call-start = ((), (), s32[]{:S(2)}) async-start(), calls=%async_computation.6 | async-start | bytes 2621440 | tf_op jit(solution)/shard_map/reduce_scatter | solution.py:141
  339.3 35.9 %copy-start.2 = (bf16[128,2048]{1,0:T(8,128)(2,1)S(1)}, bf16[128,2048]{1,0:T(8,128)(2,1)}, u32[]{:S(2)}) copy-start(bf16[128,2048]{1,0:T(8,128)(2,1)} %convolution_convert_fusion.1) | copy-start | bytes 1572868
Sparse Core Ops, SparseCore 0:
  10.7 48.6 all-gather.11
  60.9 200.2 all-gather.13
  277.8 22.5 all-gather.21
  301.9 34.4 all-gather.17
  337.8 34.4 all-gather.15
  373.7 58.6 all-gather.23
  434.0 201.5 all-gather.19
  652.4 43.8 reduce-scatter.1
where the time goes:
time: 705 us; the launch traced here: 703 us
  waiting for transfers between devices  549 us (78%)
  matrix products  50.6 us (7%)
  other arithmetic  40.7 us (6%)
  local copies, waits for them, and re-layouts  37.5 us (5%)
  between operations  13.7 us (2%)
  blocking collectives  10.8 us (2%)
    all_gather x1, waiting for transfers between devices, on_device(): lax.all_gather(w_query, ('req', 'kv'), axis=0, tiled=True)  202 us
    all_gather x1, waiting for transfers between devices, on_device(): out_full = lax.all_gather(w_out, ('req', 'kv'), axis=1, tiled=True)  148 us
    all_gather x1, waiting for transfers between devices, on_device(): whole = lax.all_gather(normed, 'tp', axis=0, tiled=True)  48 us
    reduce_scatter x1, waiting for transfers between devices, on_device(): lax.psum_scatter(jnp.dot(attended, out_full, preferred_element_type=jnp.f...  44 us
    all_gather x1, waiting for transfers between devices, combined_all(): lax.all_gather(a.astype(kind), axis)  36.2 us
    all_gather x1, waiting for transfers between devices, on_device(): lax.all_gather(w_key, ('req', 'kv'), axis=0, tiled=True)  32.9 us
    while x3, local copies, waits for them, and re-layouts, combined_all(): lax.fori_loop(1, lax.axis_size(axis), lambda source, state: join(state, t...  25.4 us
    add x3, other arithmetic, combine(): first[2] * left[..., None] + second[2] * right[..., None]  22.8 us
  transfers between devices with their start and end apart: 8, of which 8 were waited for; matrix products, arithmetic and copies ran while one was open for 12% of the time, Pallas kernels for 0%

commit v1 on v0

--- a/solution.py
+++ b/solution.py
@@ -1,6 +1,10 @@
+import functools
+
 import jax
 import jax.numpy as jnp
 from jax import lax
+from jax.experimental import pallas as pl
+from jax.experimental.pallas import tpu as pltpu
 from jax.sharding import PartitionSpec as P
 
 HQ = 64
@@ -64,7 +68,7 @@
     )
 
 
-def on_device(
+def general_path(
     tokens, norm_gain, w_query, w_key, w_value, w_out, cache_keys, cache_values, seg_ids, block_ids
 ):
     groups = seg_ids.shape[0]
@@ -147,6 +151,353 @@
     return branch[None]
 
 
+SWAP = [(0, 1), (1, 0)]
+MASKED = -1e30
+
+
+def tp_ring(count):
+    return list(range(0, count, 2)) + list(range(1, count, 2))[::-1]
+
+
+def picked(index, options):
+    result = options[0]
+    for number, option in enumerate(options[1:], 1):
+        result = jnp.where(index == number, option, result)
+    return result
+
+
+def project_kernel(half_ref, x_ref, q_ref, k_ref, v_ref, out_ref):
+    tile = pl.program_id(0)
+    last = pl.num_programs(0) - 1
+    width = q_ref.shape[1]
+    head_dim = k_ref.shape[1]
+    x = x_ref[...]
+
+    @pl.when(tile < last)
+    def _():
+        product = jnp.dot(x, q_ref[...], preferred_element_type=jnp.float32)
+        at = pl.multiple_of(tile * width, width)
+        out_ref[:, pl.ds(at, width)] = product.astype(out_ref.dtype)
+
+    @pl.when(tile == last)
+    def _():
+        base = last * width
+        for number, ref in enumerate((k_ref, v_ref)):
+            product = jnp.dot(x, ref[...], preferred_element_type=jnp.float32)
+            at = base + number * head_dim
+            out_ref[:, at : at + head_dim] = product.astype(out_ref.dtype)
+
+
+def project(x, w_query, w_key, w_value, half, kind):
+    rows, depth = x.shape
+    q_cols = w_query.shape[1] // 2
+    kv_cols = w_key.shape[1] // 2
+    width = 256
+    tiles = q_cols // width
+    total = q_cols + 2 * kv_cols
+    grid_spec = pltpu.PrefetchScalarGridSpec(
+        num_scalar_prefetch=1,
+        grid=(tiles + 1,),
+        in_specs=[
+            pl.BlockSpec((rows, depth), lambda t, h: (0, 0)),
+            pl.BlockSpec(
+                (depth, width), lambda t, h: (0, h[0] * tiles + jnp.minimum(t, tiles - 1))
+            ),
+            pl.BlockSpec((depth, kv_cols), lambda t, h: (0, h[0])),
+            pl.BlockSpec((depth, kv_cols), lambda t, h: (0, h[0])),
+        ],
+        out_specs=pl.BlockSpec((rows, total), lambda t, h: (0, 0)),
+    )
+    return pl.pallas_call(
+        project_kernel,
+        grid_spec=grid_spec,
+        out_shape=jax.ShapeDtypeStruct((rows, total), kind),
+        compiler_params=pltpu.CompilerParams(vmem_limit_bytes=32 * 2**20),
+        cost_estimate=pl.CostEstimate(
+            flops=2 * rows * depth * total,
+            bytes_accessed=2 * depth * total + 2 * rows * depth + 4 * rows * total,
+            transcendentals=0,
+        ),
+        name="project",
+    )(half, x, w_query, w_key, w_value)
+
+
+def out_kernel(half_ref, own_ref, other_ref, w_ref, out_ref):
+    depth = own_ref.shape[1]
+    mine = half_ref[0]
+    at = pl.multiple_of(mine * depth, depth)
+    off = pl.multiple_of((1 - mine) * depth, depth)
+    product = jnp.dot(own_ref[...], w_ref[pl.ds(at, depth), :], preferred_element_type=jnp.float32)
+    product += jnp.dot(
+        other_ref[...], w_ref[pl.ds(off, depth), :], preferred_element_type=jnp.float32
+    )
+    out_ref[...] = product.astype(out_ref.dtype)
+
+
+def out_project(own, other, w_out, half):
+    rows, depth = own.shape
+    columns = w_out.shape[1]
+    width = 256
+    grid_spec = pltpu.PrefetchScalarGridSpec(
+        num_scalar_prefetch=1,
+        grid=(columns // width,),
+        in_specs=[
+            pl.BlockSpec((rows, depth), lambda t, h: (0, 0)),
+            pl.BlockSpec((rows, depth), lambda t, h: (0, 0)),
+            pl.BlockSpec((2 * depth, width), lambda t, h: (0, t)),
+        ],
+        out_specs=pl.BlockSpec((rows, width), lambda t, h: (0, t)),
+    )
+    return pl.pallas_call(
+        out_kernel,
+        grid_spec=grid_spec,
+        out_shape=jax.ShapeDtypeStruct((rows, columns), jnp.bfloat16),
+        compiler_params=pltpu.CompilerParams(vmem_limit_bytes=32 * 2**20),
+        cost_estimate=pl.CostEstimate(
+            flops=4 * rows * depth * columns,
+            bytes_accessed=4 * depth * columns + 4 * rows * depth + 2 * rows * columns,
+            transcendentals=0,
+        ),
+        name="out_project",
+    )(half, own, other, w_out)
+
+
+def attend_kernel(
+    pieces, groups, steps, info_ref, keep_ref, come_ref, ck_ref, cv_ref, out_ref
+):
+    rows_all, total_cols = keep_ref.shape
+    part = rows_all // (pieces * groups)
+    rows = part * pieces
+    head_dim = ck_ref.shape[1]
+    heads = total_cols // head_dim - 2
+    scale = head_dim**-0.5
+    place = lax.broadcasted_iota(jnp.int32, (rows, rows), 0)
+    across = lax.broadcasted_iota(jnp.int32, (rows, rows), 1)
+
+    def position(index):
+        piece = index // part
+        start = jnp.full(index.shape, info_ref[0], jnp.int32)
+        for j in range(1, pieces):
+            start = jnp.where(piece == j, info_ref[j], start)
+        return start * part + index % part
+
+    row_pos = position(place)
+    col_pos = position(across)
+    own_rows = []
+    for g in range(groups):
+        own_rows.append(
+            jnp.concatenate(
+                [
+                    (
+                        keep_ref[(j * groups + g) * part : (j * groups + g + 1) * part, :]
+                        + come_ref[(j * groups + g) * part : (j * groups + g + 1) * part, :].astype(
+                            jnp.float32
+                        )
+                    ).astype(jnp.bfloat16)
+                    for j in range(pieces)
+                ],
+                axis=0,
+            )
+        )
+    for g in range(groups):
+        qkv = own_rows[g]
+        q_cols = heads * head_dim
+        keys = [ck_ref[0:ROOT_KEYS, :]]
+        values = [cv_ref[0:ROOT_KEYS, :]]
+        bias = [jnp.zeros((rows, ROOT_KEYS), jnp.float32)]
+        same = None
+        for s in range(steps):
+            at = pieces + (g * steps + s) * 4
+            start, count = info_ref[at], info_ref[at + 1]
+            low, high = info_ref[at + 2], info_ref[at + 3]
+            begin = pl.multiple_of(start, CHAIN_KEYS)
+            keys.append(ck_ref[pl.ds(begin, CHAIN_KEYS), :])
+            values.append(cv_ref[pl.ds(begin, CHAIN_KEYS), :])
+            row_in = (row_pos >= low) & (row_pos < high)
+            col_in = (col_pos >= low) & (col_pos < high)
+            both = row_in & col_in
+            same = both if same is None else same | both
+            for piece in range(CHAIN_KEYS // rows):
+                allowed = row_in & (across + piece * rows < count)
+                bias.append(jnp.where(allowed, 0.0, MASKED))
+        keys.append(qkv[:, q_cols : q_cols + head_dim])
+        values.append(qkv[:, q_cols + head_dim :])
+        bias.append(jnp.where(same & (col_pos <= row_pos), 0.0, MASKED))
+        keys = jnp.concatenate(keys, axis=0)
+        values = jnp.concatenate(values, axis=0)
+        bias = jnp.concatenate(bias, axis=1)
+        for h in range(heads):
+            query = qkv[:, h * head_dim : (h + 1) * head_dim]
+            scores = lax.dot_general(
+                query, keys, (((1,), (1,)), ((), ())), preferred_element_type=jnp.float32
+            )
+            scores = scores * scale + bias
+            top = jnp.max(scores, axis=1, keepdims=True)
+            weights = jnp.exp(scores - top)
+            total = jnp.sum(weights, axis=1, keepdims=True)
+            summed = jnp.dot(
+                weights.astype(jnp.bfloat16), values, preferred_element_type=jnp.float32
+            )
+            result = (summed / total).astype(out_ref.dtype)
+            for j in range(pieces):
+                to = (j * groups + g) * part
+                out_ref[to : to + part, h * head_dim : (h + 1) * head_dim] = result[
+                    j * part : (j + 1) * part
+                ]
+
+
+def attend(keep, come, cache_k, cache_v, info, pieces, groups, steps):
+    rows, total = keep.shape
+    head_dim = cache_k.shape[1]
+    heads = total // head_dim - 2
+    per_group = rows // groups
+    keys = ROOT_KEYS + steps * CHAIN_KEYS + per_group
+    whole = pl.BlockSpec(memory_space=pltpu.VMEM)
+    return pl.pallas_call(
+        functools.partial(attend_kernel, pieces, groups, steps),
+        in_specs=[pl.BlockSpec(memory_space=pltpu.SMEM)] + [whole] * 4,
+        out_specs=whole,
+        out_shape=jax.ShapeDtypeStruct((rows, heads * head_dim), jnp.bfloat16),
+        compiler_params=pltpu.CompilerParams(vmem_limit_bytes=32 * 2**20),
+        cost_estimate=pl.CostEstimate(
+            flops=4 * rows * heads * keys * head_dim,
+            bytes_accessed=4 * cache_k.size + 6 * rows * total,
+            transcendentals=rows * heads * keys,
+        ),
+        name="attend",
+    )(info, keep, come, cache_k, cache_v)
+
+
+ROOT_BLOCKS = 4
+CHAIN_BLOCKS = 4
+BLOCK_KEYS = 64
+ROOT_KEYS = ROOT_BLOCKS * BLOCK_KEYS
+CHAIN_KEYS = CHAIN_BLOCKS * BLOCK_KEYS
+
+
+def on_device(
+    tokens, norm_gain, w_query, w_key, w_value, w_out, cache_keys, cache_values, seg_ids, block_ids
+):
+    req, kv, tp = lax.axis_index("req"), lax.axis_index("kv"), lax.axis_index("tp")
+    cores = 2
+    head_dim = HD
+    steps = block_ids.shape[1]
+    depth = w_query.shape[0]
+    part = tokens.shape[1]
+    blocks_here = cache_keys.shape[0]
+    count = lax.axis_size("tp")
+    order = tp_ring(count)
+    forward = [(order[i], order[(i + 1) % count]) for i in range(count)]
+    half = kv.astype(jnp.int32).reshape(1)
+    other = (1 - kv).astype(jnp.int32).reshape(1)
+
+    def swap_req(x):
+        return lax.ppermute(x, "req", SWAP)
+
+    def swap_kv(x):
+        return lax.ppermute(x, "kv", SWAP)
+
+    def onward(x):
+        return lax.ppermute(x, "tp", forward)
+
+    wide = tokens[0].astype(jnp.float32)
+    normed = (
+        wide
+        * lax.rsqrt(jnp.mean(wide * wide, axis=-1, keepdims=True) + EPS)
+        * norm_gain.astype(jnp.float32)
+    ).astype(jnp.bfloat16)
+    quarters = normed.reshape(part, 2, cores, depth)
+    kept = lax.dynamic_index_in_dim(quarters, kv, 2, False)
+    came = swap_kv(lax.dynamic_index_in_dim(quarters, 1 - kv, 2, False))
+    both = jnp.where(kv == 0, jnp.stack((kept, came)), jnp.stack((came, kept)))
+    near = lax.dynamic_index_in_dim(both, req, 2, False).reshape(cores * part, depth)
+    far = swap_req(
+        lax.dynamic_index_in_dim(both, 1 - req, 2, False).reshape(cores * part, depth)
+    )
+
+    def own_head(cache):
+        local = 2 * head_dim * tp
+        mine = lax.dynamic_slice_in_dim(cache, local + kv * head_dim, head_dim, 2)
+        give = lax.dynamic_slice_in_dim(cache, local + (1 - kv) * head_dim, head_dim, 2)
+        return mine, give
+
+    k_mine, k_give = own_head(cache_keys)
+    v_mine, v_give = own_head(cache_values)
+    c_mine = jnp.stack((k_mine, v_mine))
+    c_come = swap_kv(jnp.stack((k_give, v_give)))
+    chip = jnp.where(
+        kv == 0, jnp.stack((c_mine, c_come), 1), jnp.stack((c_come, c_mine), 1)
+    )
+    chip_far = swap_req(chip)
+    cached = jnp.where(req == 0, jnp.stack((chip, chip_far), 1), jnp.stack((chip_far, chip), 1))
+    cached = cached.reshape(2, 4 * blocks_here * BLOCK_KEYS, head_dim)
+
+    seg_near = lax.dynamic_slice_in_dim(seg_ids, req * cores, cores, 0)
+    ids_near = lax.dynamic_slice_in_dim(block_ids, req * cores, cores, 0)
+    here = jnp.arange(steps, dtype=jnp.int32)
+    low = jnp.sum(seg_near[:, None, :] < here[:, None], axis=-1, dtype=jnp.int32)
+    high = jnp.sum(seg_near[:, None, :] <= here[:, None], axis=-1, dtype=jnp.int32)
+    begin = ids_near[:, :, ROOT_BLOCKS] * BLOCK_KEYS
+    length = jnp.sum(ids_near[:, :, ROOT_BLOCKS:] >= 0, axis=-1, dtype=jnp.int32) * BLOCK_KEYS
+    spot = picked(tp, [order.index(i) for i in range(count)])
+    sources = [
+        picked((spot - j) % count, [jnp.int32(i) for i in order]) for j in range(count)
+    ]
+    info = jnp.concatenate(
+        (
+            jnp.stack(sources).astype(jnp.int32),
+            jnp.stack((begin, length, low, high), axis=-1).reshape(-1).astype(jnp.int32),
+        )
+    )
+
+    near_pieces, far_pieces = [near], [far]
+    for _ in range(count - 1):
+        near_pieces.append(onward(near_pieces[-1]))
+        far_pieces.append(onward(far_pieces[-1]))
+    far_rows = jnp.concatenate(far_pieces)
+    near_rows = jnp.concatenate(near_pieces)
+    weights = (w_query, w_key, w_value)
+    far_sent = swap_kv(project(far_rows, *weights, other, jnp.bfloat16))
+    far_kept = project(far_rows, *weights, half, jnp.float32)
+    come = swap_req((far_kept + far_sent.astype(jnp.float32)).astype(jnp.bfloat16))
+    near_sent = swap_kv(project(near_rows, *weights, other, jnp.bfloat16))
+    near_kept = project(near_rows, *weights, half, jnp.float32)
+    keep = near_kept + near_sent.astype(jnp.float32)
+
+    attended = attend(keep, come, cached[0], cached[1], info, count, cores, steps)
+
+    attended_far = swap_req(attended)
+    near_sum = out_project(attended, swap_kv(attended), w_out, half)
+    far_sum = out_project(attended_far, swap_kv(attended_far), w_out, half)
+
+    def summed(terms):
+        size = cores * part
+        chunk = [terms[j * size : (j + 1) * size] for j in range(count)]
+        running = onward(chunk[1])
+        for j in range(2, count):
+            running = onward(
+                (running.astype(jnp.float32) + chunk[j].astype(jnp.float32)).astype(jnp.bfloat16)
+            )
+        return (running.astype(jnp.float32) + chunk[0].astype(jnp.float32)).astype(jnp.bfloat16)
+
+    near_out = summed(near_sum)
+    far_out = swap_req(summed(far_sum))
+    columns = near_out.shape[1]
+    outs = jnp.stack(
+        (near_out.reshape(cores, part, columns), far_out.reshape(cores, part, columns)), 2
+    )
+    mine = lax.dynamic_index_in_dim(outs, kv, 0, False)
+    come_out = swap_kv(lax.dynamic_index_in_dim(outs, 1 - kv, 0, False))
+    chip_out = jnp.where(kv == 0, jnp.stack((mine, come_out), 2), jnp.stack((come_out, mine), 2))
+    scored = jnp.where(req == 0, chip_out, chip_out[:, ::-1])
+    return scored.reshape(1, part, 4 * columns)
+
+
+def fits(shape, args):
+    local_kv = KVH // shape["tp"]
+    return shape["req"] == 2 and shape["kv"] == 2 and shape["tp"] > 1 and local_kv == 2
+
+
 def solution(mesh):
     placed = (
         P(("grp", "req", "kv"), "tp", None),
@@ -161,7 +512,7 @@
         P("grp", None, None),
     )
     return jax.shard_map(
-        on_device,
+        on_device if fits(mesh.shape, None) else general_path,
         mesh=mesh,
         in_specs=placed,
         out_specs=P(("grp", "req", "kv"), "tp", None),

time: 705 us -> 155 us (0.22)
  waiting for transfers between devices: 549 us -> 73.5 us
  matrix products: 50.6 us -> 0 us
  other arithmetic: 40.7 us -> 3.49 us
  starting transfers between devices: 0.46 us -> 34.9 us
  Pallas kernels: 0 us -> 31.2 us
  local copies, waits for them, and re-layouts: 37.5 us -> 10.9 us
  between operations: 13.7 us -> 0.61 us
  blocking collectives: 10.8 us -> 0 us
    all_gather x7 -> x0, waiting for transfers between devices: 503 us -> none  [the longest x1 202 us: on_device(): lax.all_gather(w_query, ('req', 'kv'), axis=0, tiled=True)]
    ppermute x0 -> x24, waiting for transfers between devices: none -> 73.5 us  [the longest x12 45.7 us: onward(): return lax.ppermute(x, 'tp', forward)]
    dot_general x9 -> x0, matrix products: 50.6 us -> none  [the longest x3 22.3 us: on_device(): jnp.dot(whole, piece, preferred_element_type=jnp.float32)]
    reduce_scatter x1 -> x0, waiting for transfers between devices: 44 us -> none  [on_device(): lax.psum_scatter(jnp.dot(attended, out_full, preferred_element_type=jnp.f...]
    ppermute x0 -> x24, starting transfers between devices: none -> 34.9 us  [the longest x12 26.3 us: onward(): return lax.ppermute(x, 'tp', forward)]
    pallas_call x0 -> x7, Pallas kernels: none -> 31.2 us  [the longest x4 14.9 us: project(): pl.pallas_call(project_kernel, grid_spec=grid_spec, out_shape=jax.ShapeDt...]
    while x3 -> x0, local copies, waits for them, and re-layouts: 25.4 us -> none  [combined_all(): lax.fori_loop(1, lax.axis_size(axis), lambda source, state: join(state, t...]
    add x7 -> x1, other arithmetic: 22.9 us -> 0.14 us  [on_device(): keep = near_kept + near_sent.astype(jnp.float32)]
  transfers between devices with their start and end apart: 8 -> 24, of which waited for: 8 -> 16; matrix products, arithmetic and copies ran while one was open for 12% -> 2% of each run, Pallas kernels for 0% -> 16%
where the time goes in v1:
time: 155 us
  waiting for transfers between devices  73.5 us (47%)
  starting transfers between devices  34.9 us (23%)
  Pallas kernels  31.2 us (20%)
  local copies, waits for them, and re-layouts  10.9 us (7%)
  other arithmetic  3.49 us (2%)
    ppermute x12, waiting for transfers between devices, onward(): return lax.ppermute(x, 'tp', forward)  45.7 us
    ppermute x12, starting transfers between devices, onward(): return lax.ppermute(x, 'tp', forward)  26.3 us
    ppermute x5, waiting for transfers between devices, swap_req(): return lax.ppermute(x, 'req', SWAP)  24.8 us
    pallas_call x4, Pallas kernels, project(): pl.pallas_call(project_kernel, grid_spec=grid_spec, out_shape=jax.ShapeDt...  14.9 us
    pallas_call x2, Pallas kernels, out_project(): pl.pallas_call(out_kernel, grid_spec=grid_spec, out_shape=jax.ShapeDtypeS...  9.96 us
    ppermute x5, starting transfers between devices, swap_req(): return lax.ppermute(x, 'req', SWAP)  6.77 us
    pallas_call x1, Pallas kernels, attend(): pl.pallas_call(functools.partial(attend_kernel, pieces, groups, steps), i...  6.37 us
    unnamed x25, local copies, waits for them, and re-layouts  3.68 us
  transfers between devices with their start and end apart: 24, of which 16 were waited for; matrix products, arithmetic and copies ran while one was open for 2% of the time, Pallas kernels for 16%

profile of v1, /device:TPU:0, one launch (start us, length us, event | category | flops | bytes accessed | tf_op | source)
XLA Modules:
  0.0 154.7 jit_solution(2717812694881087601)
XLA Ops:
  8.7 4.1 %collective-permute-start.1 = (bf16[64,2048]{1,0:T(8,128)(2,1)S(1)}, bf16[64,2048]{1,0:T(8,128)(2,1)S(1)}, u32[]{:S(2)}, u32[]{:S(2)}) collective-permute-start(bf16[64,2048]{1,0:T(8,128)(2,1)S(1)} %bitcast.57), channel_id=1, source_target_pairs={{0,8},{8,12},{12,4},{4,0},{1,9},{9,13},{13,5},{5,1},{2,10},{10,14}... | collective-permute-start | bytes 786440 | tf_op jit(solution)/shard_map/ppermute | solution.py:401
  15.1 3.5 %collective-permute-done.1 = bf16[64,2048]{1,0:T(8,128)(2,1)S(1)} collective-permute-done((bf16[64,2048]{1,0:T(8,128)(2,1)S(1)}, bf16[64,2048]{1,0:T(8,128)(2,1)S(1)}, u32[]{:S(2)}, u32[]{:S(2)}) %collective-permute-start.1) | collective-permute-done | bytes 262176 | tf_op jit(solution)/shard_map/ppermute | solution.py:401
  18.6 3.4 %collective-permute-start.2 = (bf16[64,2048]{1,0:T(8,128)(2,1)S(1)}, bf16[64,2048]{1,0:T(8,128)(2,1)S(1)}, u32[]{:S(2)}, u32[]{:S(2)}) collective-permute-start(bf16[64,2048]{1,0:T(8,128)(2,1)S(1)} %collective-permute-done.1), channel_id=1, source_target_pairs={{0,8},{8,12},{12,4},{4,0},{1,9},{9,13},{13,5},{5,1},{2,10},{10,14}... | collective-permute-start | bytes 786440 | tf_op jit(solution)/shard_map/ppermute | solution.py:401
  23.7 8.8 %collective-permute-done.6 = bf16[64,2048]{1,0:T(8,128)(2,1)S(1)} collective-permute-done((bf16[64,2048]{1,0:T(8,128)(2,1)S(1)}, bf16[64,2048]{1,0:T(8,128)(2,1)S(1)}, u32[]{:S(2)}, u32[]{:S(2)}) %collective-permute-start.6) | collective-permute-done | bytes 262176 | tf_op jit(solution)/shard_map/ppermute | solution.py:401
  32.5 3.4 %collective-permute-start.7 = (bf16[64,2048]{1,0:T(8,128)(2,1)S(1)}, bf16[64,2048]{1,0:T(8,128)(2,1)S(1)}, u32[]{:S(2)}, u32[]{:S(2)}) collective-permute-start(bf16[64,2048]{1,0:T(8,128)(2,1)S(1)} %collective-permute-done.6), channel_id=1, source_target_pairs={{0,8},{8,12},{12,4},{4,0},{1,9},{9,13},{13,5},{5,1},{2,10},{10,14}... | collective-permute-start | bytes 786440 | tf_op jit(solution)/shard_map/ppermute | solution.py:401
  36.1 6.5 %collective-permute-done.7 = bf16[64,2048]{1,0:T(8,128)(2,1)S(1)} collective-permute-done((bf16[64,2048]{1,0:T(8,128)(2,1)S(1)}, bf16[64,2048]{1,0:T(8,128)(2,1)S(1)}, u32[]{:S(2)}, u32[]{:S(2)}) %collective-permute-start.7) | collective-permute-done | bytes 262176 | tf_op jit(solution)/shard_map/ppermute | solution.py:401
  42.6 3.4 %collective-permute-start.8 = (bf16[64,2048]{1,0:T(8,128)(2,1)S(1)}, bf16[64,2048]{1,0:T(8,128)(2,1)S(1)}, u32[]{:S(2)}, u32[]{:S(2)}) collective-permute-start(bf16[64,2048]{1,0:T(8,128)(2,1)S(1)} %collective-permute-done.7), channel_id=1, source_target_pairs={{0,8},{8,12},{12,4},{4,0},{1,9},{9,13},{13,5},{5,1},{2,10},{10,14}... | collective-permute-start | bytes 786440 | tf_op jit(solution)/shard_map/ppermute | solution.py:401
  46.0 5.0 %collective-permute-done.8 = bf16[64,2048]{1,0:T(8,128)(2,1)S(1)} collective-permute-done((bf16[64,2048]{1,0:T(8,128)(2,1)S(1)}, bf16[64,2048]{1,0:T(8,128)(2,1)S(1)}, u32[]{:S(2)}, u32[]{:S(2)}) %collective-permute-start.8) | collective-permute-done | bytes 262176 | tf_op jit(solution)/shard_map/ppermute | solution.py:401
  51.1 3.4 %copy-done.1 = bf16[2048,2048]{1,0:T(8,128)(2,1)S(1)} copy-done((bf16[2048,2048]{1,0:T(8,128)(2,1)S(1)}, bf16[2048,2048]{1,0:T(8,128)(2,1)}, u32[]{:S(2)}) %copy-start.1) | copy-done | bytes 8388632
  54.5 3.7 %project.7 = bf16[256,1280]{1,0:T(8,128)(2,1)S(1)} custom-call(s32[1]{0:T(128)} %bitcast.12.half_ref, bf16[256,2048]{1,0:T(8,128)(2,1)S(1)} %constant_dynamic-update-slice_fusion.x_ref, bf16[2048,2048]{1,0:T(8,128)(2,1)S(1)} %copy-done.1, bf16[2048,256]{1,0:T(8,128)(2,1)S(1)} %copy-done.2, bf16[2048,256]{1,0:T(8,128)(2,1)S(1)} %copy-done.3), custom_call_target="tpu_custom_call" | custom-call | flops 1342177280 | bytes 7602176 | tf_op jit(solution)/shard_map/project/pallas_call | solution.py:211
  58.5 3.7 %project.5 = bf16[256,1280]{1,0:T(8,128)(2,1)S(1)} custom-call(s32[1]{0:T(128)} %bitcast.12.half_ref, bf16[256,2048]{1,0:T(8,128)(2,1)S(1)} %pad_maximum_fusion.x_ref, bf16[2048,2048]{1,0:T(8,128)(2,1)S(1)} %bitcast.48, bf16[2048,256]{1,0:T(8,128)(2,1)S(1)} %copy-done.2, bf16[2048,256]{1,0:T(8,128)(2,1)S(1)} %copy-done.3), custom_call_target="tpu_custom_call" | custom-call | flops 1342177280 | bytes 7602176 | tf_op jit(solution)/shard_map/project/pallas_call | solution.py:211
  62.8 3.7 %project.6 = f32[256,1280]{1,0:T(8,128)S(1)} custom-call(s32[1]{0:T(128)} %bitcast.half_ref, bf16[256,2048]{1,0:T(8,128)(2,1)S(1)} %constant_dynamic-update-slice_fusion.x_ref, bf16[2048,2048]{1,0:T(8,128)(2,1)S(1)} %bitcast.48, bf16[2048,256]{1,0:T(8,128)(2,1)S(1)} %copy-done.2, bf16[2048,256]{1,0:T(8,128)(2,1)S(1)} %copy-done.3), custom_call_target="tpu_custom_call" | custom-call | flops 1342177280 | bytes 7602176 | tf_op jit(solution)/shard_map/project/pallas_call | solution.py:211
  68.3 3.7 %project.4 = f32[256,1280]{1,0:T(8,128)S(1)} custom-call(s32[1]{0:T(128)} %bitcast.half_ref, bf16[256,2048]{1,0:T(8,128)(2,1)S(1)} %pad_maximum_fusion.x_ref, bf16[2048,2048]{1,0:T(8,128)(2,1)S(1)} %bitcast.48, bf16[2048,256]{1,0:T(8,128)(2,1)S(1)} %copy-done.2, bf16[2048,256]{1,0:T(8,128)(2,1)S(1)} %copy-done.3), custom_call_target="tpu_custom_call" | custom-call | flops 1342177280 | bytes 7602176 | tf_op jit(solution)/shard_map/project/pallas_call | solution.py:211
  72.2 11.3 %collective-permute-done.10.come_ref = bf16[256,1280]{1,0:T(8,128)(2,1)S(1)} collective-permute-done((bf16[256,1280]{1,0:T(8,128)(2,1)S(1)}, bf16[256,1280]{1,0:T(8,128)(2,1)S(1)}, u32[]{:S(2)}, u32[]{:S(2)}) %collective-permute-start.10) | collective-permute-done | bytes 655392 | tf_op jit(solution)/shard_map/ppermute | solution.py:395
  83.5 6.4 %attend.1.own_ref = bf16[256,1024]{1,0:T(8,128)(2,1)S(1)} custom-call(s32[20]{0:T(128)S(1)} %concatenate.23.info_ref, f32[256,1280]{1,0:T(8,128)S(1)} %convert_add_fusion.keep_ref, bf16[256,1280]{1,0:T(8,128)(2,1)S(1)} %collective-permute-done.10.come_ref, bf16[2048,128]{1,0:T(8,128)(2,1)S(1)} %bitcast.52, bf16[2048,128]{1,0:T(8,128)(2,1)S(1)} %bitcast.51), custom_call_target="tpu_custom_call" | custom-call | flops 939524096 | bytes 3014656 | tf_op jit(solution)/shard_map/attend/pallas_call | solution.py:356
  91.4 11.5 %collective-permute-done.17.own_ref = bf16[256,1024]{1,0:T(8,128)(2,1)S(1)} collective-permute-done((bf16[256,1024]{1,0:T(8,128)(2,1)S(1)}, bf16[256,1024]{1,0:T(8,128)(2,1)S(1)}, u32[]{:S(2)}, u32[]{:S(2)}) %collective-permute-start.17) | collective-permute-done | bytes 524320 | tf_op jit(solution)/shard_map/ppermute | solution.py:395
  104.9 5.0 %out_project.3 = bf16[256,2048]{1,0:T(8,128)(2,1)S(1)} custom-call(s32[1]{0:T(128)} %bitcast.half_ref, bf16[256,1024]{1,0:T(8,128)(2,1)S(1)} %collective-permute-done.17.own_ref, bf16[256,1024]{1,0:T(8,128)(2,1)S(1)} %collective-permute-done.18.other_ref, bf16[2048,2048]{1,0:T(8,128)(2,1)S(1)} %bitcast.50), custom_call_target="tpu_custom_call" | custom-call | flops 2147483648 | bytes 10485760 | tf_op jit(solution)/shard_map/out_project/pallas_call | solution.py:251
  109.9 3.7 %collective-permute-start.19 = (bf16[64,2048]{1,0:T(8,128)(2,1)S(1)}, bf16[64,2048]{1,0:T(8,128)(2,1)S(1)}, u32[]{:S(2)}, u32[]{:S(2)}) collective-permute-start(bf16[64,2048]{1,0:T(8,128)(2,1)S(1)} %slice.56), channel_id=1, source_target_pairs={{0,8},{8,12},{12,4},{4,0},{1,9},{9,13},{13,5},{5,1},{2,10},{10,14}... | collective-permute-start | bytes 786440 | tf_op jit(solution)/shard_map/ppermute | solution.py:401
  113.5 5.0 %out_project.2 = bf16[256,2048]{1,0:T(8,128)(2,1)S(1)} custom-call(s32[1]{0:T(128)} %bitcast.half_ref, bf16[256,1024]{1,0:T(8,128)(2,1)S(1)} %attend.1.own_ref, bf16[256,1024]{1,0:T(8,128)(2,1)S(1)} %collective-permute-done.13.other_ref, bf16[2048,2048]{1,0:T(8,128)(2,1)S(1)} %bitcast.50), custom_call_target="tpu_custom_call" | custom-call | flops 2147483648 | bytes 10485760 | tf_op jit(solution)/shard_map/out_project/pallas_call | solution.py:251
  119.9 3.4 %collective-permute-start.20 = (bf16[64,2048]{1,0:T(8,128)(2,1)S(1)}, bf16[64,2048]{1,0:T(8,128)(2,1)S(1)}, u32[]{:S(2)}, u32[]{:S(2)}) collective-permute-start(bf16[64,2048]{1,0:T(8,128)(2,1)S(1)} %add_convert_fusion.3), channel_id=1, source_target_pairs={{0,8},{8,12},{12,4},{4,0},{1,9},{9,13},{13,5},{5,1},{2,10},{10,14}... | collective-permute-start | bytes 786440 | tf_op jit(solution)/shard_map/ppermute | solution.py:401
  123.3 4.5 %collective-permute-done.14 = bf16[64,2048]{1,0:T(8,128)(2,1)S(1)} collective-permute-done((bf16[64,2048]{1,0:T(8,128)(2,1)S(1)}, bf16[64,2048]{1,0:T(8,128)(2,1)S(1)}, u32[]{:S(2)}, u32[]{:S(2)}) %collective-permute-start.14) | collective-permute-done | bytes 262176 | tf_op jit(solution)/shard_map/ppermute | solution.py:401
  129.0 4.5 %collective-permute-done.20 = bf16[64,2048]{1,0:T(8,128)(2,1)S(1)} collective-permute-done((bf16[64,2048]{1,0:T(8,128)(2,1)S(1)}, bf16[64,2048]{1,0:T(8,128)(2,1)S(1)}, u32[]{:S(2)}, u32[]{:S(2)}) %collective-permute-start.20) | collective-permute-done | bytes 262176 | tf_op jit(solution)/shard_map/ppermute | solution.py:401
  134.6 4.5 %collective-permute-done.15 = bf16[64,2048]{1,0:T(8,128)(2,1)S(1)} collective-permute-done((bf16[64,2048]{1,0:T(8,128)(2,1)S(1)}, bf16[64,2048]{1,0:T(8,128)(2,1)S(1)}, u32[]{:S(2)}, u32[]{:S(2)}) %collective-permute-start.15) | collective-permute-done | bytes 262176 | tf_op jit(solution)/shard_map/ppermute | solution.py:401
  140.2 4.5 %collective-permute-done.21 = bf16[64,2048]{1,0:T(8,128)(2,1)S(1)} collective-permute-done((bf16[64,2048]{1,0:T(8,128)(2,1)S(1)}, bf16[64,2048]{1,0:T(8,128)(2,1)S(1)}, u32[]{:S(2)}, u32[]{:S(2)}) %collective-permute-start.21) | collective-permute-done | bytes 262176 | tf_op jit(solution)/shard_map/ppermute | solution.py:401
  (104 shorter events, 33.7 us)
Async XLA Ops:
  5.5 3.1 %collective-permute-start = (bf16[32,2,2048]{2,0,1:T(8,128)(2,1)S(1)}, bf16[32,2,2048]{2,0,1:T(8,128)(2,1)S(1)}, u32[]{:S(2)}, u32[]{:S(2)}) collective-permute-start(bf16[32,2,2048]{2,0,1:T(8,128)(2,1)S(1)} %bitcast.60), channel_id=1, source_target_pairs={{0,1},{1,0},{2,3},{3,2},{4,5},{5,4},{6,7},{7,6},{8,9},{9,8},{10,11... | collective-permute-start | bytes 786440 | tf_op jit(solution)/shard_map/ppermute | solution.py:398
  7.2 7.1 %collective-permute-start.11 = (bf16[2,8,64,128]{3,2,1,0:T(8,128)(2,1)S(1)}, bf16[2,8,64,128]{3,2,1,0:T(8,128)(2,1)S(1)}, u32[]{:S(2)}, u32[]{:S(2)}) collective-permute-start(bf16[2,8,64,128]{3,2,1,0:T(8,128)(2,1)S(1)} %pad_maximum_fusion.4), channel_id=1, source_target_pairs={{0,1},{1,0},{2,3},{3,2},{4,5},{5,4},{6,7},{7,6},{8,9},{9,8},{10,11... | collective-permute-start | bytes 786440 | tf_op jit(solution)/shard_map/ppermute | solution.py:398
  8.7 9.9 %collective-permute-start.1 = (bf16[64,2048]{1,0:T(8,128)(2,1)S(1)}, bf16[64,2048]{1,0:T(8,128)(2,1)S(1)}, u32[]{:S(2)}, u32[]{:S(2)}) collective-permute-start(bf16[64,2048]{1,0:T(8,128)(2,1)S(1)} %bitcast.57), channel_id=1, source_target_pairs={{0,8},{8,12},{12,4},{4,0},{1,9},{9,13},{13,5},{5,1},{2,10},{10,14}... | collective-permute-start | bytes 786440 | tf_op jit(solution)/shard_map/ppermute | solution.py:401
  12.8 9.2 %collective-permute-start.5 = (bf16[64,2048]{1,0:T(8,128)(2,1)S(1)}, bf16[64,2048]{1,0:T(8,128)(2,1)S(1)}, u32[]{:S(2)}, u32[]{:S(2)}) collective-permute-start(bf16[64,2048]{1,0:T(8,128)(2,1)S(1)} %bitcast.61), channel_id=1, source_target_pairs={{0,2},{2,0},{1,3},{3,1},{4,6},{6,4},{5,7},{7,5},{8,10},{10,8},{9,1... | collective-permute-start | bytes 786440 | tf_op jit(solution)/shard_map/ppermute | solution.py:395
  14.4 21.6 %collective-permute-start.12 = (bf16[2,2,8,64,128]{4,3,2,1,0:T(8,128)(2,1)S(1)}, bf16[2,2,8,64,128]{4,3,2,1,0:T(8,128)(2,1)S(1)}, u32[]{:S(2)}, u32[]{:S(2)}) collective-permute-start(bf16[2,2,8,64,128]{4,3,2,1,0:T(8,128)(2,1)S(1)} %maximum_select_fusion.2), channel_id=1, source_target_pairs={{0,2},{2,0},{1,3},{3,1},{4,6},{6,4},{5,7},{7,5},{8,10},{10,8},{9,1... | collective-permute-start | bytes 1572872 | tf_op jit(solution)/shard_map/ppermute | solution.py:395
  18.6 17.3 %collective-permute-start.2 = (bf16[64,2048]{1,0:T(8,128)(2,1)S(1)}, bf16[64,2048]{1,0:T(8,128)(2,1)S(1)}, u32[]{:S(2)}, u32[]{:S(2)}) collective-permute-start(bf16[64,2048]{1,0:T(8,128)(2,1)S(1)} %collective-permute-done.1), channel_id=1, source_target_pairs={{0,8},{8,12},{12,4},{4,0},{1,9},{9,13},{13,5},{5,1},{2,10},{10,14}... | collective-permute-start | bytes 786440 | tf_op jit(solution)/shard_map/ppermute | solution.py:401
  22.0 10.5 %collective-permute-start.6 = (bf16[64,2048]{1,0:T(8,128)(2,1)S(1)}, bf16[64,2048]{1,0:T(8,128)(2,1)S(1)}, u32[]{:S(2)}, u32[]{:S(2)}) collective-permute-start(bf16[64,2048]{1,0:T(8,128)(2,1)S(1)} %collective-permute-done.5), channel_id=1, source_target_pairs={{0,8},{8,12},{12,4},{4,0},{1,9},{9,13},{13,5},{5,1},{2,10},{10,14}... | collective-permute-start | bytes 786440 | tf_op jit(solution)/shard_map/ppermute | solution.py:401
  32.5 10.1 %collective-permute-start.7 = (bf16[64,2048]{1,0:T(8,128)(2,1)S(1)}, bf16[64,2048]{1,0:T(8,128)(2,1)S(1)}, u32[]{:S(2)}, u32[]{:S(2)}) collective-permute-start(bf16[64,2048]{1,0:T(8,128)(2,1)S(1)} %collective-permute-done.6), channel_id=1, source_target_pairs={{0,8},{8,12},{12,4},{4,0},{1,9},{9,13},{13,5},{5,1},{2,10},{10,14}... | collective-permute-start | bytes 786440 | tf_op jit(solution)/shard_map/ppermute | solution.py:401
  35.9 22.5 %collective-permute-start.3 = (bf16[64,2048]{1,0:T(8,128)(2,1)S(1)}, bf16[64,2048]{1,0:T(8,128)(2,1)S(1)}, u32[]{:S(2)}, u32[]{:S(2)}) collective-permute-start(bf16[64,2048]{1,0:T(8,128)(2,1)S(1)} %collective-permute-done.2), channel_id=1, source_target_pairs={{0,8},{8,12},{12,4},{4,0},{1,9},{9,13},{13,5},{5,1},{2,10},{10,14}... | collective-permute-start | bytes 786440 | tf_op jit(solution)/shard_map/ppermute | solution.py:401
  42.6 8.5 %collective-permute-start.8 = (bf16[64,2048]{1,0:T(8,128)(2,1)S(1)}, bf16[64,2048]{1,0:T(8,128)(2,1)S(1)}, u32[]{:S(2)}, u32[]{:S(2)}) collective-permute-start(bf16[64,2048]{1,0:T(8,128)(2,1)S(1)} %collective-permute-done.7), channel_id=1, source_target_pairs={{0,8},{8,12},{12,4},{4,0},{1,9},{9,13},{13,5},{5,1},{2,10},{10,14}... | collective-permute-start | bytes 786440 | tf_op jit(solution)/shard_map/ppermute | solution.py:401
  58.2 8.3 %collective-permute-start.9 = (bf16[256,1280]{1,0:T(8,128)(2,1)S(1)}, bf16[256,1280]{1,0:T(8,128)(2,1)S(1)}, u32[]{:S(2)}, u32[]{:S(2)}) collective-permute-start(bf16[256,1280]{1,0:T(8,128)(2,1)S(1)} %project.7), channel_id=1, source_target_pairs={{0,1},{1,0},{2,3},{3,2},{4,5},{5,4},{6,7},{7,6},{8,9},{9,8},{10,11... | collective-permute-start | bytes 1966088 | tf_op jit(solution)/shard_map/ppermute | solution.py:398
  62.3 9.8 %collective-permute-start.4 = (bf16[256,1280]{1,0:T(8,128)(2,1)S(1)}, bf16[256,1280]{1,0:T(8,128)(2,1)S(1)}, u32[]{:S(2)}, u32[]{:S(2)}) collective-permute-start(bf16[256,1280]{1,0:T(8,128)(2,1)S(1)} %project.5), channel_id=1, source_target_pairs={{0,1},{1,0},{2,3},{3,2},{4,5},{5,4},{6,7},{7,6},{8,9},{9,8},{10,11... | collective-permute-start | bytes 1966088 | tf_op jit(solution)/shard_map/ppermute | solution.py:398
  66.7 16.7 %collective-permute-start.10 = (bf16[256,1280]{1,0:T(8,128)(2,1)S(1)}, bf16[256,1280]{1,0:T(8,128)(2,1)S(1)}, u32[]{:S(2)}, u32[]{:S(2)}) collective-permute-start(bf16[256,1280]{1,0:T(8,128)(2,1)S(1)} %add_convert_fusion), channel_id=1, source_target_pairs={{0,2},{2,0},{1,3},{3,1},{4,6},{6,4},{5,7},{7,5},{8,10},{10,8},{9,1... | collective-permute-start | bytes 1966088 | tf_op jit(solution)/shard_map/ppermute | solution.py:395
  89.9 13.1 %collective-permute-start.17 = (bf16[256,1024]{1,0:T(8,128)(2,1)S(1)}, bf16[256,1024]{1,0:T(8,128)(2,1)S(1)}, u32[]{:S(2)}, u32[]{:S(2)}) collective-permute-start(bf16[256,1024]{1,0:T(8,128)(2,1)S(1)} %attend.1.own_ref), channel_id=1, source_target_pairs={{0,2},{2,0},{1,3},{3,1},{4,6},{6,4},{5,7},{7,5},{8,10},{10,8},{9,1... | collective-permute-start | bytes 1572872 | tf_op jit(solution)/shard_map/ppermute | solution.py:395
  102.9 1.9 %collective-permute-start.18 = (bf16[256,1024]{1,0:T(8,128)(2,1)S(1)}, bf16[256,1024]{1,0:T(8,128)(2,1)S(1)}, u32[]{:S(2)}, u32[]{:S(2)}) collective-permute-start(bf16[256,1024]{1,0:T(8,128)(2,1)S(1)} %collective-permute-done.17.own_ref), channel_id=1, source_target_pairs={{0,1},{1,0},{2,3},{3,2},{4,5},{5,4},{6,7},{7,6},{8,9},{9,8},{10,11... | collective-permute-start | bytes 1572872 | tf_op jit(solution)/shard_map/ppermute | solution.py:398
  102.9 10.6 %collective-permute-start.13 = (bf16[256,1024]{1,0:T(8,128)(2,1)S(1)}, bf16[256,1024]{1,0:T(8,128)(2,1)S(1)}, u32[]{:S(2)}, u32[]{:S(2)}) collective-permute-start(bf16[256,1024]{1,0:T(8,128)(2,1)S(1)} %attend.1.own_ref), channel_id=1, source_target_pairs={{0,1},{1,0},{2,3},{3,2},{4,5},{5,4},{6,7},{7,6},{8,9},{9,8},{10,11... | collective-permute-start | bytes 1572872 | tf_op jit(solution)/shard_map/ppermute | solution.py:398
  109.9 10.0 %collective-permute-start.19 = (bf16[64,2048]{1,0:T(8,128)(2,1)S(1)}, bf16[64,2048]{1,0:T(8,128)(2,1)S(1)}, u32[]{:S(2)}, u32[]{:S(2)}) collective-permute-start(bf16[64,2048]{1,0:T(8,128)(2,1)S(1)} %slice.56), channel_id=1, source_target_pairs={{0,8},{8,12},{12,4},{4,0},{1,9},{9,13},{13,5},{5,1},{2,10},{10,14}... | collective-permute-start | bytes 786440 | tf_op jit(solution)/shard_map/ppermute | solution.py:401
  118.5 9.2 %collective-permute-start.14 = (bf16[64,2048]{1,0:T(8,128)(2,1)S(1)}, bf16[64,2048]{1,0:T(8,128)(2,1)S(1)}, u32[]{:S(2)}, u32[]{:S(2)}) collective-permute-start(bf16[64,2048]{1,0:T(8,128)(2,1)S(1)} %slice.52), channel_id=1, source_target_pairs={{0,8},{8,12},{12,4},{4,0},{1,9},{9,13},{13,5},{5,1},{2,10},{10,14}... | collective-permute-start | bytes 786440 | tf_op jit(solution)/shard_map/ppermute | solution.py:401
  119.9 13.5 %collective-permute-start.20 = (bf16[64,2048]{1,0:T(8,128)(2,1)S(1)}, bf16[64,2048]{1,0:T(8,128)(2,1)S(1)}, u32[]{:S(2)}, u32[]{:S(2)}) collective-permute-start(bf16[64,2048]{1,0:T(8,128)(2,1)S(1)} %add_convert_fusion.3), channel_id=1, source_target_pairs={{0,8},{8,12},{12,4},{4,0},{1,9},{9,13},{13,5},{5,1},{2,10},{10,14}... | collective-permute-start | bytes 786440 | tf_op jit(solution)/shard_map/ppermute | solution.py:401
  127.9 11.2 %collective-permute-start.15 = (bf16[64,2048]{1,0:T(8,128)(2,1)S(1)}, bf16[64,2048]{1,0:T(8,128)(2,1)S(1)}, u32[]{:S(2)}, u32[]{:S(2)}) collective-permute-start(bf16[64,2048]{1,0:T(8,128)(2,1)S(1)} %add_convert_fusion.6), channel_id=1, source_target_pairs={{0,8},{8,12},{12,4},{4,0},{1,9},{9,13},{13,5},{5,1},{2,10},{10,14}... | collective-permute-start | bytes 786440 | tf_op jit(solution)/shard_map/ppermute | solution.py:401
  133.5 11.2 %collective-permute-start.21 = (bf16[64,2048]{1,0:T(8,128)(2,1)S(1)}, bf16[64,2048]{1,0:T(8,128)(2,1)S(1)}, u32[]{:S(2)}, u32[]{:S(2)}) collective-permute-start(bf16[64,2048]{1,0:T(8,128)(2,1)S(1)} %add_convert_fusion.2), channel_id=1, source_target_pairs={{0,8},{8,12},{12,4},{4,0},{1,9},{9,13},{13,5},{5,1},{2,10},{10,14}... | collective-permute-start | bytes 786440 | tf_op jit(solution)/shard_map/ppermute | solution.py:401
  139.1 10.0 %collective-permute-start.16 = (bf16[64,2048]{1,0:T(8,128)(2,1)S(1)}, bf16[64,2048]{1,0:T(8,128)(2,1)S(1)}, u32[]{:S(2)}, u32[]{:S(2)}) collective-permute-start(bf16[64,2048]{1,0:T(8,128)(2,1)S(1)} %add_convert_fusion.5), channel_id=1, source_target_pairs={{0,8},{8,12},{12,4},{4,0},{1,9},{9,13},{13,5},{5,1},{2,10},{10,14}... | collective-permute-start | bytes 786440 | tf_op jit(solution)/shard_map/ppermute | solution.py:401
  144.7 6.4 %collective-permute-start.22 = (bf16[64,2048]{1,0:T(8,128)(2,1)S(1)}, bf16[64,2048]{1,0:T(8,128)(2,1)S(1)}, u32[]{:S(2)}, u32[]{:S(2)}) collective-permute-start(bf16[64,2048]{1,0:T(8,128)(2,1)S(1)} %add_convert_fusion.1), channel_id=1, source_target_pairs={{0,2},{2,0},{1,3},{3,1},{4,6},{6,4},{5,7},{7,5},{8,10},{10,8},{9,1... | collective-permute-start | bytes 786440 | tf_op jit(solution)/shard_map/ppermute | solution.py:395
  151.2 1.6 %collective-permute-start.23 = (bf16[32,2,2048]{2,0,1:T(8,128)(2,1)S(1)}, bf16[32,2,2048]{2,0,1:T(8,128)(2,1)S(1)}, u32[]{:S(2)}, u32[]{:S(2)}) collective-permute-start(bf16[32,2,2048]{2,0,1:T(8,128)(2,1)S(1)} %get-tuple-element.14), channel_id=1, source_target_pairs={{0,1},{1,0},{2,3},{3,2},{4,5},{5,4},{6,7},{7,6},{8,9},{9,8},{10,11... | collective-permute-start | bytes 786440 | tf_op jit(solution)/shard_map/ppermute | solution.py:398
  (10 other events, 197.0 us)

commit v2 on v0

--- a/solution.py
+++ b/solution.py
@@ -1,6 +1,10 @@
+import functools
+
 import jax
 import jax.numpy as jnp
 from jax import lax
+from jax.experimental import pallas as pl
+from jax.experimental.pallas import tpu as pltpu
 from jax.sharding import PartitionSpec as P
 
 HQ = 64
@@ -64,7 +68,7 @@
     )
 
 
-def on_device(
+def general_path(
     tokens, norm_gain, w_query, w_key, w_value, w_out, cache_keys, cache_values, seg_ids, block_ids
 ):
     groups = seg_ids.shape[0]
@@ -147,6 +151,464 @@
     return branch[None]
 
 
+SWAP = [(0, 1), (1, 0)]
+MASKED = -1e30
+MIB = 2**20
+
+
+def tp_ring(count):
+    return list(range(0, count, 2)) + list(range(1, count, 2))[::-1]
+
+
+def after(value, *gates):
+    if not gates:
+        return value
+    return lax.optimization_barrier((value, gates))[0]
+
+
+def norm_kernel(place_ref, x_ref, gain_ref, keep_ref, give_ref, far_ref, cross_ref):
+    wide = x_ref[0].astype(jnp.float32)
+    factor = lax.rsqrt(jnp.mean(wide * wide, axis=1, keepdims=True) + EPS)
+    width = keep_ref.shape[1]
+    req, kv = place_ref[0], place_ref[1]
+    to = (2 * req + kv, 2 * req + 1 - kv, 2 - 2 * req + kv, 3 - 2 * req - kv)
+    for quarter, ref in zip(to, (keep_ref, give_ref, far_ref, cross_ref)):
+        at = pl.multiple_of(quarter * width, width)
+        part = x_ref[0, :, pl.ds(at, width)].astype(jnp.float32)
+        gain = gain_ref[:, pl.ds(at, width)].astype(jnp.float32)
+        ref[...] = (part * factor * gain).astype(ref.dtype)
+
+
+def norm(place, tokens, gain):
+    rows, depth = tokens.shape[1:]
+    whole = pl.BlockSpec(memory_space=pltpu.VMEM)
+    quarter = jax.ShapeDtypeStruct((rows, depth // 4), jnp.bfloat16)
+    return pl.pallas_call(
+        norm_kernel,
+        in_specs=[pl.BlockSpec(memory_space=pltpu.SMEM), whole, whole],
+        out_specs=[whole] * 4,
+        out_shape=[quarter] * 4,
+        compiler_params=pltpu.CompilerParams(vmem_limit_bytes=4 * MIB),
+        name="norm",
+    )(place, tokens, gain.reshape(1, depth))
+
+
+def load_kernel(count, *refs):
+    copies = [
+        pltpu.make_async_copy(source, to, refs[-1].at[number])
+        for number, (source, to) in enumerate(zip(refs[:count], refs[count:]))
+    ]
+    for copy in copies:
+        copy.start()
+    for copy in copies:
+        copy.wait()
+
+
+def load(limit, *arrays):
+    count = len(arrays)
+    return pl.pallas_call(
+        functools.partial(load_kernel, count),
+        in_specs=[pl.BlockSpec(memory_space=pl.ANY)] * count,
+        out_specs=[pl.BlockSpec(memory_space=pltpu.VMEM)] * count,
+        out_shape=[pltpu.VMEM(a.shape, a.dtype) for a in arrays],
+        scratch_shapes=[pltpu.SemaphoreType.DMA((count,))],
+        compiler_params=pltpu.CompilerParams(vmem_limit_bytes=limit * MIB),
+        name="load",
+    )(*arrays)
+
+
+def heads_kernel(place_ref, k_ref, v_ref, mine_ref, give_ref, sems):
+    head_dim = mine_ref.shape[-1]
+    kv, tp = place_ref[1], place_ref[2]
+    copies = []
+    for number, (out, core) in enumerate(((mine_ref, kv), (give_ref, 1 - kv))):
+        at = pl.multiple_of((2 * tp + core) * head_dim, head_dim)
+        for which, ref in enumerate((k_ref, v_ref)):
+            copies.append(
+                pltpu.make_async_copy(
+                    ref.at[:, :, pl.ds(at, head_dim)], out.at[which], sems.at[2 * number + which]
+                )
+            )
+    for copy in copies:
+        copy.start()
+    for copy in copies:
+        copy.wait()
+
+
+def cached_heads(place, keys, values):
+    blocks, length = keys.shape[:2]
+    out = jax.ShapeDtypeStruct((2, blocks, length, HD), keys.dtype)
+    return pl.pallas_call(
+        heads_kernel,
+        in_specs=[pl.BlockSpec(memory_space=pltpu.SMEM)]
+        + [pl.BlockSpec(memory_space=pl.ANY)] * 2,
+        out_specs=[pl.BlockSpec(memory_space=pltpu.VMEM)] * 2,
+        out_shape=[out] * 2,
+        scratch_shapes=[pltpu.SemaphoreType.DMA((4,))],
+        compiler_params=pltpu.CompilerParams(vmem_limit_bytes=4 * MIB),
+        name="cached_heads",
+    )(place, keys, values)
+
+
+def merge_kernel(place_ref, mine_ref, theirs_ref, out_ref):
+    rows = mine_ref.shape[0]
+    kv = place_ref[1]
+    out_ref[pl.ds(pl.multiple_of(kv * rows, rows), rows), :] = mine_ref[...]
+    out_ref[pl.ds(pl.multiple_of((1 - kv) * rows, rows), rows), :] = theirs_ref[...]
+
+
+def merge(place, mine, theirs):
+    rows, columns = mine.shape
+    whole = pl.BlockSpec(memory_space=pltpu.VMEM)
+    return pl.pallas_call(
+        merge_kernel,
+        in_specs=[pl.BlockSpec(memory_space=pltpu.SMEM)] + [whole] * 2,
+        out_specs=whole,
+        out_shape=jax.ShapeDtypeStruct((2 * rows, columns), mine.dtype),
+        compiler_params=pltpu.CompilerParams(vmem_limit_bytes=4 * MIB),
+        name="merge",
+    )(place, mine, theirs)
+
+
+def share_kernel(place_ref, running_ref, term_ref, mine_ref, give_ref):
+    rows = mine_ref.shape[0]
+    kv = place_ref[1]
+    for core, ref in ((kv, mine_ref), (1 - kv, give_ref)):
+        at = pl.ds(pl.multiple_of(core * rows, rows), rows)
+        total = running_ref[at, :].astype(jnp.float32) + term_ref[at, :].astype(jnp.float32)
+        ref[...] = total.astype(ref.dtype)
+
+
+def share(place, running, term):
+    rows, columns = running.shape
+    whole = pl.BlockSpec(memory_space=pltpu.VMEM)
+    return pl.pallas_call(
+        share_kernel,
+        in_specs=[pl.BlockSpec(memory_space=pltpu.SMEM)] + [whole] * 2,
+        out_specs=[whole] * 2,
+        out_shape=[jax.ShapeDtypeStruct((rows // 2, columns), running.dtype)] * 2,
+        compiler_params=pltpu.CompilerParams(vmem_limit_bytes=4 * MIB),
+        name="share",
+    )(place, running, term)
+
+
+def collect_kernel(place_ref, *refs):
+    out_ref = refs[-1]
+    width = refs[0].shape[1]
+    req, kv = place_ref[0], place_ref[1]
+    of = (2 * req + kv, 2 * req + 1 - kv, 2 - 2 * req + kv, 3 - 2 * req - kv)
+    for quarter, ref in zip(of, refs[:-1]):
+        out_ref[0, :, pl.ds(pl.multiple_of(quarter * width, width), width)] = ref[...]
+
+
+def collect(place, *quarters):
+    rows, columns = quarters[0].shape
+    whole = pl.BlockSpec(memory_space=pltpu.VMEM)
+    return pl.pallas_call(
+        collect_kernel,
+        in_specs=[pl.BlockSpec(memory_space=pltpu.SMEM)] + [whole] * 4,
+        out_specs=whole,
+        out_shape=jax.ShapeDtypeStruct((1, rows, 4 * columns), quarters[0].dtype),
+        compiler_params=pltpu.CompilerParams(vmem_limit_bytes=4 * MIB),
+        name="collect",
+    )(place, *quarters)
+
+
+def project_kernel(flips, place_ref, *refs):
+    outputs = len(flips)
+    pieces = refs[: -3 - outputs]
+    q_ref, k_ref, v_ref = refs[-3 - outputs : -outputs]
+    outs = refs[-outputs:]
+    x = jnp.concatenate([piece[...] for piece in pieces], axis=0)
+    head_dim = k_ref.shape[1] // 2
+    width = 256
+    base = q_ref.shape[1] // 2
+    for number, out in enumerate(outs):
+        kv = place_ref[1]
+        half = 1 - kv if flips[number] else kv
+        for t in range(base // width):
+            at = pl.multiple_of(half * base + t * width, width)
+            product = jnp.dot(x, q_ref[:, pl.ds(at, width)], preferred_element_type=jnp.float32)
+            out[:, t * width : (t + 1) * width] = product.astype(out.dtype)
+        at = pl.ds(pl.multiple_of(half * head_dim, head_dim), head_dim)
+        both = jnp.concatenate((k_ref[:, at], v_ref[:, at]), axis=1)
+        product = jnp.dot(x, both, preferred_element_type=jnp.float32)
+        out[:, base:] = product.astype(out.dtype)
+
+
+def project(place, pieces, weights, flips, kinds):
+    rows = sum(piece.shape[0] for piece in pieces)
+    total = sum(w.shape[1] for w in weights) // 2
+    whole = pl.BlockSpec(memory_space=pltpu.VMEM)
+    return pl.pallas_call(
+        functools.partial(project_kernel, flips),
+        in_specs=[pl.BlockSpec(memory_space=pltpu.SMEM)] + [whole] * (len(pieces) + 3),
+        out_specs=[whole] * len(kinds),
+        out_shape=[jax.ShapeDtypeStruct((rows, total), kind) for kind in kinds],
+        compiler_params=pltpu.CompilerParams(vmem_limit_bytes=6 * MIB),
+        name="project",
+    )(place, *pieces, *weights)
+
+
+def out_kernel(place_ref, own_ref, other_ref, w_ref, *outs):
+    depth = own_ref.shape[1]
+    part = own_ref.shape[0] // len(outs)
+    mine = place_ref[1]
+    at = pl.multiple_of(mine * depth, depth)
+    off = pl.multiple_of((1 - mine) * depth, depth)
+    own, other = own_ref[...], other_ref[...]
+    width = 256
+    for t in range(w_ref.shape[1] // width):
+        columns = slice(t * width, (t + 1) * width)
+        product = jnp.dot(
+            own, w_ref[pl.ds(at, depth), columns], preferred_element_type=jnp.float32
+        )
+        product += jnp.dot(
+            other, w_ref[pl.ds(off, depth), columns], preferred_element_type=jnp.float32
+        )
+        product = product.astype(outs[0].dtype)
+        for j, out in enumerate(outs):
+            out[:, columns] = product[j * part : (j + 1) * part]
+
+
+def out_project(place, own, other, w_out, pieces):
+    rows = own.shape[0]
+    columns = w_out.shape[1]
+    whole = pl.BlockSpec(memory_space=pltpu.VMEM)
+    return pl.pallas_call(
+        out_kernel,
+        in_specs=[pl.BlockSpec(memory_space=pltpu.SMEM)] + [whole] * 3,
+        out_specs=[whole] * pieces,
+        out_shape=[jax.ShapeDtypeStruct((rows // pieces, columns), jnp.bfloat16)] * pieces,
+        compiler_params=pltpu.CompilerParams(vmem_limit_bytes=6 * MIB),
+        name="out_project",
+    )(place, own, other, w_out)
+
+
+def attend_kernel(wanted, order, place_ref, ids_ref, seg_ref, keep_ref, *refs):
+    come_refs, (chip_ref, away_ref, out_ref) = refs[:-3], refs[-3:]
+    req, kv, tp = place_ref[0], place_ref[1], place_ref[2]
+    groups = 2
+    steps = ids_ref.shape[1]
+    total_cols = keep_ref.shape[1]
+    rows = keep_ref.shape[0] // groups
+    part = out_ref.shape[0] // (groups * len(wanted))
+    pieces = rows // part
+    some = part * len(wanted)
+    head_dim = chip_ref.shape[-1]
+    blocks, length = chip_ref.shape[2:4]
+    heads = total_cols // head_dim - 2
+    q_cols = heads * head_dim
+    scale = head_dim**-0.5
+    stack = min(heads, max(1, 256 // some))
+    chain = CHAIN_BLOCKS * length
+
+    def looked_up(index, options):
+        result = jnp.int32(options[0])
+        for number, option in enumerate(options[1:], 1):
+            result = jnp.where(index == number, jnp.int32(option), result)
+        return result
+
+    spot = looked_up(tp, [order.index(i) for i in range(pieces)])
+    source = [looked_up(lax.rem(spot - j + pieces, pieces), order) for j in range(pieces)]
+
+    def branch(block, which):
+        device = block // blocks
+        near = device // 2 == req
+        core = jnp.where(lax.rem(device, 2) == kv, 0, 1)
+        at = lax.rem(block, blocks)
+        here = chip_ref[core, which, pl.ds(at, CHAIN_BLOCKS)]
+        there = away_ref[core, which, pl.ds(at, CHAIN_BLOCKS)]
+        return jnp.where(near, here, there).reshape(chain, head_dim)
+
+    def position(index, sources):
+        piece = index // part
+        start = jnp.full(index.shape, source[sources[0]], jnp.int32)
+        for j in range(1, len(sources)):
+            start = jnp.where(piece == j, source[sources[j]], start)
+        return start * part + index % part
+
+    row_pos = position(lax.broadcasted_iota(jnp.int32, (some, rows), 0), wanted)
+    across = lax.broadcasted_iota(jnp.int32, (some, rows), 1)
+    col_pos = position(across, range(pieces))
+    come = jnp.concatenate([ref[...] for ref in come_refs], axis=0)
+    whole = (keep_ref[...] + come.astype(jnp.float32)).astype(jnp.bfloat16)
+
+    def own_rows(g, j, columns):
+        at = (j * groups + g) * part
+        return whole[at : at + part, columns]
+
+    for g in range(groups):
+        group = 2 * req + g
+        segments = seg_ref[pl.ds(group, 1), :]
+        root = jnp.int32(0)
+        keys, values = [branch(root, 0)], [branch(root, 1)]
+        bias = [jnp.zeros((some, chain), jnp.float32)]
+        same = None
+        low = jnp.int32(0)
+        for s in range(steps):
+            first = ids_ref[group, s, ROOT_BLOCKS]
+            count = jnp.int32(0)
+            for slot in range(CHAIN_BLOCKS):
+                count += jnp.where(ids_ref[group, s, ROOT_BLOCKS + slot] >= 0, length, 0)
+            high = jnp.sum((segments <= s).astype(jnp.int32))
+            keys.append(branch(first, 0))
+            values.append(branch(first, 1))
+            row_in = (row_pos >= low) & (row_pos < high)
+            col_in = (col_pos >= low) & (col_pos < high)
+            both = row_in & col_in
+            same = both if same is None else same | both
+            for piece in range(chain // rows):
+                allowed = row_in & (across + piece * rows < count)
+                bias.append(jnp.where(allowed, 0.0, MASKED))
+            low = high
+        for j in range(pieces):
+            keys.append(own_rows(g, j, slice(q_cols, q_cols + head_dim)))
+            values.append(own_rows(g, j, slice(q_cols + head_dim, None)))
+        bias.append(jnp.where(same & (col_pos <= row_pos), 0.0, MASKED))
+        keys = jnp.concatenate(keys, axis=0)
+        values = jnp.concatenate(values, axis=0)
+        bias = jnp.concatenate(bias, axis=1)
+        bias = jnp.concatenate([bias] * stack, axis=0)
+        for low_head in range(0, heads, stack):
+            query = jnp.concatenate(
+                [
+                    own_rows(g, j, slice(h * head_dim, (h + 1) * head_dim))
+                    for h in range(low_head, low_head + stack)
+                    for j in wanted
+                ],
+                axis=0,
+            )
+            scores = lax.dot_general(
+                query, keys, (((1,), (1,)), ((), ())), preferred_element_type=jnp.float32
+            )
+            scores = scores * scale + bias
+            top = jnp.max(scores, axis=1, keepdims=True)
+            weights = jnp.exp(scores - top)
+            total = jnp.sum(weights, axis=1, keepdims=True)
+            summed = jnp.dot(
+                weights.astype(jnp.bfloat16), values, preferred_element_type=jnp.float32
+            )
+            result = (summed / total).astype(out_ref.dtype)
+            for n in range(stack):
+                columns = slice((low_head + n) * head_dim, (low_head + n + 1) * head_dim)
+                for number in range(len(wanted)):
+                    of, to = n * some + number * part, (number * groups + g) * part
+                    out_ref[to : to + part, columns] = result[of : of + part]
+
+
+def attend(wanted, order, place, ids, segments, keep, come, chip, away, part):
+    rows = 2 * len(wanted) * part
+    whole = pl.BlockSpec(memory_space=pltpu.VMEM)
+    scalars = pl.BlockSpec(memory_space=pltpu.SMEM)
+    return pl.pallas_call(
+        functools.partial(attend_kernel, wanted, order),
+        in_specs=[scalars] * 2 + [whole] * (len(come) + 4),
+        out_specs=whole,
+        out_shape=jax.ShapeDtypeStruct((rows, keep.shape[1] - 2 * HD), jnp.bfloat16),
+        compiler_params=pltpu.CompilerParams(vmem_limit_bytes=10 * MIB),
+        name="attend",
+    )(place, ids, segments, keep, *come, chip, away)
+
+
+ROOT_BLOCKS = 4
+CHAIN_BLOCKS = 4
+
+
+def on_device(
+    tokens, norm_gain, w_query, w_key, w_value, w_out, cache_keys, cache_values, seg_ids, block_ids
+):
+    req, kv, tp = lax.axis_index("req"), lax.axis_index("kv"), lax.axis_index("tp")
+    part = tokens.shape[1]
+    count = lax.axis_size("tp")
+    order = tp_ring(count)
+    forward = [(order[i], order[(i + 1) % count]) for i in range(count)]
+    place = jnp.stack((req, kv, tp)).astype(jnp.int32)
+
+    def swap_req(x):
+        return lax.ppermute(x, "req", SWAP)
+
+    def swap_kv(x):
+        return lax.ppermute(x, "kv", SWAP)
+
+    def swap_both(x):
+        return lax.ppermute(x, ("req", "kv"), [(i, 3 - i) for i in range(4)])
+
+    def onward(x):
+        return lax.ppermute(x, "tp", forward)
+
+    kept, give, far_same, far_cross = norm(place, tokens, norm_gain)
+    near = merge(place, kept, swap_kv(give))
+    far = merge(place, swap_req(far_same), swap_both(far_cross))
+
+    near_pieces, far_pieces = [near, onward(near)], [far]
+    weights = load(46, *after((w_query, w_key, w_value), near))
+    far_pieces.append(onward(after(far, weights)))
+    mine, give = cached_heads(place, *after((cache_keys, cache_values), weights))
+    chip = jnp.stack((mine, swap_kv(give)))
+    away = swap_req(chip)
+    for pieces in (near_pieces, far_pieces):
+        for _ in range(count - 2):
+            pieces.append(onward(pieces[-1]))
+
+    kinds = (jnp.bfloat16, jnp.float32)
+
+    def summed(sent, kept, kind):
+        return (kept + swap_kv(sent).astype(jnp.float32)).astype(kind)
+
+    near_terms = project(place, after(near_pieces, away), weights, (True, False), kinds)
+    keep = summed(*near_terms, jnp.float32)
+    far_pieces = after(far_pieces, near_terms)
+    sent = project(place, far_pieces, weights, (True,), kinds[:1])
+    kept = project(place, far_pieces, weights, (False,), kinds[1:])
+    far_terms = summed(*sent, *kept, jnp.bfloat16)
+    come = (swap_req(far_terms),)
+    w_out = load(38, *after((w_out,), far_terms))[0]
+
+    middle = count // 2
+    halves = (tuple(range(1, middle + 1)), tuple(j % count for j in range(middle + 1, count + 1)))
+    near_sum, far_sum = {}, {}
+
+    def attended(wanted, *gates):
+        inputs = after(keep, *gates)
+        return attend(
+            wanted, order, place, block_ids, seg_ids, inputs, come, chip, away, part
+        )
+
+    def projected(sums, wanted, own, other):
+        sums |= zip(wanted, out_project(place, own, other, w_out, middle))
+
+    def plus(running, term):
+        return (running.astype(jnp.float32) + term.astype(jnp.float32)).astype(jnp.bfloat16)
+
+    rows = attended(halves[0], w_out)
+    rows_far = swap_req(rows)
+    projected(near_sum, halves[0], rows, swap_kv(rows))
+    near_run = onward(near_sum[1])
+    last = attended(halves[1], near_sum[1])
+    last_far = swap_req(last)
+    rows_far = after(rows_far, last)
+    rows_far = after((rows_far, swap_kv(rows_far)), near_run)
+    projected(far_sum, halves[0], *rows_far)
+    far_run = onward(far_sum[1])
+    projected(near_sum, halves[1], last, swap_kv(last))
+    last_far = after(last_far, near_run)
+    projected(far_sum, halves[1], last_far, swap_kv(last_far))
+    for j in range(2, count):
+        near_term = plus(near_run, near_sum[j])
+        near_run = onward(after(near_term, far_run) if j == count - 1 else near_term)
+        far_run = onward(plus(far_run, far_sum[j]))
+    mine, give = share(place, far_run, far_sum[0])
+    away = (swap_req(mine), swap_both(give))
+    mine, give = share(place, near_run, near_sum[0])
+    return collect(place, mine, swap_kv(give), *away)
+
+
+def fits(shape):
+    local_kv = KVH // shape["tp"]
+    return shape["req"] == 2 and shape["kv"] == 2 and shape["tp"] > 1 and local_kv == 2
+
+
 def solution(mesh):
     placed = (
         P(("grp", "req", "kv"), "tp", None),
@@ -161,7 +623,7 @@
         P("grp", None, None),
     )
     return jax.shard_map(
-        on_device,
+        on_device if fits(mesh.shape) else general_path,
         mesh=mesh,
         in_specs=placed,
         out_specs=P(("grp", "req", "kv"), "tp", None),

time: 705 us -> 127 us (0.18)
  waiting for transfers between devices: 549 us -> 50.9 us
  matrix products: 50.6 us -> 0 us
  other arithmetic: 40.7 us -> 0.66 us
  starting transfers between devices: 0.46 us -> 39.6 us
  local copies, waits for them, and re-layouts: 37.5 us -> 1.8 us
  Pallas kernels: 0 us -> 33.2 us
  between operations: 13.7 us -> 0.29 us
  blocking collectives: 10.8 us -> 0 us
    all_gather x7 -> x0, waiting for transfers between devices: 503 us -> none  [the longest x1 202 us: on_device(): lax.all_gather(w_query, ('req', 'kv'), axis=0, tiled=True)]
    ppermute x0 -> x29, waiting for transfers between devices: none -> 50.9 us  [the longest x12 33.1 us: onward(): return lax.ppermute(x, 'tp', forward)]
    dot_general x9 -> x0, matrix products: 50.6 us -> none  [the longest x3 22.3 us: on_device(): jnp.dot(whole, piece, preferred_element_type=jnp.float32)]
    reduce_scatter x1 -> x0, waiting for transfers between devices: 44 us -> none  [on_device(): lax.psum_scatter(jnp.dot(attended, out_full, preferred_element_type=jnp.f...]
    ppermute x0 -> x29, starting transfers between devices: none -> 39.6 us  [the longest x12 27.4 us: onward(): return lax.ppermute(x, 'tp', forward)]
    pallas_call x0 -> x18, Pallas kernels: none -> 33.2 us  [the longest x3 7.72 us: project(): pl.pallas_call(functools.partial(project_kernel, flips), in_specs=[pl.Blo...]
    while x3 -> x0, local copies, waits for them, and re-layouts: 25.4 us -> none  [combined_all(): lax.fori_loop(1, lax.axis_size(axis), lambda source, state: join(state, t...]
    add x7 -> x1, other arithmetic: 22.9 us -> 0.14 us  [summed(): return (kept + swap_kv(sent).astype(jnp.float32)).astype(kind)]
  transfers between devices with their start and end apart: 8 -> 29, of which waited for: 8 -> 15; matrix products, arithmetic and copies ran while one was open for 12% -> 0% of each run, Pallas kernels for 0% -> 21%
where the time goes in v2:
time: 127 us; the launch traced here: 126 us
  waiting for transfers between devices  50.9 us (40%)
  starting transfers between devices  39.6 us (31%)
  Pallas kernels  33.2 us (26%)
  local copies, waits for them, and re-layouts  1.8 us (1%)
    ppermute x12, waiting for transfers between devices, onward(): return lax.ppermute(x, 'tp', forward)  33.1 us
    ppermute x12, starting transfers between devices, onward(): return lax.ppermute(x, 'tp', forward)  27.4 us
    ppermute x6, waiting for transfers between devices, swap_req(): return lax.ppermute(x, 'req', SWAP)  16.3 us
    ppermute x6, starting transfers between devices, swap_req(): return lax.ppermute(x, 'req', SWAP)  10.1 us
    pallas_call x3, Pallas kernels, project(): pl.pallas_call(functools.partial(project_kernel, flips), in_specs=[pl.Blo...  7.72 us
    pallas_call x2, Pallas kernels, load(): pl.pallas_call(functools.partial(load_kernel, count), in_specs=[pl.BlockS...  7.32 us
    pallas_call x4, Pallas kernels, out_project(): pl.pallas_call(out_kernel, in_specs=[pl.BlockSpec(memory_space=pltpu.SMEM...  7.26 us
    pallas_call x2, Pallas kernels, attend(): pl.pallas_call(functools.partial(attend_kernel, wanted, order), in_specs=...  5.6 us
  transfers between devices with their start and end apart: 29, of which 15 were waited for; matrix products, arithmetic and copies ran while one was open for 0% of the time, Pallas kernels for 21%

profile of v2, /device:TPU:0, one launch (start us, length us, event | category | flops | bytes accessed | tf_op | source)
XLA Modules:
  0.0 126.4 jit_solution(17243555762008689128)
XLA Ops:
  3.2 2.6 %collective-permute-start.7 = (bf16[32,2048]{1,0:T(8,128)(2,1)S(1)}, bf16[32,2048]{1,0:T(8,128)(2,1)S(1)}, u32[]{:S(2)}, u32[]{:S(2)}) collective-permute-start(bf16[32,2048]{1,0:T(8,128)(2,1)S(1)} %get-tuple-element.68), channel_id=1, source_target_pairs={{0,2},{2,0},{1,3},{3,1},{4,6},{6,4},{5,7},{7,5},{8,10},{10,8},{9,1... | collective-permute-start | bytes 393224 | tf_op jit(solution)/shard_map/ppermute | solution.py:529
  6.5 2.9 %collective-permute-start.1 = (bf16[64,2048]{1,0:T(8,128)(2,1)S(1)}, bf16[64,2048]{1,0:T(8,128)(2,1)S(1)}, u32[]{:S(2)}, u32[]{:S(2)}) collective-permute-start(bf16[64,2048]{1,0:T(8,128)(2,1)S(1)} %merge.2.refs_0_), channel_id=1, source_target_pairs={{0,8},{8,12},{12,4},{4,0},{1,9},{9,13},{13,5},{5,1},{2,10},{10,14}... | collective-permute-start | bytes 786440 | tf_op jit(solution)/shard_map/ppermute | solution.py:538
  9.4 3.9 %load.2 = (bf16[2048,2048]{1,0:T(8,128)(2,1)S(1)}, bf16[2048,256]{1,0:T(8,128)(2,1)S(1)}, bf16[2048,256]{1,0:T(8,128)(2,1)S(1)}) custom-call(bf16[2048,2048]{1,0:T(8,128)(2,1)} %refs_0_, bf16[2048,256]{1,0:T(8,128)(2,1)} %refs_1_, bf16[2048,256]{1,0:T(8,128)(2,1)} %refs_2_), custom_call_target="tpu_custom_call" | custom-call | tf_op jit(solution)/shard_map/load/pallas_call | solution.py:209
  16.4 2.4 %collective-permute-start.2 = (bf16[64,2048]{1,0:T(8,128)(2,1)S(1)}, bf16[64,2048]{1,0:T(8,128)(2,1)S(1)}, u32[]{:S(2)}, u32[]{:S(2)}) collective-permute-start(bf16[64,2048]{1,0:T(8,128)(2,1)S(1)} %collective-permute-done.1.refs_1_), channel_id=1, source_target_pairs={{0,8},{8,12},{12,4},{4,0},{1,9},{9,13},{13,5},{5,1},{2,10},{10,14}... | collective-permute-start | bytes 786440 | tf_op jit(solution)/shard_map/ppermute | solution.py:538
  20.4 3.5 %collective-permute-done.9.refs_1_ = bf16[64,2048]{1,0:T(8,128)(2,1)S(1)} collective-permute-done((bf16[64,2048]{1,0:T(8,128)(2,1)S(1)}, bf16[64,2048]{1,0:T(8,128)(2,1)S(1)}, u32[]{:S(2)}, u32[]{:S(2)}) %collective-permute-start.9) | collective-permute-done | bytes 262176 | tf_op jit(solution)/shard_map/ppermute | solution.py:538
  23.9 2.5 %collective-permute-start.10 = (bf16[64,2048]{1,0:T(8,128)(2,1)S(1)}, bf16[64,2048]{1,0:T(8,128)(2,1)S(1)}, u32[]{:S(2)}, u32[]{:S(2)}) collective-permute-start(bf16[64,2048]{1,0:T(8,128)(2,1)S(1)} %collective-permute-done.9.refs_1_), channel_id=1, source_target_pairs={{0,8},{8,12},{12,4},{4,0},{1,9},{9,13},{13,5},{5,1},{2,10},{10,14}... | collective-permute-start | bytes 786440 | tf_op jit(solution)/shard_map/ppermute | solution.py:538
  26.4 3.1 %collective-permute-done.2.refs_2_ = bf16[64,2048]{1,0:T(8,128)(2,1)S(1)} collective-permute-done((bf16[64,2048]{1,0:T(8,128)(2,1)S(1)}, bf16[64,2048]{1,0:T(8,128)(2,1)S(1)}, u32[]{:S(2)}, u32[]{:S(2)}) %collective-permute-start.2) | collective-permute-done | bytes 262176 | tf_op jit(solution)/shard_map/ppermute | solution.py:538
  29.5 2.5 %collective-permute-start.3 = (bf16[64,2048]{1,0:T(8,128)(2,1)S(1)}, bf16[64,2048]{1,0:T(8,128)(2,1)S(1)}, u32[]{:S(2)}, u32[]{:S(2)}) collective-permute-start(bf16[64,2048]{1,0:T(8,128)(2,1)S(1)} %collective-permute-done.2.refs_2_), channel_id=1, source_target_pairs={{0,8},{8,12},{12,4},{4,0},{1,9},{9,13},{13,5},{5,1},{2,10},{10,14}... | collective-permute-start | bytes 786440 | tf_op jit(solution)/shard_map/ppermute | solution.py:538
  32.0 3.1 %collective-permute-done.10.refs_2_ = bf16[64,2048]{1,0:T(8,128)(2,1)S(1)} collective-permute-done((bf16[64,2048]{1,0:T(8,128)(2,1)S(1)}, bf16[64,2048]{1,0:T(8,128)(2,1)S(1)}, u32[]{:S(2)}, u32[]{:S(2)}) %collective-permute-start.10) | collective-permute-done | bytes 262176 | tf_op jit(solution)/shard_map/ppermute | solution.py:538
  35.2 2.5 %collective-permute-start.11 = (bf16[64,2048]{1,0:T(8,128)(2,1)S(1)}, bf16[64,2048]{1,0:T(8,128)(2,1)S(1)}, u32[]{:S(2)}, u32[]{:S(2)}) collective-permute-start(bf16[64,2048]{1,0:T(8,128)(2,1)S(1)} %collective-permute-done.10.refs_2_), channel_id=1, source_target_pairs={{0,8},{8,12},{12,4},{4,0},{1,9},{9,13},{13,5},{5,1},{2,10},{10,14}... | collective-permute-start | bytes 786440 | tf_op jit(solution)/shard_map/ppermute | solution.py:538
  37.6 3.1 %collective-permute-done.3.refs_3_ = bf16[64,2048]{1,0:T(8,128)(2,1)S(1)} collective-permute-done((bf16[64,2048]{1,0:T(8,128)(2,1)S(1)}, bf16[64,2048]{1,0:T(8,128)(2,1)S(1)}, u32[]{:S(2)}, u32[]{:S(2)}) %collective-permute-start.3) | collective-permute-done | bytes 262176 | tf_op jit(solution)/shard_map/ppermute | solution.py:538
  40.8 3.5 %project.3 = (bf16[256,1280]{1,0:T(8,128)(2,1)S(1)}, f32[256,1280]{1,0:T(8,128)S(1)}) custom-call(s32[3]{0:T(128)S(1)} %pad_add_fusion.place_ref, bf16[64,2048]{1,0:T(8,128)(2,1)S(1)} %merge.2.refs_0_, bf16[64,2048]{1,0:T(8,128)(2,1)S(1)} %collective-permute-done.1.refs_1_, bf16[64,2048]{1,0:T(8,128)(2,1)S(1)} %collective-permute-done.2.refs_2_, ...), custom_call_target="tpu_custom_call" | custom-call | tf_op jit(solution)/shard_map/project/pallas_call | solution.py:343
  52.5 3.4 %load.3.w_ref = bf16[2048,2048]{1,0:T(8,128)(2,1)S(1)} custom-call(bf16[2048,2048]{1,0:T(8,128)(2,1)} %refs_0_.1), custom_call_target="tpu_custom_call" | custom-call | tf_op jit(solution)/shard_map/load/pallas_call | solution.py:209
  56.0 11.6 %collective-permute-done.13.refs_0_ = bf16[256,1280]{1,0:T(8,128)(2,1)S(1)} collective-permute-done((bf16[256,1280]{1,0:T(8,128)(2,1)S(1)}, bf16[256,1280]{1,0:T(8,128)(2,1)S(1)}, u32[]{:S(2)}, u32[]{:S(2)}) %collective-permute-start.13) | collective-permute-done | bytes 655392 | tf_op jit(solution)/shard_map/ppermute | solution.py:529
  67.7 2.8 %attend.2.own_ref = bf16[128,1024]{1,0:T(8,128)(2,1)S(1)} custom-call(s32[3]{0:T(128)S(1)} %pad_add_fusion.place_ref, s32[4,2,8]{2,1,0:T(2,128)S(1)} %copy-done.3, s32[4,128]{1,0:T(4,128)S(1)} %copy-done.4, f32[256,1280]{1,0:T(8,128)S(1)} %convert_add_fusion.keep_ref, bf16[256,1280]{1,0:T(8,128)(2,1)S(1)} %collective-permute-done.13.refs_0_, ...), custom_call_target="tpu_custom_call" | custom-call | tf_op jit(solution)/shard_map/attend/pallas_call | solution.py:504
  74.0 2.7 %collective-permute-start.15 = (bf16[64,2048]{1,0:T(8,128)(2,1)S(1)}, bf16[64,2048]{1,0:T(8,128)(2,1)S(1)}, u32[]{:S(2)}, u32[]{:S(2)}) collective-permute-start(bf16[64,2048]{1,0:T(8,128)(2,1)S(1)} %get-tuple-element.77), channel_id=1, source_target_pairs={{0,8},{8,12},{12,4},{4,0},{1,9},{9,13},{13,5},{5,1},{2,10},{10,14}... | collective-permute-start | bytes 786440 | tf_op jit(solution)/shard_map/ppermute | solution.py:538
  76.7 2.8 %attend.3.own_ref = bf16[128,1024]{1,0:T(8,128)(2,1)S(1)} custom-call(s32[3]{0:T(128)S(1)} %pad_add_fusion.place_ref, s32[4,2,8]{2,1,0:T(2,128)S(1)} %copy-done.3, s32[4,128]{1,0:T(4,128)S(1)} %copy-done.4, f32[256,1280]{1,0:T(8,128)S(1)} %convert_add_fusion.keep_ref, bf16[256,1280]{1,0:T(8,128)(2,1)S(1)} %collective-permute-done.13.refs_0_, ...), custom_call_target="tpu_custom_call" | custom-call | tf_op jit(solution)/shard_map/attend/pallas_call | solution.py:504
  84.4 3.4 %collective-permute-start.20 = (bf16[64,2048]{1,0:T(8,128)(2,1)S(1)}, bf16[64,2048]{1,0:T(8,128)(2,1)S(1)}, u32[]{:S(2)}, u32[]{:S(2)}) collective-permute-start(bf16[64,2048]{1,0:T(8,128)(2,1)S(1)} %get-tuple-element.84), channel_id=1, source_target_pairs={{0,8},{8,12},{12,4},{4,0},{1,9},{9,13},{13,5},{5,1},{2,10},{10,14}... | collective-permute-start | bytes 786440 | tf_op jit(solution)/shard_map/ppermute | solution.py:538
  90.2 4.4 %collective-permute-done.20 = bf16[64,2048]{1,0:T(8,128)(2,1)S(1)} collective-permute-done((bf16[64,2048]{1,0:T(8,128)(2,1)S(1)}, bf16[64,2048]{1,0:T(8,128)(2,1)S(1)}, u32[]{:S(2)}, u32[]{:S(2)}) %collective-permute-start.20) | collective-permute-done | bytes 262176 | tf_op jit(solution)/shard_map/ppermute | solution.py:538
  94.6 3.4 %collective-permute-start.21 = (bf16[64,2048]{1,0:T(8,128)(2,1)S(1)}, bf16[64,2048]{1,0:T(8,128)(2,1)S(1)}, u32[]{:S(2)}, u32[]{:S(2)}) collective-permute-start(bf16[64,2048]{1,0:T(8,128)(2,1)S(1)} %add_convert_fusion.2), channel_id=1, source_target_pairs={{0,8},{8,12},{12,4},{4,0},{1,9},{9,13},{13,5},{5,1},{2,10},{10,14}... | collective-permute-start | bytes 786440 | tf_op jit(solution)/shard_map/ppermute | solution.py:538
  100.3 3.9 %collective-permute-done.21 = bf16[64,2048]{1,0:T(8,128)(2,1)S(1)} collective-permute-done((bf16[64,2048]{1,0:T(8,128)(2,1)S(1)}, bf16[64,2048]{1,0:T(8,128)(2,1)S(1)}, u32[]{:S(2)}, u32[]{:S(2)}) %collective-permute-start.21) | collective-permute-done | bytes 262176 | tf_op jit(solution)/shard_map/ppermute | solution.py:538
  104.1 3.4 %collective-permute-start.22 = (bf16[64,2048]{1,0:T(8,128)(2,1)S(1)}, bf16[64,2048]{1,0:T(8,128)(2,1)S(1)}, u32[]{:S(2)}, u32[]{:S(2)}) collective-permute-start(bf16[64,2048]{1,0:T(8,128)(2,1)S(1)} %add_convert_fusion.3), channel_id=1, source_target_pairs={{0,8},{8,12},{12,4},{4,0},{1,9},{9,13},{13,5},{5,1},{2,10},{10,14}... | collective-permute-start | bytes 786440 | tf_op jit(solution)/shard_map/ppermute | solution.py:538
  107.6 6.6 %collective-permute-done.22.running_ref = bf16[64,2048]{1,0:T(8,128)(2,1)S(1)} collective-permute-done((bf16[64,2048]{1,0:T(8,128)(2,1)S(1)}, bf16[64,2048]{1,0:T(8,128)(2,1)S(1)}, u32[]{:S(2)}, u32[]{:S(2)}) %collective-permute-start.22) | collective-permute-done | bytes 262176 | tf_op jit(solution)/shard_map/ppermute | solution.py:538
  119.3 4.3 %collective-permute-done.27.refs_2_ = bf16[32,2048]{1,0:T(8,128)(2,1)S(1)} collective-permute-done((bf16[32,2048]{1,0:T(8,128)(2,1)S(1)}, bf16[32,2048]{1,0:T(8,128)(2,1)S(1)}, u32[]{:S(2)}, u32[]{:S(2)}) %collective-permute-start.27) | collective-permute-done | bytes 131104 | tf_op jit(solution)/shard_map/ppermute | solution.py:529
  (71 shorter events, 37.8 us)
Async XLA Ops:
  3.2 10.9 %collective-permute-start.7 = (bf16[32,2048]{1,0:T(8,128)(2,1)S(1)}, bf16[32,2048]{1,0:T(8,128)(2,1)S(1)}, u32[]{:S(2)}, u32[]{:S(2)}) collective-permute-start(bf16[32,2048]{1,0:T(8,128)(2,1)S(1)} %get-tuple-element.68), channel_id=1, source_target_pairs={{0,2},{2,0},{1,3},{3,1},{4,6},{6,4},{5,7},{7,5},{8,10},{10,8},{9,1... | collective-permute-start | bytes 393224 | tf_op jit(solution)/shard_map/ppermute | solution.py:529
  5.8 8.4 %collective-permute-start.8 = (bf16[32,2048]{1,0:T(8,128)(2,1)S(1)}, bf16[32,2048]{1,0:T(8,128)(2,1)S(1)}, u32[]{:S(2)}, u32[]{:S(2)}) collective-permute-start(bf16[32,2048]{1,0:T(8,128)(2,1)S(1)} %get-tuple-element.69), channel_id=1, source_target_pairs={{0,3},{1,2},{2,1},{3,0},{4,7},{5,6},{6,5},{7,4},{8,11},{9,10},{10,... | collective-permute-start | bytes 393224 | tf_op jit(solution)/shard_map/ppermute | solution.py:535
  6.5 9.9 %collective-permute-start.1 = (bf16[64,2048]{1,0:T(8,128)(2,1)S(1)}, bf16[64,2048]{1,0:T(8,128)(2,1)S(1)}, u32[]{:S(2)}, u32[]{:S(2)}) collective-permute-start(bf16[64,2048]{1,0:T(8,128)(2,1)S(1)} %merge.2.refs_0_), channel_id=1, source_target_pairs={{0,8},{8,12},{12,4},{4,0},{1,9},{9,13},{13,5},{5,1},{2,10},{10,14}... | collective-permute-start | bytes 786440 | tf_op jit(solution)/shard_map/ppermute | solution.py:538
  14.1 4.8 %collective-permute-start.4 = (bf16[2,8,64,128]{3,2,1,0:T(8,128)(2,1)S(1)}, bf16[2,8,64,128]{3,2,1,0:T(8,128)(2,1)S(1)}, u32[]{:S(2)}, u32[]{:S(2)}) collective-permute-start(bf16[2,8,64,128]{3,2,1,0:T(8,128)(2,1)S(1)} %get-tuple-element.61), channel_id=1, source_target_pairs={{0,1},{1,0},{2,3},{3,2},{4,5},{5,4},{6,7},{7,6},{8,9},{9,8},{10,11... | collective-permute-start | bytes 786440 | tf_op jit(solution)/shard_map/ppermute | solution.py:532
  14.8 9.2 %collective-permute-start.9 = (bf16[64,2048]{1,0:T(8,128)(2,1)S(1)}, bf16[64,2048]{1,0:T(8,128)(2,1)S(1)}, u32[]{:S(2)}, u32[]{:S(2)}) collective-permute-start(bf16[64,2048]{1,0:T(8,128)(2,1)S(1)} %merge.3.refs_0_), channel_id=1, source_target_pairs={{0,8},{8,12},{12,4},{4,0},{1,9},{9,13},{13,5},{5,1},{2,10},{10,14}... | collective-permute-start | bytes 786440 | tf_op jit(solution)/shard_map/ppermute | solution.py:538
  16.4 13.1 %collective-permute-start.2 = (bf16[64,2048]{1,0:T(8,128)(2,1)S(1)}, bf16[64,2048]{1,0:T(8,128)(2,1)S(1)}, u32[]{:S(2)}, u32[]{:S(2)}) collective-permute-start(bf16[64,2048]{1,0:T(8,128)(2,1)S(1)} %collective-permute-done.1.refs_1_), channel_id=1, source_target_pairs={{0,8},{8,12},{12,4},{4,0},{1,9},{9,13},{13,5},{5,1},{2,10},{10,14}... | collective-permute-start | bytes 786440 | tf_op jit(solution)/shard_map/ppermute | solution.py:538
  18.9 21.9 %collective-permute-start.5 = (bf16[2,2,8,64,128]{4,3,2,1,0:T(8,128)(2,1)S(1)}, bf16[2,2,8,64,128]{4,3,2,1,0:T(8,128)(2,1)S(1)}, u32[]{:S(2)}, u32[]{:S(2)}) collective-permute-start(bf16[2,2,8,64,128]{4,3,2,1,0:T(8,128)(2,1)S(1)} %pad_maximum_fusion.refs_1_), channel_id=1, source_target_pairs={{0,2},{2,0},{1,3},{3,1},{4,6},{6,4},{5,7},{7,5},{8,10},{10,8},{9,1... | collective-permute-start | bytes 1572872 | tf_op jit(solution)/shard_map/ppermute | solution.py:529
  23.9 11.2 %collective-permute-start.10 = (bf16[64,2048]{1,0:T(8,128)(2,1)S(1)}, bf16[64,2048]{1,0:T(8,128)(2,1)S(1)}, u32[]{:S(2)}, u32[]{:S(2)}) collective-permute-start(bf16[64,2048]{1,0:T(8,128)(2,1)S(1)} %collective-permute-done.9.refs_1_), channel_id=1, source_target_pairs={{0,8},{8,12},{12,4},{4,0},{1,9},{9,13},{13,5},{5,1},{2,10},{10,14}... | collective-permute-start | bytes 786440 | tf_op jit(solution)/shard_map/ppermute | solution.py:538
  29.5 11.2 %collective-permute-start.3 = (bf16[64,2048]{1,0:T(8,128)(2,1)S(1)}, bf16[64,2048]{1,0:T(8,128)(2,1)S(1)}, u32[]{:S(2)}, u32[]{:S(2)}) collective-permute-start(bf16[64,2048]{1,0:T(8,128)(2,1)S(1)} %collective-permute-done.2.refs_2_), channel_id=1, source_target_pairs={{0,8},{8,12},{12,4},{4,0},{1,9},{9,13},{13,5},{5,1},{2,10},{10,14}... | collective-permute-start | bytes 786440 | tf_op jit(solution)/shard_map/ppermute | solution.py:538
  35.2 10.8 %collective-permute-start.11 = (bf16[64,2048]{1,0:T(8,128)(2,1)S(1)}, bf16[64,2048]{1,0:T(8,128)(2,1)S(1)}, u32[]{:S(2)}, u32[]{:S(2)}) collective-permute-start(bf16[64,2048]{1,0:T(8,128)(2,1)S(1)} %collective-permute-done.10.refs_2_), channel_id=1, source_target_pairs={{0,8},{8,12},{12,4},{4,0},{1,9},{9,13},{13,5},{5,1},{2,10},{10,14}... | collective-permute-start | bytes 786440 | tf_op jit(solution)/shard_map/ppermute | solution.py:538
  48.1 7.7 %collective-permute-start.6 = (bf16[256,1280]{1,0:T(8,128)(2,1)S(1)}, bf16[256,1280]{1,0:T(8,128)(2,1)S(1)}, u32[]{:S(2)}, u32[]{:S(2)}) collective-permute-start(bf16[256,1280]{1,0:T(8,128)(2,1)S(1)} %get-tuple-element.67), channel_id=1, source_target_pairs={{0,1},{1,0},{2,3},{3,2},{4,5},{5,4},{6,7},{7,6},{8,9},{9,8},{10,11... | collective-permute-start | bytes 1966088 | tf_op jit(solution)/shard_map/ppermute | solution.py:532
  50.9 16.8 %collective-permute-start.13 = (bf16[256,1280]{1,0:T(8,128)(2,1)S(1)}, bf16[256,1280]{1,0:T(8,128)(2,1)S(1)}, u32[]{:S(2)}, u32[]{:S(2)}) collective-permute-start(bf16[256,1280]{1,0:T(8,128)(2,1)S(1)} %add_convert_fusion), channel_id=1, source_target_pairs={{0,2},{2,0},{1,3},{3,1},{4,6},{6,4},{5,7},{7,5},{8,10},{10,8},{9,1... | collective-permute-start | bytes 1966088 | tf_op jit(solution)/shard_map/ppermute | solution.py:529
  70.6 8.9 %collective-permute-start.18 = (bf16[128,1024]{1,0:T(8,128)(2,1)S(1)}, bf16[128,1024]{1,0:T(8,128)(2,1)S(1)}, u32[]{:S(2)}, u32[]{:S(2)}) collective-permute-start(bf16[128,1024]{1,0:T(8,128)(2,1)S(1)} %attend.2.own_ref), channel_id=1, source_target_pairs={{0,2},{2,0},{1,3},{3,1},{4,6},{6,4},{5,7},{7,5},{8,10},{10,8},{9,1... | collective-permute-start | bytes 786440 | tf_op jit(solution)/shard_map/ppermute | solution.py:529
  74.0 8.6 %collective-permute-start.15 = (bf16[64,2048]{1,0:T(8,128)(2,1)S(1)}, bf16[64,2048]{1,0:T(8,128)(2,1)S(1)}, u32[]{:S(2)}, u32[]{:S(2)}) collective-permute-start(bf16[64,2048]{1,0:T(8,128)(2,1)S(1)} %get-tuple-element.77), channel_id=1, source_target_pairs={{0,8},{8,12},{12,4},{4,0},{1,9},{9,13},{13,5},{5,1},{2,10},{10,14}... | collective-permute-start | bytes 786440 | tf_op jit(solution)/shard_map/ppermute | solution.py:538
  79.6 8.8 %collective-permute-start.17 = (bf16[128,1024]{1,0:T(8,128)(2,1)S(1)}, bf16[128,1024]{1,0:T(8,128)(2,1)S(1)}, u32[]{:S(2)}, u32[]{:S(2)}) collective-permute-start(bf16[128,1024]{1,0:T(8,128)(2,1)S(1)} %attend.3.own_ref), channel_id=1, source_target_pairs={{0,1},{1,0},{2,3},{3,2},{4,5},{5,4},{6,7},{7,6},{8,9},{9,8},{10,11... | collective-permute-start | bytes 786440 | tf_op jit(solution)/shard_map/ppermute | solution.py:532
  80.0 8.3 %collective-permute-start.24 = (bf16[128,1024]{1,0:T(8,128)(2,1)S(1)}, bf16[128,1024]{1,0:T(8,128)(2,1)S(1)}, u32[]{:S(2)}, u32[]{:S(2)}) collective-permute-start(bf16[128,1024]{1,0:T(8,128)(2,1)S(1)} %attend.3.own_ref), channel_id=1, source_target_pairs={{0,2},{2,0},{1,3},{3,1},{4,6},{6,4},{5,7},{7,5},{8,10},{10,8},{9,1... | collective-permute-start | bytes 786440 | tf_op jit(solution)/shard_map/ppermute | solution.py:529
  84.4 10.2 %collective-permute-start.20 = (bf16[64,2048]{1,0:T(8,128)(2,1)S(1)}, bf16[64,2048]{1,0:T(8,128)(2,1)S(1)}, u32[]{:S(2)}, u32[]{:S(2)}) collective-permute-start(bf16[64,2048]{1,0:T(8,128)(2,1)S(1)} %get-tuple-element.84), channel_id=1, source_target_pairs={{0,8},{8,12},{12,4},{4,0},{1,9},{9,13},{13,5},{5,1},{2,10},{10,14}... | collective-permute-start | bytes 786440 | tf_op jit(solution)/shard_map/ppermute | solution.py:538
  87.9 12.3 %collective-permute-start.16 = (bf16[64,2048]{1,0:T(8,128)(2,1)S(1)}, bf16[64,2048]{1,0:T(8,128)(2,1)S(1)}, u32[]{:S(2)}, u32[]{:S(2)}) collective-permute-start(bf16[64,2048]{1,0:T(8,128)(2,1)S(1)} %add_convert_fusion.4), channel_id=1, source_target_pairs={{0,8},{8,12},{12,4},{4,0},{1,9},{9,13},{13,5},{5,1},{2,10},{10,14}... | collective-permute-start | bytes 786440 | tf_op jit(solution)/shard_map/ppermute | solution.py:538
  88.3 9.7 %collective-permute-start.25 = (bf16[128,1024]{1,0:T(8,128)(2,1)S(1)}, bf16[128,1024]{1,0:T(8,128)(2,1)S(1)}, u32[]{:S(2)}, u32[]{:S(2)}) collective-permute-start(bf16[128,1024]{1,0:T(8,128)(2,1)S(1)} %collective-permute-done.24.own_ref), channel_id=1, source_target_pairs={{0,1},{1,0},{2,3},{3,2},{4,5},{5,4},{6,7},{7,6},{8,9},{9,8},{10,11... | collective-permute-start | bytes 786440 | tf_op jit(solution)/shard_map/ppermute | solution.py:532
  94.6 9.5 %collective-permute-start.21 = (bf16[64,2048]{1,0:T(8,128)(2,1)S(1)}, bf16[64,2048]{1,0:T(8,128)(2,1)S(1)}, u32[]{:S(2)}, u32[]{:S(2)}) collective-permute-start(bf16[64,2048]{1,0:T(8,128)(2,1)S(1)} %add_convert_fusion.2), channel_id=1, source_target_pairs={{0,8},{8,12},{12,4},{4,0},{1,9},{9,13},{13,5},{5,1},{2,10},{10,14}... | collective-permute-start | bytes 786440 | tf_op jit(solution)/shard_map/ppermute | solution.py:538
  104.1 10.1 %collective-permute-start.22 = (bf16[64,2048]{1,0:T(8,128)(2,1)S(1)}, bf16[64,2048]{1,0:T(8,128)(2,1)S(1)}, u32[]{:S(2)}, u32[]{:S(2)}) collective-permute-start(bf16[64,2048]{1,0:T(8,128)(2,1)S(1)} %add_convert_fusion.3), channel_id=1, source_target_pairs={{0,8},{8,12},{12,4},{4,0},{1,9},{9,13},{13,5},{5,1},{2,10},{10,14}... | collective-permute-start | bytes 786440 | tf_op jit(solution)/shard_map/ppermute | solution.py:538
  107.6 9.7 %collective-permute-start.26 = (bf16[64,2048]{1,0:T(8,128)(2,1)S(1)}, bf16[64,2048]{1,0:T(8,128)(2,1)S(1)}, u32[]{:S(2)}, u32[]{:S(2)}) collective-permute-start(bf16[64,2048]{1,0:T(8,128)(2,1)S(1)} %add_convert_fusion.1), channel_id=1, source_target_pairs={{0,8},{8,12},{12,4},{4,0},{1,9},{9,13},{13,5},{5,1},{2,10},{10,14}... | collective-permute-start | bytes 786440 | tf_op jit(solution)/shard_map/ppermute | solution.py:538
  117.9 5.7 %collective-permute-start.27 = (bf16[32,2048]{1,0:T(8,128)(2,1)S(1)}, bf16[32,2048]{1,0:T(8,128)(2,1)S(1)}, u32[]{:S(2)}, u32[]{:S(2)}) collective-permute-start(bf16[32,2048]{1,0:T(8,128)(2,1)S(1)} %get-tuple-element.93), channel_id=1, source_target_pairs={{0,2},{2,0},{1,3},{3,1},{4,6},{6,4},{5,7},{7,5},{8,10},{10,8},{9,1... | collective-permute-start | bytes 393224 | tf_op jit(solution)/shard_map/ppermute | solution.py:529
  119.3 5.8 %collective-permute-start.28 = (bf16[32,2048]{1,0:T(8,128)(2,1)S(1)}, bf16[32,2048]{1,0:T(8,128)(2,1)S(1)}, u32[]{:S(2)}, u32[]{:S(2)}) collective-permute-start(bf16[32,2048]{1,0:T(8,128)(2,1)S(1)} %get-tuple-element.94), channel_id=1, source_target_pairs={{0,3},{1,2},{2,1},{3,0},{4,7},{5,6},{6,5},{7,4},{8,11},{9,10},{10,... | collective-permute-start | bytes 393224 | tf_op jit(solution)/shard_map/ppermute | solution.py:535
  (10 other events, 53.4 us)

commit v3 on v2

--- a/solution.py
+++ b/solution.py
@@ -270,48 +270,52 @@
     )(place, mine, theirs)
 
 
-def share_kernel(place_ref, running_ref, term_ref, mine_ref, give_ref):
+def share_kernel(place_ref, *refs):
+    terms, (mine_ref, give_ref) = refs[:-2], refs[-2:]
     rows = mine_ref.shape[0]
     kv = place_ref[1]
     for core, ref in ((kv, mine_ref), (1 - kv, give_ref)):
         at = pl.ds(pl.multiple_of(core * rows, rows), rows)
-        total = running_ref[at, :].astype(jnp.float32) + term_ref[at, :].astype(jnp.float32)
+        total = sum(term[at, :].astype(jnp.float32) for term in terms)
         ref[...] = total.astype(ref.dtype)
 
 
-def share(place, running, term):
-    rows, columns = running.shape
+def share(place, *terms):
+    rows, columns = terms[0].shape
     whole = pl.BlockSpec(memory_space=pltpu.VMEM)
     return pl.pallas_call(
         share_kernel,
-        in_specs=[pl.BlockSpec(memory_space=pltpu.SMEM)] + [whole] * 2,
+        in_specs=[pl.BlockSpec(memory_space=pltpu.SMEM)] + [whole] * len(terms),
         out_specs=[whole] * 2,
-        out_shape=[jax.ShapeDtypeStruct((rows // 2, columns), running.dtype)] * 2,
+        out_shape=[jax.ShapeDtypeStruct((rows // 2, columns), terms[0].dtype)] * 2,
         compiler_params=pltpu.CompilerParams(vmem_limit_bytes=4 * MIB),
         name="share",
-    )(place, running, term)
+    )(place, *terms)
 
 
 def collect_kernel(place_ref, *refs):
-    out_ref = refs[-1]
-    width = refs[0].shape[1]
+    terms, out_ref = refs[:-1], refs[-1]
+    width = terms[0].shape[1]
     req, kv = place_ref[0], place_ref[1]
     of = (2 * req + kv, 2 * req + 1 - kv, 2 - 2 * req + kv, 3 - 2 * req - kv)
-    for quarter, ref in zip(of, refs[:-1]):
-        out_ref[0, :, pl.ds(pl.multiple_of(quarter * width, width), width)] = ref[...]
-
-
-def collect(place, *quarters):
-    rows, columns = quarters[0].shape
+    pairs = (terms[:1], terms[1:2], terms[2:4], terms[4:])
+    for quarter, pair in zip(of, pairs):
+        total = sum(term[...].astype(jnp.float32) for term in pair)
+        at = pl.ds(pl.multiple_of(quarter * width, width), width)
+        out_ref[0, :, at] = total.astype(out_ref.dtype)
+
+
+def collect(place, mine, theirs, same, cross):
+    rows, columns = mine.shape
     whole = pl.BlockSpec(memory_space=pltpu.VMEM)
     return pl.pallas_call(
         collect_kernel,
-        in_specs=[pl.BlockSpec(memory_space=pltpu.SMEM)] + [whole] * 4,
+        in_specs=[pl.BlockSpec(memory_space=pltpu.SMEM)] + [whole] * 6,
         out_specs=whole,
-        out_shape=jax.ShapeDtypeStruct((1, rows, 4 * columns), quarters[0].dtype),
+        out_shape=jax.ShapeDtypeStruct((1, rows, 4 * columns), mine.dtype),
         compiler_params=pltpu.CompilerParams(vmem_limit_bytes=4 * MIB),
         name="collect",
-    )(place, *quarters)
+    )(place, mine, theirs, *same, *cross)
 
 
 def project_kernel(flips, place_ref, *refs):
@@ -537,6 +541,22 @@
     def onward(x):
         return lax.ppermute(x, "tp", forward)
 
+    def slanted(same, cross):
+        axes = ("tp", "req", "kv")
+        return [
+            lax.ppermute(
+                x,
+                axes,
+                [
+                    (4 * low + 2 * r + c, 4 * high + 2 * (1 - r) + (c ^ flip))
+                    for low, high in forward
+                    for r in range(2)
+                    for c in range(2)
+                ],
+            )
+            for flip, x in enumerate((same, cross))
+        ]
+
     kept, give, far_same, far_cross = norm(place, tokens, norm_gain)
     near = merge(place, kept, swap_kv(give))
     far = merge(place, swap_req(far_same), swap_both(far_cross))
@@ -594,14 +614,16 @@
     projected(near_sum, halves[1], last, swap_kv(last))
     last_far = after(last_far, near_run)
     projected(far_sum, halves[1], last_far, swap_kv(last_far))
+
+    beside = share(place, after(far_sum[0], far_run))
+    beside = (swap_req(beside[0]), swap_both(beside[1]))
     for j in range(2, count):
-        near_term = plus(near_run, near_sum[j])
-        near_run = onward(after(near_term, far_run) if j == count - 1 else near_term)
-        far_run = onward(plus(far_run, far_sum[j]))
-    mine, give = share(place, far_run, far_sum[0])
-    away = (swap_req(mine), swap_both(give))
+        near_run = onward(plus(near_run, near_sum[j]))
+        if j < count - 1:
+            far_run = onward(plus(far_run, far_sum[j]))
+    ends = slanted(*share(place, far_run, far_sum[count - 1]))
     mine, give = share(place, near_run, near_sum[0])
-    return collect(place, mine, swap_kv(give), *away)
+    return collect(place, mine, swap_kv(give), *zip(ends, beside))
 
 
 def fits(shape):

time: 127 us -> 120 us (0.945)
  waiting for transfers between devices: 50.9 us -> 38.8 us
  starting transfers between devices: 39.6 us -> 44.3 us
    ppermute x12 -> x11, waiting for transfers between devices: 33.1 us -> 21.5 us  [onward(): return lax.ppermute(x, 'tp', forward)]
    ppermute x6, waiting for transfers between devices: 16.3 us -> 12 us  [swap_req(): return lax.ppermute(x, 'req', SWAP)]
    ppermute x0 -> x2, starting transfers between devices: none -> 4.26 us  [slanted(): lax.ppermute(x, axes, [(4 * low + 2 * r + c, 4 * high + 2 * (1 - r) + (c...]
    ppermute x2, waiting for transfers between devices: 1.5 us -> 3.91 us  [swap_both(): return lax.ppermute(x, ('req', 'kv'), [(i, 3 - i) for i in range(4)])]
    ppermute x0 -> x2, waiting for transfers between devices: none -> 1.37 us  [slanted(): lax.ppermute(x, axes, [(4 * low + 2 * r + c, 4 * high + 2 * (1 - r) + (c...]
    ppermute x12 -> x11, starting transfers between devices: 27.4 us -> 27.4 us  [onward(): return lax.ppermute(x, 'tp', forward)]
  transfers between devices with their start and end apart: 29 -> 30, of which waited for: 15 -> 13; matrix products, arithmetic and copies ran while one was open for 0% -> 0% of each run, Pallas kernels for 21% -> 22%
where the time goes in v3:
time: 120 us
  starting transfers between devices  44.3 us (37%)
  waiting for transfers between devices  38.8 us (32%)
  Pallas kernels  33.8 us (28%)
  local copies, waits for them, and re-layouts  1.8 us (2%)
    ppermute x11, starting transfers between devices, onward(): return lax.ppermute(x, 'tp', forward)  27.4 us
    ppermute x11, waiting for transfers between devices, onward(): return lax.ppermute(x, 'tp', forward)  21.5 us
    ppermute x6, waiting for transfers between devices, swap_req(): return lax.ppermute(x, 'req', SWAP)  12 us
    ppermute x6, starting transfers between devices, swap_req(): return lax.ppermute(x, 'req', SWAP)  10.3 us
    pallas_call x3, Pallas kernels, project(): pl.pallas_call(functools.partial(project_kernel, flips), in_specs=[pl.Blo...  7.72 us
    pallas_call x2, Pallas kernels, load(): pl.pallas_call(functools.partial(load_kernel, count), in_specs=[pl.BlockS...  7.32 us
    pallas_call x4, Pallas kernels, out_project(): pl.pallas_call(out_kernel, in_specs=[pl.BlockSpec(memory_space=pltpu.SMEM...  7.26 us
    pallas_call x2, Pallas kernels, attend(): pl.pallas_call(functools.partial(attend_kernel, wanted, order), in_specs=...  5.6 us
  transfers between devices with their start and end apart: 30, of which 13 were waited for; matrix products, arithmetic and copies ran while one was open for 0% of the time, Pallas kernels for 22%

profile of v3, /device:TPU:0, one launch (start us, length us, event | category | flops | bytes accessed | tf_op | source)
XLA Modules:
  0.0 119.6 jit_solution(4396309949179060054)
XLA Ops:
  3.2 2.6 %collective-permute-start.7 = (bf16[32,2048]{1,0:T(8,128)(2,1)S(1)}, bf16[32,2048]{1,0:T(8,128)(2,1)S(1)}, u32[]{:S(2)}, u32[]{:S(2)}) collective-permute-start(bf16[32,2048]{1,0:T(8,128)(2,1)S(1)} %get-tuple-element.70), channel_id=1, source_target_pairs={{0,2},{2,0},{1,3},{3,1},{4,6},{6,4},{5,7},{7,5},{8,10},{10,8},{9,1... | collective-permute-start | bytes 393224 | tf_op jit(solution)/shard_map/ppermute | solution.py:533
  6.5 2.9 %collective-permute-start.1 = (bf16[64,2048]{1,0:T(8,128)(2,1)S(1)}, bf16[64,2048]{1,0:T(8,128)(2,1)S(1)}, u32[]{:S(2)}, u32[]{:S(2)}) collective-permute-start(bf16[64,2048]{1,0:T(8,128)(2,1)S(1)} %merge.2.refs_0_), channel_id=1, source_target_pairs={{0,8},{8,12},{12,4},{4,0},{1,9},{9,13},{13,5},{5,1},{2,10},{10,14}... | collective-permute-start | bytes 786440 | tf_op jit(solution)/shard_map/ppermute | solution.py:542
  9.4 3.9 %load.2 = (bf16[2048,2048]{1,0:T(8,128)(2,1)S(1)}, bf16[2048,256]{1,0:T(8,128)(2,1)S(1)}, bf16[2048,256]{1,0:T(8,128)(2,1)S(1)}) custom-call(bf16[2048,2048]{1,0:T(8,128)(2,1)} %refs_0_, bf16[2048,256]{1,0:T(8,128)(2,1)} %refs_1_, bf16[2048,256]{1,0:T(8,128)(2,1)} %refs_2_), custom_call_target="tpu_custom_call" | custom-call | tf_op jit(solution)/shard_map/load/pallas_call | solution.py:209
  16.4 2.4 %collective-permute-start.2 = (bf16[64,2048]{1,0:T(8,128)(2,1)S(1)}, bf16[64,2048]{1,0:T(8,128)(2,1)S(1)}, u32[]{:S(2)}, u32[]{:S(2)}) collective-permute-start(bf16[64,2048]{1,0:T(8,128)(2,1)S(1)} %collective-permute-done.1.refs_1_), channel_id=1, source_target_pairs={{0,8},{8,12},{12,4},{4,0},{1,9},{9,13},{13,5},{5,1},{2,10},{10,14}... | collective-permute-start | bytes 786440 | tf_op jit(solution)/shard_map/ppermute | solution.py:542
  20.4 3.5 %collective-permute-done.9.refs_1_ = bf16[64,2048]{1,0:T(8,128)(2,1)S(1)} collective-permute-done((bf16[64,2048]{1,0:T(8,128)(2,1)S(1)}, bf16[64,2048]{1,0:T(8,128)(2,1)S(1)}, u32[]{:S(2)}, u32[]{:S(2)}) %collective-permute-start.9) | collective-permute-done | bytes 262176 | tf_op jit(solution)/shard_map/ppermute | solution.py:542
  23.9 2.5 %collective-permute-start.10 = (bf16[64,2048]{1,0:T(8,128)(2,1)S(1)}, bf16[64,2048]{1,0:T(8,128)(2,1)S(1)}, u32[]{:S(2)}, u32[]{:S(2)}) collective-permute-start(bf16[64,2048]{1,0:T(8,128)(2,1)S(1)} %collective-permute-done.9.refs_1_), channel_id=1, source_target_pairs={{0,8},{8,12},{12,4},{4,0},{1,9},{9,13},{13,5},{5,1},{2,10},{10,14}... | collective-permute-start | bytes 786440 | tf_op jit(solution)/shard_map/ppermute | solution.py:542
  26.4 3.1 %collective-permute-done.2.refs_2_ = bf16[64,2048]{1,0:T(8,128)(2,1)S(1)} collective-permute-done((bf16[64,2048]{1,0:T(8,128)(2,1)S(1)}, bf16[64,2048]{1,0:T(8,128)(2,1)S(1)}, u32[]{:S(2)}, u32[]{:S(2)}) %collective-permute-start.2) | collective-permute-done | bytes 262176 | tf_op jit(solution)/shard_map/ppermute | solution.py:542
  29.5 2.5 %collective-permute-start.3 = (bf16[64,2048]{1,0:T(8,128)(2,1)S(1)}, bf16[64,2048]{1,0:T(8,128)(2,1)S(1)}, u32[]{:S(2)}, u32[]{:S(2)}) collective-permute-start(bf16[64,2048]{1,0:T(8,128)(2,1)S(1)} %collective-permute-done.2.refs_2_), channel_id=1, source_target_pairs={{0,8},{8,12},{12,4},{4,0},{1,9},{9,13},{13,5},{5,1},{2,10},{10,14}... | collective-permute-start | bytes 786440 | tf_op jit(solution)/shard_map/ppermute | solution.py:542
  32.0 3.1 %collective-permute-done.10.refs_2_ = bf16[64,2048]{1,0:T(8,128)(2,1)S(1)} collective-permute-done((bf16[64,2048]{1,0:T(8,128)(2,1)S(1)}, bf16[64,2048]{1,0:T(8,128)(2,1)S(1)}, u32[]{:S(2)}, u32[]{:S(2)}) %collective-permute-start.10) | collective-permute-done | bytes 262176 | tf_op jit(solution)/shard_map/ppermute | solution.py:542
  35.2 2.5 %collective-permute-start.11 = (bf16[64,2048]{1,0:T(8,128)(2,1)S(1)}, bf16[64,2048]{1,0:T(8,128)(2,1)S(1)}, u32[]{:S(2)}, u32[]{:S(2)}) collective-permute-start(bf16[64,2048]{1,0:T(8,128)(2,1)S(1)} %collective-permute-done.10.refs_2_), channel_id=1, source_target_pairs={{0,8},{8,12},{12,4},{4,0},{1,9},{9,13},{13,5},{5,1},{2,10},{10,14}... | collective-permute-start | bytes 786440 | tf_op jit(solution)/shard_map/ppermute | solution.py:542
  37.6 3.1 %collective-permute-done.3.refs_3_ = bf16[64,2048]{1,0:T(8,128)(2,1)S(1)} collective-permute-done((bf16[64,2048]{1,0:T(8,128)(2,1)S(1)}, bf16[64,2048]{1,0:T(8,128)(2,1)S(1)}, u32[]{:S(2)}, u32[]{:S(2)}) %collective-permute-start.3) | collective-permute-done | bytes 262176 | tf_op jit(solution)/shard_map/ppermute | solution.py:542
  40.8 3.5 %project.3 = (bf16[256,1280]{1,0:T(8,128)(2,1)S(1)}, f32[256,1280]{1,0:T(8,128)S(1)}) custom-call(s32[3]{0:T(128)S(1)} %pad_add_fusion.place_ref, bf16[64,2048]{1,0:T(8,128)(2,1)S(1)} %merge.2.refs_0_, bf16[64,2048]{1,0:T(8,128)(2,1)S(1)} %collective-permute-done.1.refs_1_, bf16[64,2048]{1,0:T(8,128)(2,1)S(1)} %collective-permute-done.2.refs_2_, ...), custom_call_target="tpu_custom_call" | custom-call | tf_op jit(solution)/shard_map/project/pallas_call | solution.py:347
  52.5 3.4 %load.3.w_ref = bf16[2048,2048]{1,0:T(8,128)(2,1)S(1)} custom-call(bf16[2048,2048]{1,0:T(8,128)(2,1)} %refs_0_.1), custom_call_target="tpu_custom_call" | custom-call | tf_op jit(solution)/shard_map/load/pallas_call | solution.py:209
  56.0 11.6 %collective-permute-done.13.refs_0_ = bf16[256,1280]{1,0:T(8,128)(2,1)S(1)} collective-permute-done((bf16[256,1280]{1,0:T(8,128)(2,1)S(1)}, bf16[256,1280]{1,0:T(8,128)(2,1)S(1)}, u32[]{:S(2)}, u32[]{:S(2)}) %collective-permute-start.13) | collective-permute-done | bytes 655392 | tf_op jit(solution)/shard_map/ppermute | solution.py:533
  67.7 2.8 %attend.2.own_ref = bf16[128,1024]{1,0:T(8,128)(2,1)S(1)} custom-call(s32[3]{0:T(128)S(1)} %pad_add_fusion.place_ref, s32[4,2,8]{2,1,0:T(2,128)S(1)} %copy-done.3, s32[4,128]{1,0:T(4,128)S(1)} %copy-done.4, f32[256,1280]{1,0:T(8,128)S(1)} %convert_add_fusion.keep_ref, bf16[256,1280]{1,0:T(8,128)(2,1)S(1)} %collective-permute-done.13.refs_0_, ...), custom_call_target="tpu_custom_call" | custom-call | tf_op jit(solution)/shard_map/attend/pallas_call | solution.py:508
  74.0 2.7 %collective-permute-start.15 = (bf16[64,2048]{1,0:T(8,128)(2,1)S(1)}, bf16[64,2048]{1,0:T(8,128)(2,1)S(1)}, u32[]{:S(2)}, u32[]{:S(2)}) collective-permute-start(bf16[64,2048]{1,0:T(8,128)(2,1)S(1)} %get-tuple-element.79), channel_id=1, source_target_pairs={{0,8},{8,12},{12,4},{4,0},{1,9},{9,13},{13,5},{5,1},{2,10},{10,14}... | collective-permute-start | bytes 786440 | tf_op jit(solution)/shard_map/ppermute | solution.py:542
  76.7 2.8 %attend.3.own_ref = bf16[128,1024]{1,0:T(8,128)(2,1)S(1)} custom-call(s32[3]{0:T(128)S(1)} %pad_add_fusion.place_ref, s32[4,2,8]{2,1,0:T(2,128)S(1)} %copy-done.3, s32[4,128]{1,0:T(4,128)S(1)} %copy-done.4, f32[256,1280]{1,0:T(8,128)S(1)} %convert_add_fusion.keep_ref, bf16[256,1280]{1,0:T(8,128)(2,1)S(1)} %collective-permute-done.13.refs_0_, ...), custom_call_target="tpu_custom_call" | custom-call | tf_op jit(solution)/shard_map/attend/pallas_call | solution.py:508
  82.6 3.4 %collective-permute-start.16 = (bf16[64,2048]{1,0:T(8,128)(2,1)S(1)}, bf16[64,2048]{1,0:T(8,128)(2,1)S(1)}, u32[]{:S(2)}, u32[]{:S(2)}) collective-permute-start(bf16[64,2048]{1,0:T(8,128)(2,1)S(1)} %add_convert_fusion.3), channel_id=1, source_target_pairs={{0,8},{8,12},{12,4},{4,0},{1,9},{9,13},{13,5},{5,1},{2,10},{10,14}... | collective-permute-start | bytes 786440 | tf_op jit(solution)/shard_map/ppermute | solution.py:542
  90.1 2.7 %collective-permute-done.16 = bf16[64,2048]{1,0:T(8,128)(2,1)S(1)} collective-permute-done((bf16[64,2048]{1,0:T(8,128)(2,1)S(1)}, bf16[64,2048]{1,0:T(8,128)(2,1)S(1)}, u32[]{:S(2)}, u32[]{:S(2)}) %collective-permute-start.16) | collective-permute-done | bytes 262176 | tf_op jit(solution)/shard_map/ppermute | solution.py:542
  92.9 3.4 %collective-permute-start.18 = (bf16[64,2048]{1,0:T(8,128)(2,1)S(1)}, bf16[64,2048]{1,0:T(8,128)(2,1)S(1)}, u32[]{:S(2)}, u32[]{:S(2)}) collective-permute-start(bf16[64,2048]{1,0:T(8,128)(2,1)S(1)} %add_convert_fusion.2), channel_id=1, source_target_pairs={{0,8},{8,12},{12,4},{4,0},{1,9},{9,13},{13,5},{5,1},{2,10},{10,14}... | collective-permute-start | bytes 786440 | tf_op jit(solution)/shard_map/ppermute | solution.py:542
  96.3 2.1 %collective-permute-done.22 = bf16[64,2048]{1,0:T(8,128)(2,1)S(1)} collective-permute-done((bf16[64,2048]{1,0:T(8,128)(2,1)S(1)}, bf16[64,2048]{1,0:T(8,128)(2,1)S(1)}, u32[]{:S(2)}, u32[]{:S(2)}) %collective-permute-start.22) | collective-permute-done | bytes 262176 | tf_op jit(solution)/shard_map/ppermute | solution.py:542
  98.5 3.4 %collective-permute-start.23 = (bf16[64,2048]{1,0:T(8,128)(2,1)S(1)}, bf16[64,2048]{1,0:T(8,128)(2,1)S(1)}, u32[]{:S(2)}, u32[]{:S(2)}) collective-permute-start(bf16[64,2048]{1,0:T(8,128)(2,1)S(1)} %add_convert_fusion.1), channel_id=1, source_target_pairs={{0,8},{8,12},{12,4},{4,0},{1,9},{9,13},{13,5},{5,1},{2,10},{10,14}... | collective-permute-start | bytes 786440 | tf_op jit(solution)/shard_map/ppermute | solution.py:542
  108.6 4.3 %collective-permute-start.26 = (bf16[32,2048]{1,0:T(8,128)(2,1)S(1)}, bf16[32,2048]{1,0:T(8,128)(2,1)S(1)}, u32[]{:S(2)}, u32[]{:S(2)}) collective-permute-start(bf16[32,2048]{1,0:T(8,128)(2,1)S(1)} %get-tuple-element.93), channel_id=1, source_target_pairs={{0,10},{1,11},{2,8},{3,9},{8,14},{9,15},{10,12},{11,13},{12,6},{13... | collective-permute-start | bytes 393224 | tf_op jit(solution)/shard_map/ppermute | solution.py:547
  112.9 3.9 %collective-permute-done.29.refs_5_ = bf16[32,2048]{1,0:T(8,128)(2,1)S(1)} collective-permute-done((bf16[32,2048]{1,0:T(8,128)(2,1)S(1)}, bf16[32,2048]{1,0:T(8,128)(2,1)S(1)}, u32[]{:S(2)}, u32[]{:S(2)}) %collective-permute-start.29) | collective-permute-done | bytes 131104 | tf_op jit(solution)/shard_map/ppermute | solution.py:539
  (73 shorter events, 37.0 us)
Async XLA Ops:
  3.2 10.9 %collective-permute-start.7 = (bf16[32,2048]{1,0:T(8,128)(2,1)S(1)}, bf16[32,2048]{1,0:T(8,128)(2,1)S(1)}, u32[]{:S(2)}, u32[]{:S(2)}) collective-permute-start(bf16[32,2048]{1,0:T(8,128)(2,1)S(1)} %get-tuple-element.70), channel_id=1, source_target_pairs={{0,2},{2,0},{1,3},{3,1},{4,6},{6,4},{5,7},{7,5},{8,10},{10,8},{9,1... | collective-permute-start | bytes 393224 | tf_op jit(solution)/shard_map/ppermute | solution.py:533
  5.8 8.4 %collective-permute-start.8 = (bf16[32,2048]{1,0:T(8,128)(2,1)S(1)}, bf16[32,2048]{1,0:T(8,128)(2,1)S(1)}, u32[]{:S(2)}, u32[]{:S(2)}) collective-permute-start(bf16[32,2048]{1,0:T(8,128)(2,1)S(1)} %get-tuple-element.71), channel_id=1, source_target_pairs={{0,3},{1,2},{2,1},{3,0},{4,7},{5,6},{6,5},{7,4},{8,11},{9,10},{10,... | collective-permute-start | bytes 393224 | tf_op jit(solution)/shard_map/ppermute | solution.py:539
  6.5 9.9 %collective-permute-start.1 = (bf16[64,2048]{1,0:T(8,128)(2,1)S(1)}, bf16[64,2048]{1,0:T(8,128)(2,1)S(1)}, u32[]{:S(2)}, u32[]{:S(2)}) collective-permute-start(bf16[64,2048]{1,0:T(8,128)(2,1)S(1)} %merge.2.refs_0_), channel_id=1, source_target_pairs={{0,8},{8,12},{12,4},{4,0},{1,9},{9,13},{13,5},{5,1},{2,10},{10,14}... | collective-permute-start | bytes 786440 | tf_op jit(solution)/shard_map/ppermute | solution.py:542
  14.8 9.2 %collective-permute-start.9 = (bf16[64,2048]{1,0:T(8,128)(2,1)S(1)}, bf16[64,2048]{1,0:T(8,128)(2,1)S(1)}, u32[]{:S(2)}, u32[]{:S(2)}) collective-permute-start(bf16[64,2048]{1,0:T(8,128)(2,1)S(1)} %merge.3.refs_0_), channel_id=1, source_target_pairs={{0,8},{8,12},{12,4},{4,0},{1,9},{9,13},{13,5},{5,1},{2,10},{10,14}... | collective-permute-start | bytes 786440 | tf_op jit(solution)/shard_map/ppermute | solution.py:542
  16.4 13.1 %collective-permute-start.2 = (bf16[64,2048]{1,0:T(8,128)(2,1)S(1)}, bf16[64,2048]{1,0:T(8,128)(2,1)S(1)}, u32[]{:S(2)}, u32[]{:S(2)}) collective-permute-start(bf16[64,2048]{1,0:T(8,128)(2,1)S(1)} %collective-permute-done.1.refs_1_), channel_id=1, source_target_pairs={{0,8},{8,12},{12,4},{4,0},{1,9},{9,13},{13,5},{5,1},{2,10},{10,14}... | collective-permute-start | bytes 786440 | tf_op jit(solution)/shard_map/ppermute | solution.py:542
  18.9 21.9 %collective-permute-start.5 = (bf16[2,2,8,64,128]{4,3,2,1,0:T(8,128)(2,1)S(1)}, bf16[2,2,8,64,128]{4,3,2,1,0:T(8,128)(2,1)S(1)}, u32[]{:S(2)}, u32[]{:S(2)}) collective-permute-start(bf16[2,2,8,64,128]{4,3,2,1,0:T(8,128)(2,1)S(1)} %pad_maximum_fusion.refs_1_), channel_id=1, source_target_pairs={{0,2},{2,0},{1,3},{3,1},{4,6},{6,4},{5,7},{7,5},{8,10},{10,8},{9,1... | collective-permute-start | bytes 1572872 | tf_op jit(solution)/shard_map/ppermute | solution.py:533
  23.9 11.2 %collective-permute-start.10 = (bf16[64,2048]{1,0:T(8,128)(2,1)S(1)}, bf16[64,2048]{1,0:T(8,128)(2,1)S(1)}, u32[]{:S(2)}, u32[]{:S(2)}) collective-permute-start(bf16[64,2048]{1,0:T(8,128)(2,1)S(1)} %collective-permute-done.9.refs_1_), channel_id=1, source_target_pairs={{0,8},{8,12},{12,4},{4,0},{1,9},{9,13},{13,5},{5,1},{2,10},{10,14}... | collective-permute-start | bytes 786440 | tf_op jit(solution)/shard_map/ppermute | solution.py:542
  29.5 11.2 %collective-permute-start.3 = (bf16[64,2048]{1,0:T(8,128)(2,1)S(1)}, bf16[64,2048]{1,0:T(8,128)(2,1)S(1)}, u32[]{:S(2)}, u32[]{:S(2)}) collective-permute-start(bf16[64,2048]{1,0:T(8,128)(2,1)S(1)} %collective-permute-done.2.refs_2_), channel_id=1, source_target_pairs={{0,8},{8,12},{12,4},{4,0},{1,9},{9,13},{13,5},{5,1},{2,10},{10,14}... | collective-permute-start | bytes 786440 | tf_op jit(solution)/shard_map/ppermute | solution.py:542
  35.2 10.8 %collective-permute-start.11 = (bf16[64,2048]{1,0:T(8,128)(2,1)S(1)}, bf16[64,2048]{1,0:T(8,128)(2,1)S(1)}, u32[]{:S(2)}, u32[]{:S(2)}) collective-permute-start(bf16[64,2048]{1,0:T(8,128)(2,1)S(1)} %collective-permute-done.10.refs_2_), channel_id=1, source_target_pairs={{0,8},{8,12},{12,4},{4,0},{1,9},{9,13},{13,5},{5,1},{2,10},{10,14}... | collective-permute-start | bytes 786440 | tf_op jit(solution)/shard_map/ppermute | solution.py:542
  48.1 7.7 %collective-permute-start.6 = (bf16[256,1280]{1,0:T(8,128)(2,1)S(1)}, bf16[256,1280]{1,0:T(8,128)(2,1)S(1)}, u32[]{:S(2)}, u32[]{:S(2)}) collective-permute-start(bf16[256,1280]{1,0:T(8,128)(2,1)S(1)} %get-tuple-element.69), channel_id=1, source_target_pairs={{0,1},{1,0},{2,3},{3,2},{4,5},{5,4},{6,7},{7,6},{8,9},{9,8},{10,11... | collective-permute-start | bytes 1966088 | tf_op jit(solution)/shard_map/ppermute | solution.py:536
  50.9 16.8 %collective-permute-start.13 = (bf16[256,1280]{1,0:T(8,128)(2,1)S(1)}, bf16[256,1280]{1,0:T(8,128)(2,1)S(1)}, u32[]{:S(2)}, u32[]{:S(2)}) collective-permute-start(bf16[256,1280]{1,0:T(8,128)(2,1)S(1)} %add_convert_fusion), channel_id=1, source_target_pairs={{0,2},{2,0},{1,3},{3,1},{4,6},{6,4},{5,7},{7,5},{8,10},{10,8},{9,1... | collective-permute-start | bytes 1966088 | tf_op jit(solution)/shard_map/ppermute | solution.py:533
  70.6 10.5 %collective-permute-start.20 = (bf16[128,1024]{1,0:T(8,128)(2,1)S(1)}, bf16[128,1024]{1,0:T(8,128)(2,1)S(1)}, u32[]{:S(2)}, u32[]{:S(2)}) collective-permute-start(bf16[128,1024]{1,0:T(8,128)(2,1)S(1)} %attend.2.own_ref), channel_id=1, source_target_pairs={{0,2},{2,0},{1,3},{3,1},{4,6},{6,4},{5,7},{7,5},{8,10},{10,8},{9,1... | collective-permute-start | bytes 786440 | tf_op jit(solution)/shard_map/ppermute | solution.py:533
  74.0 8.6 %collective-permute-start.15 = (bf16[64,2048]{1,0:T(8,128)(2,1)S(1)}, bf16[64,2048]{1,0:T(8,128)(2,1)S(1)}, u32[]{:S(2)}, u32[]{:S(2)}) collective-permute-start(bf16[64,2048]{1,0:T(8,128)(2,1)S(1)} %get-tuple-element.79), channel_id=1, source_target_pairs={{0,8},{8,12},{12,4},{4,0},{1,9},{9,13},{13,5},{5,1},{2,10},{10,14}... | collective-permute-start | bytes 786440 | tf_op jit(solution)/shard_map/ppermute | solution.py:542
  79.5 8.8 %collective-permute-start.17 = (bf16[128,1024]{1,0:T(8,128)(2,1)S(1)}, bf16[128,1024]{1,0:T(8,128)(2,1)S(1)}, u32[]{:S(2)}, u32[]{:S(2)}) collective-permute-start(bf16[128,1024]{1,0:T(8,128)(2,1)S(1)} %attend.3.own_ref), channel_id=1, source_target_pairs={{0,1},{1,0},{2,3},{3,2},{4,5},{5,4},{6,7},{7,6},{8,9},{9,8},{10,11... | collective-permute-start | bytes 786440 | tf_op jit(solution)/shard_map/ppermute | solution.py:536
  79.5 8.7 %collective-permute-start.24 = (bf16[128,1024]{1,0:T(8,128)(2,1)S(1)}, bf16[128,1024]{1,0:T(8,128)(2,1)S(1)}, u32[]{:S(2)}, u32[]{:S(2)}) collective-permute-start(bf16[128,1024]{1,0:T(8,128)(2,1)S(1)} %attend.3.own_ref), channel_id=1, source_target_pairs={{0,2},{2,0},{1,3},{3,1},{4,6},{6,4},{5,7},{7,5},{8,10},{10,8},{9,1... | collective-permute-start | bytes 786440 | tf_op jit(solution)/shard_map/ppermute | solution.py:533
  82.6 10.2 %collective-permute-start.16 = (bf16[64,2048]{1,0:T(8,128)(2,1)S(1)}, bf16[64,2048]{1,0:T(8,128)(2,1)S(1)}, u32[]{:S(2)}, u32[]{:S(2)}) collective-permute-start(bf16[64,2048]{1,0:T(8,128)(2,1)S(1)} %add_convert_fusion.3), channel_id=1, source_target_pairs={{0,8},{8,12},{12,4},{4,0},{1,9},{9,13},{13,5},{5,1},{2,10},{10,14}... | collective-permute-start | bytes 786440 | tf_op jit(solution)/shard_map/ppermute | solution.py:542
  87.9 10.6 %collective-permute-start.22 = (bf16[64,2048]{1,0:T(8,128)(2,1)S(1)}, bf16[64,2048]{1,0:T(8,128)(2,1)S(1)}, u32[]{:S(2)}, u32[]{:S(2)}) collective-permute-start(bf16[64,2048]{1,0:T(8,128)(2,1)S(1)} %get-tuple-element.89), channel_id=1, source_target_pairs={{0,8},{8,12},{12,4},{4,0},{1,9},{9,13},{13,5},{5,1},{2,10},{10,14}... | collective-permute-start | bytes 786440 | tf_op jit(solution)/shard_map/ppermute | solution.py:542
  88.3 13.7 %collective-permute-start.25 = (bf16[128,1024]{1,0:T(8,128)(2,1)S(1)}, bf16[128,1024]{1,0:T(8,128)(2,1)S(1)}, u32[]{:S(2)}, u32[]{:S(2)}) collective-permute-start(bf16[128,1024]{1,0:T(8,128)(2,1)S(1)} %collective-permute-done.24.own_ref), channel_id=1, source_target_pairs={{0,1},{1,0},{2,3},{3,2},{4,5},{5,4},{6,7},{7,6},{8,9},{9,8},{10,11... | collective-permute-start | bytes 786440 | tf_op jit(solution)/shard_map/ppermute | solution.py:536
  92.9 12.9 %collective-permute-start.18 = (bf16[64,2048]{1,0:T(8,128)(2,1)S(1)}, bf16[64,2048]{1,0:T(8,128)(2,1)S(1)}, u32[]{:S(2)}, u32[]{:S(2)}) collective-permute-start(bf16[64,2048]{1,0:T(8,128)(2,1)S(1)} %add_convert_fusion.2), channel_id=1, source_target_pairs={{0,8},{8,12},{12,4},{4,0},{1,9},{9,13},{13,5},{5,1},{2,10},{10,14}... | collective-permute-start | bytes 786440 | tf_op jit(solution)/shard_map/ppermute | solution.py:542
  98.5 9.5 %collective-permute-start.23 = (bf16[64,2048]{1,0:T(8,128)(2,1)S(1)}, bf16[64,2048]{1,0:T(8,128)(2,1)S(1)}, u32[]{:S(2)}, u32[]{:S(2)}) collective-permute-start(bf16[64,2048]{1,0:T(8,128)(2,1)S(1)} %add_convert_fusion.1), channel_id=1, source_target_pairs={{0,8},{8,12},{12,4},{4,0},{1,9},{9,13},{13,5},{5,1},{2,10},{10,14}... | collective-permute-start | bytes 786440 | tf_op jit(solution)/shard_map/ppermute | solution.py:542
  104.3 8.5 %collective-permute-start.27 = (bf16[32,2048]{1,0:T(8,128)(2,1)S(1)}, bf16[32,2048]{1,0:T(8,128)(2,1)S(1)}, u32[]{:S(2)}, u32[]{:S(2)}) collective-permute-start(bf16[32,2048]{1,0:T(8,128)(2,1)S(1)} %get-tuple-element.96), channel_id=1, source_target_pairs={{0,2},{2,0},{1,3},{3,1},{4,6},{6,4},{5,7},{7,5},{8,10},{10,8},{9,1... | collective-permute-start | bytes 393224 | tf_op jit(solution)/shard_map/ppermute | solution.py:533
  105.8 10.9 %collective-permute-start.29 = (bf16[32,2048]{1,0:T(8,128)(2,1)S(1)}, bf16[32,2048]{1,0:T(8,128)(2,1)S(1)}, u32[]{:S(2)}, u32[]{:S(2)}) collective-permute-start(bf16[32,2048]{1,0:T(8,128)(2,1)S(1)} %get-tuple-element.98), channel_id=1, source_target_pairs={{0,3},{1,2},{2,1},{3,0},{4,7},{5,6},{6,5},{7,4},{8,11},{9,10},{10,... | collective-permute-start | bytes 393224 | tf_op jit(solution)/shard_map/ppermute | solution.py:539
  106.4 10.3 %collective-permute-start.19 = (bf16[32,2048]{1,0:T(8,128)(2,1)S(1)}, bf16[32,2048]{1,0:T(8,128)(2,1)S(1)}, u32[]{:S(2)}, u32[]{:S(2)}) collective-permute-start(bf16[32,2048]{1,0:T(8,128)(2,1)S(1)} %get-tuple-element.85), channel_id=1, source_target_pairs={{0,1},{1,0},{2,3},{3,2},{4,5},{5,4},{6,7},{7,6},{8,9},{9,8},{10,11... | collective-permute-start | bytes 393224 | tf_op jit(solution)/shard_map/ppermute | solution.py:536
  108.6 8.2 %collective-permute-start.26 = (bf16[32,2048]{1,0:T(8,128)(2,1)S(1)}, bf16[32,2048]{1,0:T(8,128)(2,1)S(1)}, u32[]{:S(2)}, u32[]{:S(2)}) collective-permute-start(bf16[32,2048]{1,0:T(8,128)(2,1)S(1)} %get-tuple-element.93), channel_id=1, source_target_pairs={{0,10},{1,11},{2,8},{3,9},{8,14},{9,15},{10,12},{11,13},{12,6},{13... | collective-permute-start | bytes 393224 | tf_op jit(solution)/shard_map/ppermute | solution.py:547
  (11 other events, 60.9 us)

commit v4 on v3

--- a/solution.py
+++ b/solution.py
@@ -389,13 +389,14 @@
     )(place, own, other, w_out)
 
 
-def attend_kernel(wanted, order, place_ref, ids_ref, seg_ref, keep_ref, *refs):
-    come_refs, (chip_ref, away_ref, out_ref) = refs[:-3], refs[-3:]
+def attend_kernel(wanted, order, parts, place_ref, ids_ref, seg_ref, *refs):
+    keep_refs, come_refs = refs[:parts], refs[parts:-3]
+    chip_ref, away_ref, out_ref = refs[-3:]
     req, kv, tp = place_ref[0], place_ref[1], place_ref[2]
     groups = 2
     steps = ids_ref.shape[1]
-    total_cols = keep_ref.shape[1]
-    rows = keep_ref.shape[0] // groups
+    total_cols = keep_refs[0].shape[1]
+    rows = sum(ref.shape[0] for ref in keep_refs) // groups
     part = out_ref.shape[0] // (groups * len(wanted))
     pieces = rows // part
     some = part * len(wanted)
@@ -435,8 +436,9 @@
     row_pos = position(lax.broadcasted_iota(jnp.int32, (some, rows), 0), wanted)
     across = lax.broadcasted_iota(jnp.int32, (some, rows), 1)
     col_pos = position(across, range(pieces))
+    keep = jnp.concatenate([ref[...] for ref in keep_refs], axis=0)
     come = jnp.concatenate([ref[...] for ref in come_refs], axis=0)
-    whole = (keep_ref[...] + come.astype(jnp.float32)).astype(jnp.bfloat16)
+    whole = (keep + come.astype(jnp.float32)).astype(jnp.bfloat16)
 
     def own_rows(g, j, columns):
         at = (j * groups + g) * part
@@ -506,13 +508,13 @@
     whole = pl.BlockSpec(memory_space=pltpu.VMEM)
     scalars = pl.BlockSpec(memory_space=pltpu.SMEM)
     return pl.pallas_call(
-        functools.partial(attend_kernel, wanted, order),
-        in_specs=[scalars] * 2 + [whole] * (len(come) + 4),
+        functools.partial(attend_kernel, wanted, order, len(keep)),
+        in_specs=[scalars] * 2 + [whole] * (len(keep) + len(come) + 3),
         out_specs=whole,
-        out_shape=jax.ShapeDtypeStruct((rows, keep.shape[1] - 2 * HD), jnp.bfloat16),
+        out_shape=jax.ShapeDtypeStruct((rows, keep[0].shape[1] - 2 * HD), jnp.bfloat16),
         compiler_params=pltpu.CompilerParams(vmem_limit_bytes=10 * MIB),
         name="attend",
-    )(place, ids, segments, keep, *come, chip, away)
+    )(place, ids, segments, *keep, *come, chip, away)
 
 
 ROOT_BLOCKS = 4
@@ -561,29 +563,32 @@
     near = merge(place, kept, swap_kv(give))
     far = merge(place, swap_req(far_same), swap_both(far_cross))
 
+    kinds = (jnp.bfloat16, jnp.float32)
+
+    def summed(sent, kept, kind):
+        return (kept + swap_kv(sent).astype(jnp.float32)).astype(kind)
+
     near_pieces, far_pieces = [near, onward(near)], [far]
     weights = load(46, *after((w_query, w_key, w_value), near))
     far_pieces.append(onward(after(far, weights)))
     mine, give = cached_heads(place, *after((cache_keys, cache_values), weights))
     chip = jnp.stack((mine, swap_kv(give)))
     away = swap_req(chip)
-    for pieces in (near_pieces, far_pieces):
-        for _ in range(count - 2):
-            pieces.append(onward(pieces[-1]))
-
-    kinds = (jnp.bfloat16, jnp.float32)
-
-    def summed(sent, kept, kind):
-        return (kept + swap_kv(sent).astype(jnp.float32)).astype(kind)
+    far_first = project(place, far_pieces, weights, (True, False), kinds)
+    for step in range(1, count - 1):
+        piece = near_pieces[step]
+        near_pieces.append(onward(after(piece, far_first) if step == count - 2 else piece))
+        far_pieces.append(onward(far_pieces[step]))
+    first_terms = summed(*far_first, jnp.bfloat16)
 
     near_terms = project(place, after(near_pieces, away), weights, (True, False), kinds)
-    keep = summed(*near_terms, jnp.float32)
-    far_pieces = after(far_pieces, near_terms)
-    sent = project(place, far_pieces, weights, (True,), kinds[:1])
-    kept = project(place, far_pieces, weights, (False,), kinds[1:])
-    far_terms = summed(*sent, *kept, jnp.bfloat16)
-    come = (swap_req(far_terms),)
-    w_out = load(38, *after((w_out,), far_terms))[0]
+    keep = (summed(*near_terms, jnp.float32),)
+    pieces = after(far_pieces[2:], near_terms)
+    sent = project(place, pieces, weights, (True,), kinds[:1])
+    kept = project(place, pieces, weights, (False,), kinds[1:])
+    last_terms = summed(*sent, *kept, jnp.bfloat16)
+    come = (swap_req(first_terms), swap_req(last_terms))
+    w_out = load(38, *after((w_out,), last_terms))[0]
 
     middle = count // 2
     halves = (tuple(range(1, middle + 1)), tuple(j % count for j in range(middle + 1, count + 1)))
@@ -596,7 +601,7 @@
         )
 
     def projected(sums, wanted, own, other):
-        sums |= zip(wanted, out_project(place, own, other, w_out, middle))
+        sums |= zip(wanted, out_project(place, own, other, w_out, len(wanted)))
 
     def plus(running, term):
         return (running.astype(jnp.float32) + term.astype(jnp.float32)).astype(jnp.bfloat16)
@@ -604,21 +609,22 @@
     rows = attended(halves[0], w_out)
     rows_far = swap_req(rows)
     projected(near_sum, halves[0], rows, swap_kv(rows))
-    near_run = onward(near_sum[1])
+    near_run = near_one = onward(near_sum[1])
     last = attended(halves[1], near_sum[1])
     last_far = swap_req(last)
     rows_far = after(rows_far, last)
-    rows_far = after((rows_far, swap_kv(rows_far)), near_run)
+    rows_far = after((rows_far, swap_kv(rows_far)), last)
     projected(far_sum, halves[0], *rows_far)
     far_run = onward(far_sum[1])
     projected(near_sum, halves[1], last, swap_kv(last))
-    last_far = after(last_far, near_run)
+    last_far = after(last_far, near_one)
     projected(far_sum, halves[1], last_far, swap_kv(last_far))
 
-    beside = share(place, after(far_sum[0], far_run))
-    beside = (swap_req(beside[0]), swap_both(beside[1]))
+    terms = share(place, after(far_sum[0], far_run))
+    beside = (swap_req(terms[0]), swap_both(terms[1]))
     for j in range(2, count):
-        near_run = onward(plus(near_run, near_sum[j]))
+        near_term = plus(near_run, near_sum[j])
+        near_run = onward(after(near_term, terms) if j == count - 1 else near_term)
         if j < count - 1:
             far_run = onward(plus(far_run, far_sum[j]))
     ends = slanted(*share(place, far_run, far_sum[count - 1]))

time: 120 us -> 117 us (0.975)
  starting transfers between devices: 44.3 us -> 41.4 us
  waiting for transfers between devices: 38.8 us -> 37.2 us
    ppermute x2, waiting for transfers between devices: 3.91 us -> 0.01 us  [swap_both(): return lax.ppermute(x, ('req', 'kv'), [(i, 3 - i) for i in range(4)])]
    ppermute x11, waiting for transfers between devices: 21.5 us -> 17.7 us  [onward(): return lax.ppermute(x, 'tp', forward)]
    ppermute x6 -> x7, waiting for transfers between devices: 12 us -> 15.1 us  [swap_req(): return lax.ppermute(x, 'req', SWAP)]
    ppermute x2, waiting for transfers between devices: 1.37 us -> 4.28 us  [slanted(): lax.ppermute(x, axes, [(4 * low + 2 * r + c, 4 * high + 2 * (1 - r) + (c...]
    ppermute x9 -> x10, starting transfers between devices: 2.31 us -> 1.01 us  [swap_kv(): return lax.ppermute(x, 'kv', SWAP)]
    pallas_call x3 -> x4, Pallas kernels: 7.72 us -> 8.58 us  [project(): pl.pallas_call(functools.partial(project_kernel, flips), in_specs=[pl.Blo...]
    ppermute x6 -> x7, starting transfers between devices: 10.3 us -> 9.86 us  [swap_req(): return lax.ppermute(x, 'req', SWAP)]
  transfers between devices with their start and end apart: 30 -> 32, of which waited for: 13 -> 16; matrix products, arithmetic and copies ran while one was open for 0% -> 0% of each run, Pallas kernels for 22% -> 26%
where the time goes in v4:
time: 117 us; the launch traced here: 116 us
  starting transfers between devices  41.4 us (35%)
  waiting for transfers between devices  37.2 us (32%)
  Pallas kernels  34.6 us (30%)
  local copies, waits for them, and re-layouts  1.8 us (2%)
    ppermute x11, starting transfers between devices, onward(): return lax.ppermute(x, 'tp', forward)  27.2 us
    ppermute x11, waiting for transfers between devices, onward(): return lax.ppermute(x, 'tp', forward)  17.7 us
    ppermute x7, waiting for transfers between devices, swap_req(): return lax.ppermute(x, 'req', SWAP)  15.1 us
    ppermute x7, starting transfers between devices, swap_req(): return lax.ppermute(x, 'req', SWAP)  9.86 us
    pallas_call x4, Pallas kernels, project(): pl.pallas_call(functools.partial(project_kernel, flips), in_specs=[pl.Blo...  8.58 us
    pallas_call x2, Pallas kernels, load(): pl.pallas_call(functools.partial(load_kernel, count), in_specs=[pl.BlockS...  7.32 us
    pallas_call x4, Pallas kernels, out_project(): pl.pallas_call(out_kernel, in_specs=[pl.BlockSpec(memory_space=pltpu.SMEM...  7.24 us
    pallas_call x2, Pallas kernels, attend(): pl.pallas_call(functools.partial(attend_kernel, wanted, order, len(keep))...  5.6 us
  transfers between devices with their start and end apart: 32, of which 16 were waited for; matrix products, arithmetic and copies ran while one was open for 0% of the time, Pallas kernels for 26%

profile of v4, /device:TPU:0, one launch (start us, length us, event | category | flops | bytes accessed | tf_op | source)
XLA Modules:
  0.0 115.9 jit_solution(13189609121907436558)
XLA Ops:
  3.2 2.6 %collective-permute-start.3 = (bf16[32,2048]{1,0:T(8,128)(2,1)S(1)}, bf16[32,2048]{1,0:T(8,128)(2,1)S(1)}, u32[]{:S(2)}, u32[]{:S(2)}) collective-permute-start(bf16[32,2048]{1,0:T(8,128)(2,1)S(1)} %get-tuple-element.56), channel_id=1, source_target_pairs={{0,2},{2,0},{1,3},{3,1},{4,6},{6,4},{5,7},{7,5},{8,10},{10,8},{9,1... | collective-permute-start | bytes 393224 | tf_op jit(solution)/shard_map/ppermute | solution.py:535
  6.5 2.9 %collective-permute-start.1 = (bf16[64,2048]{1,0:T(8,128)(2,1)S(1)}, bf16[64,2048]{1,0:T(8,128)(2,1)S(1)}, u32[]{:S(2)}, u32[]{:S(2)}) collective-permute-start(bf16[64,2048]{1,0:T(8,128)(2,1)S(1)} %merge.2.refs_0_), channel_id=1, source_target_pairs={{0,8},{8,12},{12,4},{4,0},{1,9},{9,13},{13,5},{5,1},{2,10},{10,14}... | collective-permute-start | bytes 786440 | tf_op jit(solution)/shard_map/ppermute | solution.py:544
  9.4 3.9 %load.2 = (bf16[2048,2048]{1,0:T(8,128)(2,1)S(1)}, bf16[2048,256]{1,0:T(8,128)(2,1)S(1)}, bf16[2048,256]{1,0:T(8,128)(2,1)S(1)}) custom-call(bf16[2048,2048]{1,0:T(8,128)(2,1)} %refs_0_, bf16[2048,256]{1,0:T(8,128)(2,1)} %refs_1_, bf16[2048,256]{1,0:T(8,128)(2,1)} %refs_2_), custom_call_target="tpu_custom_call" | custom-call | tf_op jit(solution)/shard_map/load/pallas_call | solution.py:209
  16.4 2.4 %collective-permute-start.2 = (bf16[64,2048]{1,0:T(8,128)(2,1)S(1)}, bf16[64,2048]{1,0:T(8,128)(2,1)S(1)}, u32[]{:S(2)}, u32[]{:S(2)}) collective-permute-start(bf16[64,2048]{1,0:T(8,128)(2,1)S(1)} %collective-permute-done.1.refs_1_), channel_id=1, source_target_pairs={{0,8},{8,12},{12,4},{4,0},{1,9},{9,13},{13,5},{5,1},{2,10},{10,14}... | collective-permute-start | bytes 786440 | tf_op jit(solution)/shard_map/ppermute | solution.py:544
  20.4 3.5 %collective-permute-done.5.refs_1_ = bf16[64,2048]{1,0:T(8,128)(2,1)S(1)} collective-permute-done((bf16[64,2048]{1,0:T(8,128)(2,1)S(1)}, bf16[64,2048]{1,0:T(8,128)(2,1)S(1)}, u32[]{:S(2)}, u32[]{:S(2)}) %collective-permute-start.5) | collective-permute-done | bytes 262176 | tf_op jit(solution)/shard_map/ppermute | solution.py:544
  23.9 2.5 %collective-permute-start.10 = (bf16[64,2048]{1,0:T(8,128)(2,1)S(1)}, bf16[64,2048]{1,0:T(8,128)(2,1)S(1)}, u32[]{:S(2)}, u32[]{:S(2)}) collective-permute-start(bf16[64,2048]{1,0:T(8,128)(2,1)S(1)} %collective-permute-done.5.refs_1_), channel_id=1, source_target_pairs={{0,8},{8,12},{12,4},{4,0},{1,9},{9,13},{13,5},{5,1},{2,10},{10,14}... | collective-permute-start | bytes 786440 | tf_op jit(solution)/shard_map/ppermute | solution.py:544
  29.5 2.5 %collective-permute-start.6 = (bf16[64,2048]{1,0:T(8,128)(2,1)S(1)}, bf16[64,2048]{1,0:T(8,128)(2,1)S(1)}, u32[]{:S(2)}, u32[]{:S(2)}) collective-permute-start(bf16[64,2048]{1,0:T(8,128)(2,1)S(1)} %collective-permute-done.2.refs_2_), channel_id=1, source_target_pairs={{0,8},{8,12},{12,4},{4,0},{1,9},{9,13},{13,5},{5,1},{2,10},{10,14}... | collective-permute-start | bytes 786440 | tf_op jit(solution)/shard_map/ppermute | solution.py:544
  32.0 3.1 %collective-permute-done.10.refs_0_ = bf16[64,2048]{1,0:T(8,128)(2,1)S(1)} collective-permute-done((bf16[64,2048]{1,0:T(8,128)(2,1)S(1)}, bf16[64,2048]{1,0:T(8,128)(2,1)S(1)}, u32[]{:S(2)}, u32[]{:S(2)}) %collective-permute-start.10) | collective-permute-done | bytes 262176 | tf_op jit(solution)/shard_map/ppermute | solution.py:544
  35.2 2.5 %collective-permute-start.11 = (bf16[64,2048]{1,0:T(8,128)(2,1)S(1)}, bf16[64,2048]{1,0:T(8,128)(2,1)S(1)}, u32[]{:S(2)}, u32[]{:S(2)}) collective-permute-start(bf16[64,2048]{1,0:T(8,128)(2,1)S(1)} %collective-permute-done.10.refs_0_), channel_id=1, source_target_pairs={{0,8},{8,12},{12,4},{4,0},{1,9},{9,13},{13,5},{5,1},{2,10},{10,14}... | collective-permute-start | bytes 786440 | tf_op jit(solution)/shard_map/ppermute | solution.py:544
  37.6 3.1 %collective-permute-done.6.refs_3_ = bf16[64,2048]{1,0:T(8,128)(2,1)S(1)} collective-permute-done((bf16[64,2048]{1,0:T(8,128)(2,1)S(1)}, bf16[64,2048]{1,0:T(8,128)(2,1)S(1)}, u32[]{:S(2)}, u32[]{:S(2)}) %collective-permute-start.6) | collective-permute-done | bytes 262176 | tf_op jit(solution)/shard_map/ppermute | solution.py:544
  40.8 3.5 %project.5 = (bf16[256,1280]{1,0:T(8,128)(2,1)S(1)}, f32[256,1280]{1,0:T(8,128)S(1)}) custom-call(s32[3]{0:T(128)S(1)} %pad_add_fusion.place_ref, bf16[64,2048]{1,0:T(8,128)(2,1)S(1)} %merge.2.refs_0_, bf16[64,2048]{1,0:T(8,128)(2,1)S(1)} %collective-permute-done.1.refs_1_, bf16[64,2048]{1,0:T(8,128)(2,1)S(1)} %collective-permute-done.2.refs_2_, ...), custom_call_target="tpu_custom_call" | custom-call | tf_op jit(solution)/shard_map/project/pallas_call | solution.py:347
  51.3 3.4 %load.3.w_ref = bf16[2048,2048]{1,0:T(8,128)(2,1)S(1)} custom-call(bf16[2048,2048]{1,0:T(8,128)(2,1)} %refs_0_.1), custom_call_target="tpu_custom_call" | custom-call | tf_op jit(solution)/shard_map/load/pallas_call | solution.py:209
  54.8 3.3 %collective-permute-done.14.refs_1_ = bf16[128,1280]{1,0:T(8,128)(2,1)S(1)} collective-permute-done((bf16[128,1280]{1,0:T(8,128)(2,1)S(1)}, bf16[128,1280]{1,0:T(8,128)(2,1)S(1)}, u32[]{:S(2)}, u32[]{:S(2)}) %collective-permute-start.14) | collective-permute-done | bytes 327712 | tf_op jit(solution)/shard_map/ppermute | solution.py:535
  58.1 6.6 %collective-permute-done.15.refs_2_ = bf16[128,1280]{1,0:T(8,128)(2,1)S(1)} collective-permute-done((bf16[128,1280]{1,0:T(8,128)(2,1)S(1)}, bf16[128,1280]{1,0:T(8,128)(2,1)S(1)}, u32[]{:S(2)}, u32[]{:S(2)}) %collective-permute-start.15) | collective-permute-done | bytes 327712 | tf_op jit(solution)/shard_map/ppermute | solution.py:535
  64.8 2.8 %attend.2.own_ref = bf16[128,1024]{1,0:T(8,128)(2,1)S(1)} custom-call(s32[3]{0:T(128)S(1)} %pad_add_fusion.place_ref, s32[4,2,8]{2,1,0:T(2,128)S(1)} %copy-done.3, s32[4,128]{1,0:T(4,128)S(1)} %copy-done.4, f32[256,1280]{1,0:T(8,128)S(1)} %convert_add_fusion.refs_0_, bf16[128,1280]{1,0:T(8,128)(2,1)S(1)} %collective-permute-done.14.refs_1_, ...), custom_call_target="tpu_custom_call" | custom-call | tf_op jit(solution)/shard_map/attend/pallas_call | solution.py:510
  71.0 2.8 %attend.3.own_ref = bf16[128,1024]{1,0:T(8,128)(2,1)S(1)} custom-call(s32[3]{0:T(128)S(1)} %pad_add_fusion.place_ref, s32[4,2,8]{2,1,0:T(2,128)S(1)} %copy-done.3, s32[4,128]{1,0:T(4,128)S(1)} %copy-done.4, f32[256,1280]{1,0:T(8,128)S(1)} %convert_add_fusion.refs_0_, bf16[128,1280]{1,0:T(8,128)(2,1)S(1)} %collective-permute-done.14.refs_1_, ...), custom_call_target="tpu_custom_call" | custom-call | tf_op jit(solution)/shard_map/attend/pallas_call | solution.py:510
  73.8 2.5 %collective-permute-done.22.own_ref = bf16[128,1024]{1,0:T(8,128)(2,1)S(1)} collective-permute-done((bf16[128,1024]{1,0:T(8,128)(2,1)S(1)}, bf16[128,1024]{1,0:T(8,128)(2,1)S(1)}, u32[]{:S(2)}, u32[]{:S(2)}) %collective-permute-start.22) | collective-permute-done | bytes 262176 | tf_op jit(solution)/shard_map/ppermute | solution.py:535
  77.9 2.5 %collective-permute-start.17 = (bf16[64,2048]{1,0:T(8,128)(2,1)S(1)}, bf16[64,2048]{1,0:T(8,128)(2,1)S(1)}, u32[]{:S(2)}, u32[]{:S(2)}) collective-permute-start(bf16[64,2048]{1,0:T(8,128)(2,1)S(1)} %get-tuple-element.82), channel_id=1, source_target_pairs={{0,8},{8,12},{12,4},{4,0},{1,9},{9,13},{13,5},{5,1},{2,10},{10,14}... | collective-permute-start | bytes 786440 | tf_op jit(solution)/shard_map/ppermute | solution.py:544
  82.4 2.6 %collective-permute-done.20.own_ref = bf16[128,1024]{1,0:T(8,128)(2,1)S(1)} collective-permute-done((bf16[128,1024]{1,0:T(8,128)(2,1)S(1)}, bf16[128,1024]{1,0:T(8,128)(2,1)S(1)}, u32[]{:S(2)}, u32[]{:S(2)}) %collective-permute-start.20) | collective-permute-done | bytes 262176 | tf_op jit(solution)/shard_map/ppermute | solution.py:535
  87.1 3.6 %collective-permute-start.18 = (bf16[64,2048]{1,0:T(8,128)(2,1)S(1)}, bf16[64,2048]{1,0:T(8,128)(2,1)S(1)}, u32[]{:S(2)}, u32[]{:S(2)}) collective-permute-start(bf16[64,2048]{1,0:T(8,128)(2,1)S(1)} %add_convert_fusion.4), channel_id=1, source_target_pairs={{0,8},{8,12},{12,4},{4,0},{1,9},{9,13},{13,5},{5,1},{2,10},{10,14}... | collective-permute-start | bytes 786440 | tf_op jit(solution)/shard_map/ppermute | solution.py:544
  92.7 3.2 %collective-permute-start.27 = (bf16[64,2048]{1,0:T(8,128)(2,1)S(1)}, bf16[64,2048]{1,0:T(8,128)(2,1)S(1)}, u32[]{:S(2)}, u32[]{:S(2)}) collective-permute-start(bf16[64,2048]{1,0:T(8,128)(2,1)S(1)} %add_convert_fusion.2), channel_id=1, source_target_pairs={{0,8},{8,12},{12,4},{4,0},{1,9},{9,13},{13,5},{5,1},{2,10},{10,14}... | collective-permute-start | bytes 786440 | tf_op jit(solution)/shard_map/ppermute | solution.py:544
  98.9 3.2 %collective-permute-start.25 = (bf16[64,2048]{1,0:T(8,128)(2,1)S(1)}, bf16[64,2048]{1,0:T(8,128)(2,1)S(1)}, u32[]{:S(2)}, u32[]{:S(2)}) collective-permute-start(bf16[64,2048]{1,0:T(8,128)(2,1)S(1)} %add_convert_fusion.3), channel_id=1, source_target_pairs={{0,8},{8,12},{12,4},{4,0},{1,9},{9,13},{13,5},{5,1},{2,10},{10,14}... | collective-permute-start | bytes 786440 | tf_op jit(solution)/shard_map/ppermute | solution.py:544
  104.5 3.2 %collective-permute-start.28 = (bf16[32,2048]{1,0:T(8,128)(2,1)S(1)}, bf16[32,2048]{1,0:T(8,128)(2,1)S(1)}, u32[]{:S(2)}, u32[]{:S(2)}) collective-permute-start(bf16[32,2048]{1,0:T(8,128)(2,1)S(1)} %get-tuple-element.101), channel_id=1, source_target_pairs={{0,10},{1,11},{2,8},{3,9},{8,14},{9,15},{10,12},{11,13},{12,6},{13... | collective-permute-start | bytes 393224 | tf_op jit(solution)/shard_map/ppermute | solution.py:549
  112.1 2.4 %collective-permute-done.30.refs_4_ = bf16[32,2048]{1,0:T(8,128)(2,1)S(1)} collective-permute-done((bf16[32,2048]{1,0:T(8,128)(2,1)S(1)}, bf16[32,2048]{1,0:T(8,128)(2,1)S(1)}, u32[]{:S(2)}, u32[]{:S(2)}) %collective-permute-start.30) | collective-permute-done | bytes 131104 | tf_op jit(solution)/shard_map/ppermute | solution.py:549
  (79 shorter events, 40.8 us)
Async XLA Ops:
  3.2 10.9 %collective-permute-start.3 = (bf16[32,2048]{1,0:T(8,128)(2,1)S(1)}, bf16[32,2048]{1,0:T(8,128)(2,1)S(1)}, u32[]{:S(2)}, u32[]{:S(2)}) collective-permute-start(bf16[32,2048]{1,0:T(8,128)(2,1)S(1)} %get-tuple-element.56), channel_id=1, source_target_pairs={{0,2},{2,0},{1,3},{3,1},{4,6},{6,4},{5,7},{7,5},{8,10},{10,8},{9,1... | collective-permute-start | bytes 393224 | tf_op jit(solution)/shard_map/ppermute | solution.py:535
  5.8 8.4 %collective-permute-start.4 = (bf16[32,2048]{1,0:T(8,128)(2,1)S(1)}, bf16[32,2048]{1,0:T(8,128)(2,1)S(1)}, u32[]{:S(2)}, u32[]{:S(2)}) collective-permute-start(bf16[32,2048]{1,0:T(8,128)(2,1)S(1)} %get-tuple-element.57), channel_id=1, source_target_pairs={{0,3},{1,2},{2,1},{3,0},{4,7},{5,6},{6,5},{7,4},{8,11},{9,10},{10,... | collective-permute-start | bytes 393224 | tf_op jit(solution)/shard_map/ppermute | solution.py:541
  6.5 9.9 %collective-permute-start.1 = (bf16[64,2048]{1,0:T(8,128)(2,1)S(1)}, bf16[64,2048]{1,0:T(8,128)(2,1)S(1)}, u32[]{:S(2)}, u32[]{:S(2)}) collective-permute-start(bf16[64,2048]{1,0:T(8,128)(2,1)S(1)} %merge.2.refs_0_), channel_id=1, source_target_pairs={{0,8},{8,12},{12,4},{4,0},{1,9},{9,13},{13,5},{5,1},{2,10},{10,14}... | collective-permute-start | bytes 786440 | tf_op jit(solution)/shard_map/ppermute | solution.py:544
  14.8 9.2 %collective-permute-start.5 = (bf16[64,2048]{1,0:T(8,128)(2,1)S(1)}, bf16[64,2048]{1,0:T(8,128)(2,1)S(1)}, u32[]{:S(2)}, u32[]{:S(2)}) collective-permute-start(bf16[64,2048]{1,0:T(8,128)(2,1)S(1)} %merge.3.refs_0_), channel_id=1, source_target_pairs={{0,8},{8,12},{12,4},{4,0},{1,9},{9,13},{13,5},{5,1},{2,10},{10,14}... | collective-permute-start | bytes 786440 | tf_op jit(solution)/shard_map/ppermute | solution.py:544
  16.4 13.1 %collective-permute-start.2 = (bf16[64,2048]{1,0:T(8,128)(2,1)S(1)}, bf16[64,2048]{1,0:T(8,128)(2,1)S(1)}, u32[]{:S(2)}, u32[]{:S(2)}) collective-permute-start(bf16[64,2048]{1,0:T(8,128)(2,1)S(1)} %collective-permute-done.1.refs_1_), channel_id=1, source_target_pairs={{0,8},{8,12},{12,4},{4,0},{1,9},{9,13},{13,5},{5,1},{2,10},{10,14}... | collective-permute-start | bytes 786440 | tf_op jit(solution)/shard_map/ppermute | solution.py:544
  18.9 18.8 %collective-permute-start.8 = (bf16[2,2,8,64,128]{4,3,2,1,0:T(8,128)(2,1)S(1)}, bf16[2,2,8,64,128]{4,3,2,1,0:T(8,128)(2,1)S(1)}, u32[]{:S(2)}, u32[]{:S(2)}) collective-permute-start(bf16[2,2,8,64,128]{4,3,2,1,0:T(8,128)(2,1)S(1)} %pad_maximum_fusion.refs_3_), channel_id=1, source_target_pairs={{0,2},{2,0},{1,3},{3,1},{4,6},{6,4},{5,7},{7,5},{8,10},{10,8},{9,1... | collective-permute-start | bytes 1572872 | tf_op jit(solution)/shard_map/ppermute | solution.py:535
  23.9 11.2 %collective-permute-start.10 = (bf16[64,2048]{1,0:T(8,128)(2,1)S(1)}, bf16[64,2048]{1,0:T(8,128)(2,1)S(1)}, u32[]{:S(2)}, u32[]{:S(2)}) collective-permute-start(bf16[64,2048]{1,0:T(8,128)(2,1)S(1)} %collective-permute-done.5.refs_1_), channel_id=1, source_target_pairs={{0,8},{8,12},{12,4},{4,0},{1,9},{9,13},{13,5},{5,1},{2,10},{10,14}... | collective-permute-start | bytes 786440 | tf_op jit(solution)/shard_map/ppermute | solution.py:544
  28.6 18.9 %collective-permute-start.13 = (bf16[128,1280]{1,0:T(8,128)(2,1)S(1)}, bf16[128,1280]{1,0:T(8,128)(2,1)S(1)}, u32[]{:S(2)}, u32[]{:S(2)}) collective-permute-start(bf16[128,1280]{1,0:T(8,128)(2,1)S(1)} %get-tuple-element.65), channel_id=1, source_target_pairs={{0,1},{1,0},{2,3},{3,2},{4,5},{5,4},{6,7},{7,6},{8,9},{9,8},{10,11... | collective-permute-start | bytes 983048 | tf_op jit(solution)/shard_map/ppermute | solution.py:538
  29.5 11.2 %collective-permute-start.6 = (bf16[64,2048]{1,0:T(8,128)(2,1)S(1)}, bf16[64,2048]{1,0:T(8,128)(2,1)S(1)}, u32[]{:S(2)}, u32[]{:S(2)}) collective-permute-start(bf16[64,2048]{1,0:T(8,128)(2,1)S(1)} %collective-permute-done.2.refs_2_), channel_id=1, source_target_pairs={{0,8},{8,12},{12,4},{4,0},{1,9},{9,13},{13,5},{5,1},{2,10},{10,14}... | collective-permute-start | bytes 786440 | tf_op jit(solution)/shard_map/ppermute | solution.py:544
  35.2 10.8 %collective-permute-start.11 = (bf16[64,2048]{1,0:T(8,128)(2,1)S(1)}, bf16[64,2048]{1,0:T(8,128)(2,1)S(1)}, u32[]{:S(2)}, u32[]{:S(2)}) collective-permute-start(bf16[64,2048]{1,0:T(8,128)(2,1)S(1)} %collective-permute-done.10.refs_0_), channel_id=1, source_target_pairs={{0,8},{8,12},{12,4},{4,0},{1,9},{9,13},{13,5},{5,1},{2,10},{10,14}... | collective-permute-start | bytes 786440 | tf_op jit(solution)/shard_map/ppermute | solution.py:544
  44.3 10.4 %collective-permute-start.9 = (bf16[256,1280]{1,0:T(8,128)(2,1)S(1)}, bf16[256,1280]{1,0:T(8,128)(2,1)S(1)}, u32[]{:S(2)}, u32[]{:S(2)}) collective-permute-start(bf16[256,1280]{1,0:T(8,128)(2,1)S(1)} %get-tuple-element.77), channel_id=1, source_target_pairs={{0,1},{1,0},{2,3},{3,2},{4,5},{5,4},{6,7},{7,6},{8,9},{9,8},{10,11... | collective-permute-start | bytes 1966088 | tf_op jit(solution)/shard_map/ppermute | solution.py:538
  47.6 10.6 %collective-permute-start.14 = (bf16[128,1280]{1,0:T(8,128)(2,1)S(1)}, bf16[128,1280]{1,0:T(8,128)(2,1)S(1)}, u32[]{:S(2)}, u32[]{:S(2)}) collective-permute-start(bf16[128,1280]{1,0:T(8,128)(2,1)S(1)} %add_convert_fusion), channel_id=1, source_target_pairs={{0,2},{2,0},{1,3},{3,1},{4,6},{6,4},{5,7},{7,5},{8,10},{10,8},{9,1... | collective-permute-start | bytes 983048 | tf_op jit(solution)/shard_map/ppermute | solution.py:535
  50.7 14.1 %collective-permute-start.15 = (bf16[128,1280]{1,0:T(8,128)(2,1)S(1)}, bf16[128,1280]{1,0:T(8,128)(2,1)S(1)}, u32[]{:S(2)}, u32[]{:S(2)}) collective-permute-start(bf16[128,1280]{1,0:T(8,128)(2,1)S(1)} %add_convert_fusion.1), channel_id=1, source_target_pairs={{0,2},{2,0},{1,3},{3,1},{4,6},{6,4},{5,7},{7,5},{8,10},{10,8},{9,1... | collective-permute-start | bytes 983048 | tf_op jit(solution)/shard_map/ppermute | solution.py:535
  67.6 8.7 %collective-permute-start.22 = (bf16[128,1024]{1,0:T(8,128)(2,1)S(1)}, bf16[128,1024]{1,0:T(8,128)(2,1)S(1)}, u32[]{:S(2)}, u32[]{:S(2)}) collective-permute-start(bf16[128,1024]{1,0:T(8,128)(2,1)S(1)} %attend.2.own_ref), channel_id=1, source_target_pairs={{0,2},{2,0},{1,3},{3,1},{4,6},{6,4},{5,7},{7,5},{8,10},{10,8},{9,1... | collective-permute-start | bytes 786440 | tf_op jit(solution)/shard_map/ppermute | solution.py:535
  76.4 8.7 %collective-permute-start.20 = (bf16[128,1024]{1,0:T(8,128)(2,1)S(1)}, bf16[128,1024]{1,0:T(8,128)(2,1)S(1)}, u32[]{:S(2)}, u32[]{:S(2)}) collective-permute-start(bf16[128,1024]{1,0:T(8,128)(2,1)S(1)} %attend.3.own_ref), channel_id=1, source_target_pairs={{0,2},{2,0},{1,3},{3,1},{4,6},{6,4},{5,7},{7,5},{8,10},{10,8},{9,1... | collective-permute-start | bytes 786440 | tf_op jit(solution)/shard_map/ppermute | solution.py:535
  77.9 9.1 %collective-permute-start.17 = (bf16[64,2048]{1,0:T(8,128)(2,1)S(1)}, bf16[64,2048]{1,0:T(8,128)(2,1)S(1)}, u32[]{:S(2)}, u32[]{:S(2)}) collective-permute-start(bf16[64,2048]{1,0:T(8,128)(2,1)S(1)} %get-tuple-element.82), channel_id=1, source_target_pairs={{0,8},{8,12},{12,4},{4,0},{1,9},{9,13},{13,5},{5,1},{2,10},{10,14}... | collective-permute-start | bytes 786440 | tf_op jit(solution)/shard_map/ppermute | solution.py:544
  80.3 10.4 %collective-permute-start.19 = (bf16[128,1024]{1,0:T(8,128)(2,1)S(1)}, bf16[128,1024]{1,0:T(8,128)(2,1)S(1)}, u32[]{:S(2)}, u32[]{:S(2)}) collective-permute-start(bf16[128,1024]{1,0:T(8,128)(2,1)S(1)} %attend.3.own_ref), channel_id=1, source_target_pairs={{0,1},{1,0},{2,3},{3,2},{4,5},{5,4},{6,7},{7,6},{8,9},{9,8},{10,11... | collective-permute-start | bytes 786440 | tf_op jit(solution)/shard_map/ppermute | solution.py:538
  82.2 10.5 %collective-permute-start.24 = (bf16[64,2048]{1,0:T(8,128)(2,1)S(1)}, bf16[64,2048]{1,0:T(8,128)(2,1)S(1)}, u32[]{:S(2)}, u32[]{:S(2)}) collective-permute-start(bf16[64,2048]{1,0:T(8,128)(2,1)S(1)} %get-tuple-element.91), channel_id=1, source_target_pairs={{0,8},{8,12},{12,4},{4,0},{1,9},{9,13},{13,5},{5,1},{2,10},{10,14}... | collective-permute-start | bytes 786440 | tf_op jit(solution)/shard_map/ppermute | solution.py:544
  87.0 8.9 %collective-permute-start.21 = (bf16[128,1024]{1,0:T(8,128)(2,1)S(1)}, bf16[128,1024]{1,0:T(8,128)(2,1)S(1)}, u32[]{:S(2)}, u32[]{:S(2)}) collective-permute-start(bf16[128,1024]{1,0:T(8,128)(2,1)S(1)} %collective-permute-done.20.own_ref), channel_id=1, source_target_pairs={{0,1},{1,0},{2,3},{3,2},{4,5},{5,4},{6,7},{7,6},{8,9},{9,8},{10,11... | collective-permute-start | bytes 786440 | tf_op jit(solution)/shard_map/ppermute | solution.py:538
  87.1 11.2 %collective-permute-start.18 = (bf16[64,2048]{1,0:T(8,128)(2,1)S(1)}, bf16[64,2048]{1,0:T(8,128)(2,1)S(1)}, u32[]{:S(2)}, u32[]{:S(2)}) collective-permute-start(bf16[64,2048]{1,0:T(8,128)(2,1)S(1)} %add_convert_fusion.4), channel_id=1, source_target_pairs={{0,8},{8,12},{12,4},{4,0},{1,9},{9,13},{13,5},{5,1},{2,10},{10,14}... | collective-permute-start | bytes 786440 | tf_op jit(solution)/shard_map/ppermute | solution.py:544
  92.7 11.2 %collective-permute-start.27 = (bf16[64,2048]{1,0:T(8,128)(2,1)S(1)}, bf16[64,2048]{1,0:T(8,128)(2,1)S(1)}, u32[]{:S(2)}, u32[]{:S(2)}) collective-permute-start(bf16[64,2048]{1,0:T(8,128)(2,1)S(1)} %add_convert_fusion.2), channel_id=1, source_target_pairs={{0,8},{8,12},{12,4},{4,0},{1,9},{9,13},{13,5},{5,1},{2,10},{10,14}... | collective-permute-start | bytes 786440 | tf_op jit(solution)/shard_map/ppermute | solution.py:544
  98.9 10.6 %collective-permute-start.25 = (bf16[64,2048]{1,0:T(8,128)(2,1)S(1)}, bf16[64,2048]{1,0:T(8,128)(2,1)S(1)}, u32[]{:S(2)}, u32[]{:S(2)}) collective-permute-start(bf16[64,2048]{1,0:T(8,128)(2,1)S(1)} %add_convert_fusion.3), channel_id=1, source_target_pairs={{0,8},{8,12},{12,4},{4,0},{1,9},{9,13},{13,5},{5,1},{2,10},{10,14}... | collective-permute-start | bytes 786440 | tf_op jit(solution)/shard_map/ppermute | solution.py:544
  102.1 8.1 %collective-permute-start.29 = (bf16[32,2048]{1,0:T(8,128)(2,1)S(1)}, bf16[32,2048]{1,0:T(8,128)(2,1)S(1)}, u32[]{:S(2)}, u32[]{:S(2)}) collective-permute-start(bf16[32,2048]{1,0:T(8,128)(2,1)S(1)} %get-tuple-element.93), channel_id=1, source_target_pairs={{0,2},{2,0},{1,3},{3,1},{4,6},{6,4},{5,7},{7,5},{8,10},{10,8},{9,1... | collective-permute-start | bytes 393224 | tf_op jit(solution)/shard_map/ppermute | solution.py:535
  104.5 7.6 %collective-permute-start.28 = (bf16[32,2048]{1,0:T(8,128)(2,1)S(1)}, bf16[32,2048]{1,0:T(8,128)(2,1)S(1)}, u32[]{:S(2)}, u32[]{:S(2)}) collective-permute-start(bf16[32,2048]{1,0:T(8,128)(2,1)S(1)} %get-tuple-element.101), channel_id=1, source_target_pairs={{0,10},{1,11},{2,8},{3,9},{8,14},{9,15},{10,12},{11,13},{12,6},{13... | collective-permute-start | bytes 393224 | tf_op jit(solution)/shard_map/ppermute | solution.py:549
  (13 other events, 70.3 us)

commit v5 on v4

--- a/solution.py
+++ b/solution.py
@@ -248,49 +248,6 @@
         compiler_params=pltpu.CompilerParams(vmem_limit_bytes=4 * MIB),
         name="cached_heads",
     )(place, keys, values)
-
-
-def merge_kernel(place_ref, mine_ref, theirs_ref, out_ref):
-    rows = mine_ref.shape[0]
-    kv = place_ref[1]
-    out_ref[pl.ds(pl.multiple_of(kv * rows, rows), rows), :] = mine_ref[...]
-    out_ref[pl.ds(pl.multiple_of((1 - kv) * rows, rows), rows), :] = theirs_ref[...]
-
-
-def merge(place, mine, theirs):
-    rows, columns = mine.shape
-    whole = pl.BlockSpec(memory_space=pltpu.VMEM)
-    return pl.pallas_call(
-        merge_kernel,
-        in_specs=[pl.BlockSpec(memory_space=pltpu.SMEM)] + [whole] * 2,
-        out_specs=whole,
-        out_shape=jax.ShapeDtypeStruct((2 * rows, columns), mine.dtype),
-        compiler_params=pltpu.CompilerParams(vmem_limit_bytes=4 * MIB),
-        name="merge",
-    )(place, mine, theirs)
-
-
-def share_kernel(place_ref, *refs):
-    terms, (mine_ref, give_ref) = refs[:-2], refs[-2:]
-    rows = mine_ref.shape[0]
-    kv = place_ref[1]
-    for core, ref in ((kv, mine_ref), (1 - kv, give_ref)):
-        at = pl.ds(pl.multiple_of(core * rows, rows), rows)
-        total = sum(term[at, :].astype(jnp.float32) for term in terms)
-        ref[...] = total.astype(ref.dtype)
-
-
-def share(place, *terms):
-    rows, columns = terms[0].shape
-    whole = pl.BlockSpec(memory_space=pltpu.VMEM)
-    return pl.pallas_call(
-        share_kernel,
-        in_specs=[pl.BlockSpec(memory_space=pltpu.SMEM)] + [whole] * len(terms),
-        out_specs=[whole] * 2,
-        out_shape=[jax.ShapeDtypeStruct((rows // 2, columns), terms[0].dtype)] * 2,
-        compiler_params=pltpu.CompilerParams(vmem_limit_bytes=4 * MIB),
-        name="share",
-    )(place, *terms)
 
 
 def collect_kernel(place_ref, *refs):
@@ -559,9 +516,20 @@
             for flip, x in enumerate((same, cross))
         ]
 
+    first = kv == 0
+
+    def merged(mine, theirs):
+        return jnp.where(
+            first, jnp.concatenate((mine, theirs)), jnp.concatenate((theirs, mine))
+        )
+
+    def shared(rows):
+        low, high = rows[:part], rows[part:]
+        return jnp.where(first, low, high), jnp.where(first, high, low)
+
     kept, give, far_same, far_cross = norm(place, tokens, norm_gain)
-    near = merge(place, kept, swap_kv(give))
-    far = merge(place, swap_req(far_same), swap_both(far_cross))
+    near = merged(kept, swap_kv(give))
+    far = merged(swap_req(far_same), swap_both(far_cross))
 
     kinds = (jnp.bfloat16, jnp.float32)
 
@@ -620,15 +588,15 @@
     last_far = after(last_far, near_one)
     projected(far_sum, halves[1], last_far, swap_kv(last_far))
 
-    terms = share(place, after(far_sum[0], far_run))
+    terms = shared(after(far_sum[0], far_run))
     beside = (swap_req(terms[0]), swap_both(terms[1]))
     for j in range(2, count):
         near_term = plus(near_run, near_sum[j])
         near_run = onward(after(near_term, terms) if j == count - 1 else near_term)
         if j < count - 1:
             far_run = onward(plus(far_run, far_sum[j]))
-    ends = slanted(*share(place, far_run, far_sum[count - 1]))
-    mine, give = share(place, near_run, near_sum[0])
+    ends = slanted(*shared(plus(far_run, far_sum[count - 1])))
+    mine, give = shared(plus(near_run, near_sum[0]))
     return collect(place, mine, swap_kv(give), *zip(ends, beside))
 
 

time: 117 us -> 115 us (0.983)
  Pallas kernels: 34.6 us -> 31.7 us
    pallas_call x5 -> x0, Pallas kernels: 2.91 us -> none  [the longest x3 1.78 us: share(): pl.pallas_call(share_kernel, in_specs=[pl.BlockSpec(memory_space=pltpu.SM...]
  transfers between devices with their start and end apart: 32 -> 32, of which waited for: 16 -> 15; matrix products, arithmetic and copies ran while one was open for 0% -> 1% of each run, Pallas kernels for 26% -> 23%
where the time goes in v5:
time: 115 us
  starting transfers between devices  42.2 us (37%)
  waiting for transfers between devices  37.7 us (33%)
  Pallas kernels  31.7 us (28%)
  local copies, waits for them, and re-layouts  1.8 us (2%)
    ppermute x11, starting transfers between devices, onward(): return lax.ppermute(x, 'tp', forward)  27.9 us
    ppermute x11, waiting for transfers between devices, onward(): return lax.ppermute(x, 'tp', forward)  18.3 us
    ppermute x7, waiting for transfers between devices, swap_req(): return lax.ppermute(x, 'req', SWAP)  14.7 us
    ppermute x7, starting transfers between devices, swap_req(): return lax.ppermute(x, 'req', SWAP)  9.92 us
    pallas_call x4, Pallas kernels, project(): pl.pallas_call(functools.partial(project_kernel, flips), in_specs=[pl.Blo...  8.58 us
    pallas_call x2, Pallas kernels, load(): pl.pallas_call(functools.partial(load_kernel, count), in_specs=[pl.BlockS...  7.32 us
    pallas_call x4, Pallas kernels, out_project(): pl.pallas_call(out_kernel, in_specs=[pl.BlockSpec(memory_space=pltpu.SMEM...  7.25 us
    pallas_call x2, Pallas kernels, attend(): pl.pallas_call(functools.partial(attend_kernel, wanted, order, len(keep))...  5.6 us
  transfers between devices with their start and end apart: 32, of which 15 were waited for; matrix products, arithmetic and copies ran while one was open for 1% of the time, Pallas kernels for 23%

profile of v5, /device:TPU:0, one launch (start us, length us, event | category | flops | bytes accessed | tf_op | source)
XLA Modules:
  0.0 114.8 jit_solution(136499017048381222)
XLA Ops:
  3.2 2.6 %collective-permute-start.3 = (bf16[32,2048]{1,0:T(8,128)(2,1)S(1)}, bf16[32,2048]{1,0:T(8,128)(2,1)S(1)}, u32[]{:S(2)}, u32[]{:S(2)}) collective-permute-start(bf16[32,2048]{1,0:T(8,128)(2,1)S(1)} %get-tuple-element.50), channel_id=1, source_target_pairs={{0,2},{2,0},{1,3},{3,1},{4,6},{6,4},{5,7},{7,5},{8,10},{10,8},{9,1... | collective-permute-start | bytes 393224 | tf_op jit(solution)/shard_map/ppermute | solution.py:492
  6.0 2.9 %collective-permute-start.1 = (bf16[64,2048]{1,0:T(8,128)(2,1)S(1)}, bf16[64,2048]{1,0:T(8,128)(2,1)S(1)}, u32[]{:S(2)}, u32[]{:S(2)}) collective-permute-start(bf16[64,2048]{1,0:T(8,128)(2,1)S(1)} %maximum_select_fusion.refs_0_), channel_id=1, source_target_pairs={{0,8},{8,12},{12,4},{4,0},{1,9},{9,13},{13,5},{5,1},{2,10},{10,14}... | collective-permute-start | bytes 786440 | tf_op jit(solution)/shard_map/ppermute | solution.py:501
  8.8 3.9 %load.2 = (bf16[2048,2048]{1,0:T(8,128)(2,1)S(1)}, bf16[2048,256]{1,0:T(8,128)(2,1)S(1)}, bf16[2048,256]{1,0:T(8,128)(2,1)S(1)}) custom-call(bf16[2048,2048]{1,0:T(8,128)(2,1)} %refs_0_, bf16[2048,256]{1,0:T(8,128)(2,1)} %refs_1_, bf16[2048,256]{1,0:T(8,128)(2,1)} %refs_2_), custom_call_target="tpu_custom_call" | custom-call | tf_op jit(solution)/shard_map/load/pallas_call | solution.py:209
  15.4 2.9 %collective-permute-start.2 = (bf16[64,2048]{1,0:T(8,128)(2,1)S(1)}, bf16[64,2048]{1,0:T(8,128)(2,1)S(1)}, u32[]{:S(2)}, u32[]{:S(2)}) collective-permute-start(bf16[64,2048]{1,0:T(8,128)(2,1)S(1)} %collective-permute-done.1.refs_1_), channel_id=1, source_target_pairs={{0,8},{8,12},{12,4},{4,0},{1,9},{9,13},{13,5},{5,1},{2,10},{10,14}... | collective-permute-start | bytes 786440 | tf_op jit(solution)/shard_map/ppermute | solution.py:501
  19.9 3.0 %collective-permute-done.5.refs_1_ = bf16[64,2048]{1,0:T(8,128)(2,1)S(1)} collective-permute-done((bf16[64,2048]{1,0:T(8,128)(2,1)S(1)}, bf16[64,2048]{1,0:T(8,128)(2,1)S(1)}, u32[]{:S(2)}, u32[]{:S(2)}) %collective-permute-start.5) | collective-permute-done | bytes 262176 | tf_op jit(solution)/shard_map/ppermute | solution.py:501
  22.9 2.5 %collective-permute-start.10 = (bf16[64,2048]{1,0:T(8,128)(2,1)S(1)}, bf16[64,2048]{1,0:T(8,128)(2,1)S(1)}, u32[]{:S(2)}, u32[]{:S(2)}) collective-permute-start(bf16[64,2048]{1,0:T(8,128)(2,1)S(1)} %collective-permute-done.5.refs_1_), channel_id=1, source_target_pairs={{0,8},{8,12},{12,4},{4,0},{1,9},{9,13},{13,5},{5,1},{2,10},{10,14}... | collective-permute-start | bytes 786440 | tf_op jit(solution)/shard_map/ppermute | solution.py:501
  28.5 2.5 %collective-permute-start.6 = (bf16[64,2048]{1,0:T(8,128)(2,1)S(1)}, bf16[64,2048]{1,0:T(8,128)(2,1)S(1)}, u32[]{:S(2)}, u32[]{:S(2)}) collective-permute-start(bf16[64,2048]{1,0:T(8,128)(2,1)S(1)} %collective-permute-done.2.refs_2_), channel_id=1, source_target_pairs={{0,8},{8,12},{12,4},{4,0},{1,9},{9,13},{13,5},{5,1},{2,10},{10,14}... | collective-permute-start | bytes 786440 | tf_op jit(solution)/shard_map/ppermute | solution.py:501
  31.0 3.1 %collective-permute-done.10.refs_0_ = bf16[64,2048]{1,0:T(8,128)(2,1)S(1)} collective-permute-done((bf16[64,2048]{1,0:T(8,128)(2,1)S(1)}, bf16[64,2048]{1,0:T(8,128)(2,1)S(1)}, u32[]{:S(2)}, u32[]{:S(2)}) %collective-permute-start.10) | collective-permute-done | bytes 262176 | tf_op jit(solution)/shard_map/ppermute | solution.py:501
  34.1 2.5 %collective-permute-start.11 = (bf16[64,2048]{1,0:T(8,128)(2,1)S(1)}, bf16[64,2048]{1,0:T(8,128)(2,1)S(1)}, u32[]{:S(2)}, u32[]{:S(2)}) collective-permute-start(bf16[64,2048]{1,0:T(8,128)(2,1)S(1)} %collective-permute-done.10.refs_0_), channel_id=1, source_target_pairs={{0,8},{8,12},{12,4},{4,0},{1,9},{9,13},{13,5},{5,1},{2,10},{10,14}... | collective-permute-start | bytes 786440 | tf_op jit(solution)/shard_map/ppermute | solution.py:501
  36.6 3.1 %collective-permute-done.6.refs_3_ = bf16[64,2048]{1,0:T(8,128)(2,1)S(1)} collective-permute-done((bf16[64,2048]{1,0:T(8,128)(2,1)S(1)}, bf16[64,2048]{1,0:T(8,128)(2,1)S(1)}, u32[]{:S(2)}, u32[]{:S(2)}) %collective-permute-start.6) | collective-permute-done | bytes 262176 | tf_op jit(solution)/shard_map/ppermute | solution.py:501
  39.7 3.5 %project.5 = (bf16[256,1280]{1,0:T(8,128)(2,1)S(1)}, f32[256,1280]{1,0:T(8,128)S(1)}) custom-call(s32[3]{0:T(128)S(1)} %pad_add_fusion.place_ref, bf16[64,2048]{1,0:T(8,128)(2,1)S(1)} %maximum_select_fusion.refs_0_, bf16[64,2048]{1,0:T(8,128)(2,1)S(1)} %collective-permute-done.1.refs_1_, bf16[64,2048]{1,0:T(8,128)(2,1)S(1)} %collective-permute-done.2.refs_2_, ...), custom_call_target="tpu_custom_call" | custom-call | tf_op jit(solution)/shard_map/project/pallas_call | solution.py:304
  50.2 3.4 %load.3.w_ref = bf16[2048,2048]{1,0:T(8,128)(2,1)S(1)} custom-call(bf16[2048,2048]{1,0:T(8,128)(2,1)} %refs_0_.1), custom_call_target="tpu_custom_call" | custom-call | tf_op jit(solution)/shard_map/load/pallas_call | solution.py:209
  53.8 3.3 %collective-permute-done.14.refs_1_ = bf16[128,1280]{1,0:T(8,128)(2,1)S(1)} collective-permute-done((bf16[128,1280]{1,0:T(8,128)(2,1)S(1)}, bf16[128,1280]{1,0:T(8,128)(2,1)S(1)}, u32[]{:S(2)}, u32[]{:S(2)}) %collective-permute-start.14) | collective-permute-done | bytes 327712 | tf_op jit(solution)/shard_map/ppermute | solution.py:492
  57.1 6.6 %collective-permute-done.15.refs_2_ = bf16[128,1280]{1,0:T(8,128)(2,1)S(1)} collective-permute-done((bf16[128,1280]{1,0:T(8,128)(2,1)S(1)}, bf16[128,1280]{1,0:T(8,128)(2,1)S(1)}, u32[]{:S(2)}, u32[]{:S(2)}) %collective-permute-start.15) | collective-permute-done | bytes 327712 | tf_op jit(solution)/shard_map/ppermute | solution.py:492
  63.7 2.8 %attend.2.own_ref = bf16[128,1024]{1,0:T(8,128)(2,1)S(1)} custom-call(s32[3]{0:T(128)S(1)} %pad_add_fusion.place_ref, s32[4,2,8]{2,1,0:T(2,128)S(1)} %copy-done.3, s32[4,128]{1,0:T(4,128)S(1)} %copy-done.4, f32[256,1280]{1,0:T(8,128)S(1)} %convert_add_fusion.refs_0_, bf16[128,1280]{1,0:T(8,128)(2,1)S(1)} %collective-permute-done.14.refs_1_, ...), custom_call_target="tpu_custom_call" | custom-call | tf_op jit(solution)/shard_map/attend/pallas_call | solution.py:467
  70.0 2.8 %attend.3.own_ref = bf16[128,1024]{1,0:T(8,128)(2,1)S(1)} custom-call(s32[3]{0:T(128)S(1)} %pad_add_fusion.place_ref, s32[4,2,8]{2,1,0:T(2,128)S(1)} %copy-done.3, s32[4,128]{1,0:T(4,128)S(1)} %copy-done.4, f32[256,1280]{1,0:T(8,128)S(1)} %convert_add_fusion.refs_0_, bf16[128,1280]{1,0:T(8,128)(2,1)S(1)} %collective-permute-done.14.refs_1_, ...), custom_call_target="tpu_custom_call" | custom-call | tf_op jit(solution)/shard_map/attend/pallas_call | solution.py:467
  72.8 2.5 %collective-permute-done.22.own_ref = bf16[128,1024]{1,0:T(8,128)(2,1)S(1)} collective-permute-done((bf16[128,1024]{1,0:T(8,128)(2,1)S(1)}, bf16[128,1024]{1,0:T(8,128)(2,1)S(1)}, u32[]{:S(2)}, u32[]{:S(2)}) %collective-permute-start.22) | collective-permute-done | bytes 262176 | tf_op jit(solution)/shard_map/ppermute | solution.py:492
  76.8 2.5 %collective-permute-start.17 = (bf16[64,2048]{1,0:T(8,128)(2,1)S(1)}, bf16[64,2048]{1,0:T(8,128)(2,1)S(1)}, u32[]{:S(2)}, u32[]{:S(2)}) collective-permute-start(bf16[64,2048]{1,0:T(8,128)(2,1)S(1)} %get-tuple-element.76), channel_id=1, source_target_pairs={{0,8},{8,12},{12,4},{4,0},{1,9},{9,13},{13,5},{5,1},{2,10},{10,14}... | collective-permute-start | bytes 786440 | tf_op jit(solution)/shard_map/ppermute | solution.py:501
  86.0 3.6 %collective-permute-start.18 = (bf16[64,2048]{1,0:T(8,128)(2,1)S(1)}, bf16[64,2048]{1,0:T(8,128)(2,1)S(1)}, u32[]{:S(2)}, u32[]{:S(2)}) collective-permute-start(bf16[64,2048]{1,0:T(8,128)(2,1)S(1)} %add_convert_fusion.6), channel_id=1, source_target_pairs={{0,8},{8,12},{12,4},{4,0},{1,9},{9,13},{13,5},{5,1},{2,10},{10,14}... | collective-permute-start | bytes 786440 | tf_op jit(solution)/shard_map/ppermute | solution.py:501
  91.6 3.2 %collective-permute-start.27 = (bf16[64,2048]{1,0:T(8,128)(2,1)S(1)}, bf16[64,2048]{1,0:T(8,128)(2,1)S(1)}, u32[]{:S(2)}, u32[]{:S(2)}) collective-permute-start(bf16[64,2048]{1,0:T(8,128)(2,1)S(1)} %add_convert_fusion.3), channel_id=1, source_target_pairs={{0,8},{8,12},{12,4},{4,0},{1,9},{9,13},{13,5},{5,1},{2,10},{10,14}... | collective-permute-start | bytes 786440 | tf_op jit(solution)/shard_map/ppermute | solution.py:501
  97.5 3.0 %collective-permute-start.25 = (bf16[64,2048]{1,0:T(8,128)(2,1)S(1)}, bf16[64,2048]{1,0:T(8,128)(2,1)S(1)}, u32[]{:S(2)}, u32[]{:S(2)}) collective-permute-start(bf16[64,2048]{1,0:T(8,128)(2,1)S(1)} %add_convert_fusion.5), channel_id=1, source_target_pairs={{0,8},{8,12},{12,4},{4,0},{1,9},{9,13},{13,5},{5,1},{2,10},{10,14}... | collective-permute-start | bytes 786440 | tf_op jit(solution)/shard_map/ppermute | solution.py:501
  100.5 2.3 %collective-permute-done.27 = bf16[64,2048]{1,0:T(8,128)(2,1)S(1)} collective-permute-done((bf16[64,2048]{1,0:T(8,128)(2,1)S(1)}, bf16[64,2048]{1,0:T(8,128)(2,1)S(1)}, u32[]{:S(2)}, u32[]{:S(2)}) %collective-permute-start.27) | collective-permute-done | bytes 262176 | tf_op jit(solution)/shard_map/ppermute | solution.py:501
  108.6 2.4 %collective-permute-done.30.refs_4_ = bf16[32,2048]{1,0:T(8,128)(2,1)S(1)} collective-permute-done((bf16[32,2048]{1,0:T(8,128)(2,1)S(1)}, bf16[32,2048]{1,0:T(8,128)(2,1)S(1)}, u32[]{:S(2)}, u32[]{:S(2)}) %collective-permute-start.30) | collective-permute-done | bytes 131104 | tf_op jit(solution)/shard_map/ppermute | solution.py:506
  111.0 2.3 %collective-permute-done.28.refs_2_ = bf16[32,2048]{1,0:T(8,128)(2,1)S(1)} collective-permute-done((bf16[32,2048]{1,0:T(8,128)(2,1)S(1)}, bf16[32,2048]{1,0:T(8,128)(2,1)S(1)}, u32[]{:S(2)}, u32[]{:S(2)}) %collective-permute-start.28) | collective-permute-done | bytes 131104 | tf_op jit(solution)/shard_map/ppermute | solution.py:506
  (81 shorter events, 41.1 us)
Async XLA Ops:
  3.2 10.4 %collective-permute-start.3 = (bf16[32,2048]{1,0:T(8,128)(2,1)S(1)}, bf16[32,2048]{1,0:T(8,128)(2,1)S(1)}, u32[]{:S(2)}, u32[]{:S(2)}) collective-permute-start(bf16[32,2048]{1,0:T(8,128)(2,1)S(1)} %get-tuple-element.50), channel_id=1, source_target_pairs={{0,2},{2,0},{1,3},{3,1},{4,6},{6,4},{5,7},{7,5},{8,10},{10,8},{9,1... | collective-permute-start | bytes 393224 | tf_op jit(solution)/shard_map/ppermute | solution.py:492
  6.0 9.4 %collective-permute-start.1 = (bf16[64,2048]{1,0:T(8,128)(2,1)S(1)}, bf16[64,2048]{1,0:T(8,128)(2,1)S(1)}, u32[]{:S(2)}, u32[]{:S(2)}) collective-permute-start(bf16[64,2048]{1,0:T(8,128)(2,1)S(1)} %maximum_select_fusion.refs_0_), channel_id=1, source_target_pairs={{0,8},{8,12},{12,4},{4,0},{1,9},{9,13},{13,5},{5,1},{2,10},{10,14}... | collective-permute-start | bytes 786440 | tf_op jit(solution)/shard_map/ppermute | solution.py:501
  13.7 9.2 %collective-permute-start.5 = (bf16[64,2048]{1,0:T(8,128)(2,1)S(1)}, bf16[64,2048]{1,0:T(8,128)(2,1)S(1)}, u32[]{:S(2)}, u32[]{:S(2)}) collective-permute-start(bf16[64,2048]{1,0:T(8,128)(2,1)S(1)} %maximum_select_fusion.1.refs_0_), channel_id=1, source_target_pairs={{0,8},{8,12},{12,4},{4,0},{1,9},{9,13},{13,5},{5,1},{2,10},{10,14}... | collective-permute-start | bytes 786440 | tf_op jit(solution)/shard_map/ppermute | solution.py:501
  15.4 13.1 %collective-permute-start.2 = (bf16[64,2048]{1,0:T(8,128)(2,1)S(1)}, bf16[64,2048]{1,0:T(8,128)(2,1)S(1)}, u32[]{:S(2)}, u32[]{:S(2)}) collective-permute-start(bf16[64,2048]{1,0:T(8,128)(2,1)S(1)} %collective-permute-done.1.refs_1_), channel_id=1, source_target_pairs={{0,8},{8,12},{12,4},{4,0},{1,9},{9,13},{13,5},{5,1},{2,10},{10,14}... | collective-permute-start | bytes 786440 | tf_op jit(solution)/shard_map/ppermute | solution.py:501
  18.3 18.3 %collective-permute-start.8 = (bf16[2,2,8,64,128]{4,3,2,1,0:T(8,128)(2,1)S(1)}, bf16[2,2,8,64,128]{4,3,2,1,0:T(8,128)(2,1)S(1)}, u32[]{:S(2)}, u32[]{:S(2)}) collective-permute-start(bf16[2,2,8,64,128]{4,3,2,1,0:T(8,128)(2,1)S(1)} %pad_maximum_fusion.refs_3_), channel_id=1, source_target_pairs={{0,2},{2,0},{1,3},{3,1},{4,6},{6,4},{5,7},{7,5},{8,10},{10,8},{9,1... | collective-permute-start | bytes 1572872 | tf_op jit(solution)/shard_map/ppermute | solution.py:492
  22.9 11.2 %collective-permute-start.10 = (bf16[64,2048]{1,0:T(8,128)(2,1)S(1)}, bf16[64,2048]{1,0:T(8,128)(2,1)S(1)}, u32[]{:S(2)}, u32[]{:S(2)}) collective-permute-start(bf16[64,2048]{1,0:T(8,128)(2,1)S(1)} %collective-permute-done.5.refs_1_), channel_id=1, source_target_pairs={{0,8},{8,12},{12,4},{4,0},{1,9},{9,13},{13,5},{5,1},{2,10},{10,14}... | collective-permute-start | bytes 786440 | tf_op jit(solution)/shard_map/ppermute | solution.py:501
  27.5 18.9 %collective-permute-start.13 = (bf16[128,1280]{1,0:T(8,128)(2,1)S(1)}, bf16[128,1280]{1,0:T(8,128)(2,1)S(1)}, u32[]{:S(2)}, u32[]{:S(2)}) collective-permute-start(bf16[128,1280]{1,0:T(8,128)(2,1)S(1)} %get-tuple-element.59), channel_id=1, source_target_pairs={{0,1},{1,0},{2,3},{3,2},{4,5},{5,4},{6,7},{7,6},{8,9},{9,8},{10,11... | collective-permute-start | bytes 983048 | tf_op jit(solution)/shard_map/ppermute | solution.py:495
  28.5 11.2 %collective-permute-start.6 = (bf16[64,2048]{1,0:T(8,128)(2,1)S(1)}, bf16[64,2048]{1,0:T(8,128)(2,1)S(1)}, u32[]{:S(2)}, u32[]{:S(2)}) collective-permute-start(bf16[64,2048]{1,0:T(8,128)(2,1)S(1)} %collective-permute-done.2.refs_2_), channel_id=1, source_target_pairs={{0,8},{8,12},{12,4},{4,0},{1,9},{9,13},{13,5},{5,1},{2,10},{10,14}... | collective-permute-start | bytes 786440 | tf_op jit(solution)/shard_map/ppermute | solution.py:501
  34.1 10.8 %collective-permute-start.11 = (bf16[64,2048]{1,0:T(8,128)(2,1)S(1)}, bf16[64,2048]{1,0:T(8,128)(2,1)S(1)}, u32[]{:S(2)}, u32[]{:S(2)}) collective-permute-start(bf16[64,2048]{1,0:T(8,128)(2,1)S(1)} %collective-permute-done.10.refs_0_), channel_id=1, source_target_pairs={{0,8},{8,12},{12,4},{4,0},{1,9},{9,13},{13,5},{5,1},{2,10},{10,14}... | collective-permute-start | bytes 786440 | tf_op jit(solution)/shard_map/ppermute | solution.py:501
  43.2 10.4 %collective-permute-start.9 = (bf16[256,1280]{1,0:T(8,128)(2,1)S(1)}, bf16[256,1280]{1,0:T(8,128)(2,1)S(1)}, u32[]{:S(2)}, u32[]{:S(2)}) collective-permute-start(bf16[256,1280]{1,0:T(8,128)(2,1)S(1)} %get-tuple-element.71), channel_id=1, source_target_pairs={{0,1},{1,0},{2,3},{3,2},{4,5},{5,4},{6,7},{7,6},{8,9},{9,8},{10,11... | collective-permute-start | bytes 1966088 | tf_op jit(solution)/shard_map/ppermute | solution.py:495
  46.5 10.6 %collective-permute-start.14 = (bf16[128,1280]{1,0:T(8,128)(2,1)S(1)}, bf16[128,1280]{1,0:T(8,128)(2,1)S(1)}, u32[]{:S(2)}, u32[]{:S(2)}) collective-permute-start(bf16[128,1280]{1,0:T(8,128)(2,1)S(1)} %add_convert_fusion), channel_id=1, source_target_pairs={{0,2},{2,0},{1,3},{3,1},{4,6},{6,4},{5,7},{7,5},{8,10},{10,8},{9,1... | collective-permute-start | bytes 983048 | tf_op jit(solution)/shard_map/ppermute | solution.py:492
  49.6 14.1 %collective-permute-start.15 = (bf16[128,1280]{1,0:T(8,128)(2,1)S(1)}, bf16[128,1280]{1,0:T(8,128)(2,1)S(1)}, u32[]{:S(2)}, u32[]{:S(2)}) collective-permute-start(bf16[128,1280]{1,0:T(8,128)(2,1)S(1)} %add_convert_fusion.1), channel_id=1, source_target_pairs={{0,2},{2,0},{1,3},{3,1},{4,6},{6,4},{5,7},{7,5},{8,10},{10,8},{9,1... | collective-permute-start | bytes 983048 | tf_op jit(solution)/shard_map/ppermute | solution.py:492
  66.6 8.7 %collective-permute-start.22 = (bf16[128,1024]{1,0:T(8,128)(2,1)S(1)}, bf16[128,1024]{1,0:T(8,128)(2,1)S(1)}, u32[]{:S(2)}, u32[]{:S(2)}) collective-permute-start(bf16[128,1024]{1,0:T(8,128)(2,1)S(1)} %attend.2.own_ref), channel_id=1, source_target_pairs={{0,2},{2,0},{1,3},{3,1},{4,6},{6,4},{5,7},{7,5},{8,10},{10,8},{9,1... | collective-permute-start | bytes 786440 | tf_op jit(solution)/shard_map/ppermute | solution.py:492
  75.3 8.7 %collective-permute-start.20 = (bf16[128,1024]{1,0:T(8,128)(2,1)S(1)}, bf16[128,1024]{1,0:T(8,128)(2,1)S(1)}, u32[]{:S(2)}, u32[]{:S(2)}) collective-permute-start(bf16[128,1024]{1,0:T(8,128)(2,1)S(1)} %attend.3.own_ref), channel_id=1, source_target_pairs={{0,2},{2,0},{1,3},{3,1},{4,6},{6,4},{5,7},{7,5},{8,10},{10,8},{9,1... | collective-permute-start | bytes 786440 | tf_op jit(solution)/shard_map/ppermute | solution.py:492
  76.8 9.1 %collective-permute-start.17 = (bf16[64,2048]{1,0:T(8,128)(2,1)S(1)}, bf16[64,2048]{1,0:T(8,128)(2,1)S(1)}, u32[]{:S(2)}, u32[]{:S(2)}) collective-permute-start(bf16[64,2048]{1,0:T(8,128)(2,1)S(1)} %get-tuple-element.76), channel_id=1, source_target_pairs={{0,8},{8,12},{12,4},{4,0},{1,9},{9,13},{13,5},{5,1},{2,10},{10,14}... | collective-permute-start | bytes 786440 | tf_op jit(solution)/shard_map/ppermute | solution.py:501
  79.3 10.4 %collective-permute-start.19 = (bf16[128,1024]{1,0:T(8,128)(2,1)S(1)}, bf16[128,1024]{1,0:T(8,128)(2,1)S(1)}, u32[]{:S(2)}, u32[]{:S(2)}) collective-permute-start(bf16[128,1024]{1,0:T(8,128)(2,1)S(1)} %attend.3.own_ref), channel_id=1, source_target_pairs={{0,1},{1,0},{2,3},{3,2},{4,5},{5,4},{6,7},{7,6},{8,9},{9,8},{10,11... | collective-permute-start | bytes 786440 | tf_op jit(solution)/shard_map/ppermute | solution.py:495
  81.1 10.5 %collective-permute-start.24 = (bf16[64,2048]{1,0:T(8,128)(2,1)S(1)}, bf16[64,2048]{1,0:T(8,128)(2,1)S(1)}, u32[]{:S(2)}, u32[]{:S(2)}) collective-permute-start(bf16[64,2048]{1,0:T(8,128)(2,1)S(1)} %get-tuple-element.85), channel_id=1, source_target_pairs={{0,8},{8,12},{12,4},{4,0},{1,9},{9,13},{13,5},{5,1},{2,10},{10,14}... | collective-permute-start | bytes 786440 | tf_op jit(solution)/shard_map/ppermute | solution.py:501
  86.0 8.9 %collective-permute-start.21 = (bf16[128,1024]{1,0:T(8,128)(2,1)S(1)}, bf16[128,1024]{1,0:T(8,128)(2,1)S(1)}, u32[]{:S(2)}, u32[]{:S(2)}) collective-permute-start(bf16[128,1024]{1,0:T(8,128)(2,1)S(1)} %collective-permute-done.20.own_ref), channel_id=1, source_target_pairs={{0,1},{1,0},{2,3},{3,2},{4,5},{5,4},{6,7},{7,6},{8,9},{9,8},{10,11... | collective-permute-start | bytes 786440 | tf_op jit(solution)/shard_map/ppermute | solution.py:495
  86.0 11.4 %collective-permute-start.18 = (bf16[64,2048]{1,0:T(8,128)(2,1)S(1)}, bf16[64,2048]{1,0:T(8,128)(2,1)S(1)}, u32[]{:S(2)}, u32[]{:S(2)}) collective-permute-start(bf16[64,2048]{1,0:T(8,128)(2,1)S(1)} %add_convert_fusion.6), channel_id=1, source_target_pairs={{0,8},{8,12},{12,4},{4,0},{1,9},{9,13},{13,5},{5,1},{2,10},{10,14}... | collective-permute-start | bytes 786440 | tf_op jit(solution)/shard_map/ppermute | solution.py:501
  91.6 11.2 %collective-permute-start.27 = (bf16[64,2048]{1,0:T(8,128)(2,1)S(1)}, bf16[64,2048]{1,0:T(8,128)(2,1)S(1)}, u32[]{:S(2)}, u32[]{:S(2)}) collective-permute-start(bf16[64,2048]{1,0:T(8,128)(2,1)S(1)} %add_convert_fusion.3), channel_id=1, source_target_pairs={{0,8},{8,12},{12,4},{4,0},{1,9},{9,13},{13,5},{5,1},{2,10},{10,14}... | collective-permute-start | bytes 786440 | tf_op jit(solution)/shard_map/ppermute | solution.py:501
  96.7 11.9 %collective-permute-start.31 = (bf16[32,2048]{1,0:T(8,128)(2,1)S(1)}, bf16[32,2048]{1,0:T(8,128)(2,1)S(1)}, u32[]{:S(2)}, u32[]{:S(2)}) collective-permute-start(bf16[32,2048]{1,0:T(8,128)(2,1)S(1)} %get-tuple-element.95), channel_id=1, source_target_pairs={{0,3},{1,2},{2,1},{3,0},{4,7},{5,6},{6,5},{7,4},{8,11},{9,10},{10,... | collective-permute-start | bytes 393224 | tf_op jit(solution)/shard_map/ppermute | solution.py:498
  96.8 11.8 %collective-permute-start.29 = (bf16[32,2048]{1,0:T(8,128)(2,1)S(1)}, bf16[32,2048]{1,0:T(8,128)(2,1)S(1)}, u32[]{:S(2)}, u32[]{:S(2)}) collective-permute-start(bf16[32,2048]{1,0:T(8,128)(2,1)S(1)} %get-tuple-element.96), channel_id=1, source_target_pairs={{0,2},{2,0},{1,3},{3,1},{4,6},{6,4},{5,7},{7,5},{8,10},{10,8},{9,1... | collective-permute-start | bytes 393224 | tf_op jit(solution)/shard_map/ppermute | solution.py:492
  97.5 10.9 %collective-permute-start.25 = (bf16[64,2048]{1,0:T(8,128)(2,1)S(1)}, bf16[64,2048]{1,0:T(8,128)(2,1)S(1)}, u32[]{:S(2)}, u32[]{:S(2)}) collective-permute-start(bf16[64,2048]{1,0:T(8,128)(2,1)S(1)} %add_convert_fusion.5), channel_id=1, source_target_pairs={{0,8},{8,12},{12,4},{4,0},{1,9},{9,13},{13,5},{5,1},{2,10},{10,14}... | collective-permute-start | bytes 786440 | tf_op jit(solution)/shard_map/ppermute | solution.py:501
  104.8 8.5 %collective-permute-start.28 = (bf16[32,2048]{1,0:T(8,128)(2,1)S(1)}, bf16[32,2048]{1,0:T(8,128)(2,1)S(1)}, u32[]{:S(2)}, u32[]{:S(2)}) collective-permute-start(bf16[32,2048]{1,0:T(8,128)(2,1)S(1)} %get-tuple-element.92), channel_id=1, source_target_pairs={{0,10},{1,11},{2,8},{3,9},{8,14},{9,15},{10,12},{11,13},{12,6},{13... | collective-permute-start | bytes 393224 | tf_op jit(solution)/shard_map/ppermute | solution.py:506
  (13 other events, 72.4 us)

commit v6 on v5

--- a/solution.py
+++ b/solution.py
@@ -1,4 +1,5 @@
 import functools
+import math
 
 import jax
 import jax.numpy as jnp
@@ -361,7 +362,7 @@
     blocks, length = chip_ref.shape[2:4]
     heads = total_cols // head_dim - 2
     q_cols = heads * head_dim
-    scale = head_dim**-0.5
+    scale = head_dim**-0.5 * math.log2(math.e)
     stack = min(heads, max(1, 256 // some))
     chain = CHAIN_BLOCKS * length
 
@@ -406,7 +407,7 @@
         segments = seg_ref[pl.ds(group, 1), :]
         root = jnp.int32(0)
         keys, values = [branch(root, 0)], [branch(root, 1)]
-        bias = [jnp.zeros((some, chain), jnp.float32)]
+        bias = []
         same = None
         low = jnp.int32(0)
         for s in range(steps):
@@ -445,9 +446,10 @@
             scores = lax.dot_general(
                 query, keys, (((1,), (1,)), ((), ())), preferred_element_type=jnp.float32
             )
-            scores = scores * scale + bias
+            scores = scores * scale
+            scores = jnp.concatenate((scores[:, :chain], scores[:, chain:] + bias), axis=1)
             top = jnp.max(scores, axis=1, keepdims=True)
-            weights = jnp.exp(scores - top)
+            weights = jnp.exp2(scores - top)
             total = jnp.sum(weights, axis=1, keepdims=True)
             summed = jnp.dot(
                 weights.astype(jnp.bfloat16), values, preferred_element_type=jnp.float32
@@ -549,9 +551,9 @@
         far_pieces.append(onward(far_pieces[step]))
     first_terms = summed(*far_first, jnp.bfloat16)
 
-    near_terms = project(place, after(near_pieces, away), weights, (True, False), kinds)
+    near_terms = project(place, near_pieces, weights, (True, False), kinds)
     keep = (summed(*near_terms, jnp.float32),)
-    pieces = after(far_pieces[2:], near_terms)
+    pieces = after(far_pieces[2:], near_terms, away)
     sent = project(place, pieces, weights, (True,), kinds[:1])
     kept = project(place, pieces, weights, (False,), kinds[1:])
     last_terms = summed(*sent, *kept, jnp.bfloat16)

time: 115 us -> 115 us (level)
  starting transfers between devices: 42.2 us -> 44.3 us
  waiting for transfers between devices: 37.7 us -> 35.7 us
    ppermute x11, starting transfers between devices: 27.9 us -> 29.5 us  [onward(): return lax.ppermute(x, 'tp', forward)]
    ppermute x11, waiting for transfers between devices: 18.3 us -> 16.9 us  [onward(): return lax.ppermute(x, 'tp', forward)]
  transfers between devices with their start and end apart: 32 -> 32, of which waited for: 15 -> 13; matrix products, arithmetic and copies ran while one was open for 1% -> 1% of each run, Pallas kernels for 23% -> 23%
where the time goes in v6:
time: 115 us
  starting transfers between devices  44.3 us (39%)
  waiting for transfers between devices  35.7 us (31%)
  Pallas kernels  31.6 us (27%)
  local copies, waits for them, and re-layouts  1.8 us (2%)
    ppermute x11, starting transfers between devices, onward(): return lax.ppermute(x, 'tp', forward)  29.5 us
    ppermute x11, waiting for transfers between devices, onward(): return lax.ppermute(x, 'tp', forward)  16.9 us
    ppermute x7, waiting for transfers between devices, swap_req(): return lax.ppermute(x, 'req', SWAP)  13.8 us
    ppermute x7, starting transfers between devices, swap_req(): return lax.ppermute(x, 'req', SWAP)  9.94 us
    pallas_call x4, Pallas kernels, project(): pl.pallas_call(functools.partial(project_kernel, flips), in_specs=[pl.Blo...  8.57 us
    pallas_call x2, Pallas kernels, load(): pl.pallas_call(functools.partial(load_kernel, count), in_specs=[pl.BlockS...  7.32 us
    pallas_call x4, Pallas kernels, out_project(): pl.pallas_call(out_kernel, in_specs=[pl.BlockSpec(memory_space=pltpu.SMEM...  7.24 us
    pallas_call x2, Pallas kernels, attend(): pl.pallas_call(functools.partial(attend_kernel, wanted, order, len(keep))...  5.52 us
  transfers between devices with their start and end apart: 32, of which 13 were waited for; matrix products, arithmetic and copies ran while one was open for 1% of the time, Pallas kernels for 23%

profile of v6, /device:TPU:0, one launch (start us, length us, event | category | flops | bytes accessed | tf_op | source)
XLA Modules:
  0.0 114.7 jit_solution(427954994208143588)
XLA Ops:
  3.2 2.6 %collective-permute-start.3 = (bf16[32,2048]{1,0:T(8,128)(2,1)S(1)}, bf16[32,2048]{1,0:T(8,128)(2,1)S(1)}, u32[]{:S(2)}, u32[]{:S(2)}) collective-permute-start(bf16[32,2048]{1,0:T(8,128)(2,1)S(1)} %get-tuple-element.46), channel_id=1, source_target_pairs={{0,2},{2,0},{1,3},{3,1},{4,6},{6,4},{5,7},{7,5},{8,10},{10,8},{9,1... | collective-permute-start | bytes 393224 | tf_op jit(solution)/shard_map/ppermute | solution.py:494
  6.0 2.9 %collective-permute-start.1 = (bf16[64,2048]{1,0:T(8,128)(2,1)S(1)}, bf16[64,2048]{1,0:T(8,128)(2,1)S(1)}, u32[]{:S(2)}, u32[]{:S(2)}) collective-permute-start(bf16[64,2048]{1,0:T(8,128)(2,1)S(1)} %maximum_select_fusion.refs_0_), channel_id=1, source_target_pairs={{0,8},{8,12},{12,4},{4,0},{1,9},{9,13},{13,5},{5,1},{2,10},{10,14}... | collective-permute-start | bytes 786440 | tf_op jit(solution)/shard_map/ppermute | solution.py:503
  8.8 3.9 %load.2 = (bf16[2048,2048]{1,0:T(8,128)(2,1)S(1)}, bf16[2048,256]{1,0:T(8,128)(2,1)S(1)}, bf16[2048,256]{1,0:T(8,128)(2,1)S(1)}) custom-call(bf16[2048,2048]{1,0:T(8,128)(2,1)} %refs_0_, bf16[2048,256]{1,0:T(8,128)(2,1)} %refs_1_, bf16[2048,256]{1,0:T(8,128)(2,1)} %refs_2_), custom_call_target="tpu_custom_call" | custom-call | tf_op jit(solution)/shard_map/load/pallas_call | solution.py:210
  12.9 2.4 %collective-permute-start.5 = (bf16[64,2048]{1,0:T(8,128)(2,1)S(1)}, bf16[64,2048]{1,0:T(8,128)(2,1)S(1)}, u32[]{:S(2)}, u32[]{:S(2)}) collective-permute-start(bf16[64,2048]{1,0:T(8,128)(2,1)S(1)} %maximum_select_fusion.1.refs_0_), channel_id=1, source_target_pairs={{0,8},{8,12},{12,4},{4,0},{1,9},{9,13},{13,5},{5,1},{2,10},{10,14}... | collective-permute-start | bytes 786440 | tf_op jit(solution)/shard_map/ppermute | solution.py:503
  18.3 3.8 %collective-permute-done.5.refs_1_ = bf16[64,2048]{1,0:T(8,128)(2,1)S(1)} collective-permute-done((bf16[64,2048]{1,0:T(8,128)(2,1)S(1)}, bf16[64,2048]{1,0:T(8,128)(2,1)S(1)}, u32[]{:S(2)}, u32[]{:S(2)}) %collective-permute-start.5) | collective-permute-done | bytes 262176 | tf_op jit(solution)/shard_map/ppermute | solution.py:503
  22.1 3.1 %collective-permute-start.8 = (bf16[64,2048]{1,0:T(8,128)(2,1)S(1)}, bf16[64,2048]{1,0:T(8,128)(2,1)S(1)}, u32[]{:S(2)}, u32[]{:S(2)}) collective-permute-start(bf16[64,2048]{1,0:T(8,128)(2,1)S(1)} %collective-permute-done.5.refs_1_), channel_id=1, source_target_pairs={{0,8},{8,12},{12,4},{4,0},{1,9},{9,13},{13,5},{5,1},{2,10},{10,14}... | collective-permute-start | bytes 786440 | tf_op jit(solution)/shard_map/ppermute | solution.py:503
  26.8 2.2 %project.4 = (bf16[128,1280]{1,0:T(8,128)(2,1)S(1)}, f32[128,1280]{1,0:T(8,128)S(1)}) custom-call(s32[3]{0:T(128)S(1)} %pad_add_fusion.place_ref, bf16[64,2048]{1,0:T(8,128)(2,1)S(1)} %maximum_select_fusion.1.refs_0_, bf16[64,2048]{1,0:T(8,128)(2,1)S(1)} %collective-permute-done.5.refs_1_, bf16[2048,2048]{1,0:T(8,128)(2,1)S(1)} %get-tuple-element.51.refs_2_.refs_4_, ...), custom_call_target="tpu_custom_call" | custom-call | tf_op jit(solution)/shard_map/project/pallas_call | solution.py:305
  30.8 2.2 %collective-permute-done.8.refs_0_ = bf16[64,2048]{1,0:T(8,128)(2,1)S(1)} collective-permute-done((bf16[64,2048]{1,0:T(8,128)(2,1)S(1)}, bf16[64,2048]{1,0:T(8,128)(2,1)S(1)}, u32[]{:S(2)}, u32[]{:S(2)}) %collective-permute-start.8) | collective-permute-done | bytes 262176 | tf_op jit(solution)/shard_map/ppermute | solution.py:503
  33.1 3.4 %collective-permute-start.9 = (bf16[64,2048]{1,0:T(8,128)(2,1)S(1)}, bf16[64,2048]{1,0:T(8,128)(2,1)S(1)}, u32[]{:S(2)}, u32[]{:S(2)}) collective-permute-start(bf16[64,2048]{1,0:T(8,128)(2,1)S(1)} %collective-permute-done.8.refs_0_), channel_id=1, source_target_pairs={{0,8},{8,12},{12,4},{4,0},{1,9},{9,13},{13,5},{5,1},{2,10},{10,14}... | collective-permute-start | bytes 786440 | tf_op jit(solution)/shard_map/ppermute | solution.py:503
  36.4 2.2 %collective-permute-done.6.refs_3_ = bf16[64,2048]{1,0:T(8,128)(2,1)S(1)} collective-permute-done((bf16[64,2048]{1,0:T(8,128)(2,1)S(1)}, bf16[64,2048]{1,0:T(8,128)(2,1)S(1)}, u32[]{:S(2)}, u32[]{:S(2)}) %collective-permute-start.6) | collective-permute-done | bytes 262176 | tf_op jit(solution)/shard_map/ppermute | solution.py:503
  38.7 3.5 %project.5 = (bf16[256,1280]{1,0:T(8,128)(2,1)S(1)}, f32[256,1280]{1,0:T(8,128)S(1)}) custom-call(s32[3]{0:T(128)S(1)} %pad_add_fusion.place_ref, bf16[64,2048]{1,0:T(8,128)(2,1)S(1)} %maximum_select_fusion.refs_0_, bf16[64,2048]{1,0:T(8,128)(2,1)S(1)} %collective-permute-done.1.refs_1_, bf16[64,2048]{1,0:T(8,128)(2,1)S(1)} %collective-permute-done.2.refs_2_, ...), custom_call_target="tpu_custom_call" | custom-call | tf_op jit(solution)/shard_map/project/pallas_call | solution.py:305
  49.3 3.4 %load.3.w_ref = bf16[2048,2048]{1,0:T(8,128)(2,1)S(1)} custom-call(bf16[2048,2048]{1,0:T(8,128)(2,1)} %refs_0_.1), custom_call_target="tpu_custom_call" | custom-call | tf_op jit(solution)/shard_map/load/pallas_call | solution.py:210
  52.9 3.3 %collective-permute-done.14.refs_1_ = bf16[128,1280]{1,0:T(8,128)(2,1)S(1)} collective-permute-done((bf16[128,1280]{1,0:T(8,128)(2,1)S(1)}, bf16[128,1280]{1,0:T(8,128)(2,1)S(1)}, u32[]{:S(2)}, u32[]{:S(2)}) %collective-permute-start.14) | collective-permute-done | bytes 327712 | tf_op jit(solution)/shard_map/ppermute | solution.py:494
  56.2 6.6 %collective-permute-done.15.refs_2_ = bf16[128,1280]{1,0:T(8,128)(2,1)S(1)} collective-permute-done((bf16[128,1280]{1,0:T(8,128)(2,1)S(1)}, bf16[128,1280]{1,0:T(8,128)(2,1)S(1)}, u32[]{:S(2)}, u32[]{:S(2)}) %collective-permute-start.15) | collective-permute-done | bytes 327712 | tf_op jit(solution)/shard_map/ppermute | solution.py:494
  62.8 2.8 %attend.2.own_ref = bf16[128,1024]{1,0:T(8,128)(2,1)S(1)} custom-call(s32[3]{0:T(128)S(1)} %pad_add_fusion.place_ref, s32[4,2,8]{2,1,0:T(2,128)S(1)} %copy-done.3, s32[4,128]{1,0:T(4,128)S(1)} %copy-done.4, f32[256,1280]{1,0:T(8,128)S(1)} %convert_add_fusion.refs_0_, bf16[128,1280]{1,0:T(8,128)(2,1)S(1)} %collective-permute-done.14.refs_1_, ...), custom_call_target="tpu_custom_call" | custom-call | tf_op jit(solution)/shard_map/attend/pallas_call | solution.py:469
  69.0 2.8 %attend.3.own_ref = bf16[128,1024]{1,0:T(8,128)(2,1)S(1)} custom-call(s32[3]{0:T(128)S(1)} %pad_add_fusion.place_ref, s32[4,2,8]{2,1,0:T(2,128)S(1)} %copy-done.3, s32[4,128]{1,0:T(4,128)S(1)} %copy-done.4, f32[256,1280]{1,0:T(8,128)S(1)} %convert_add_fusion.refs_0_, bf16[128,1280]{1,0:T(8,128)(2,1)S(1)} %collective-permute-done.14.refs_1_, ...), custom_call_target="tpu_custom_call" | custom-call | tf_op jit(solution)/shard_map/attend/pallas_call | solution.py:469
  71.8 2.6 %collective-permute-done.22.own_ref = bf16[128,1024]{1,0:T(8,128)(2,1)S(1)} collective-permute-done((bf16[128,1024]{1,0:T(8,128)(2,1)S(1)}, bf16[128,1024]{1,0:T(8,128)(2,1)S(1)}, u32[]{:S(2)}, u32[]{:S(2)}) %collective-permute-start.22) | collective-permute-done | bytes 262176 | tf_op jit(solution)/shard_map/ppermute | solution.py:494
  75.9 3.4 %collective-permute-start.17 = (bf16[64,2048]{1,0:T(8,128)(2,1)S(1)}, bf16[64,2048]{1,0:T(8,128)(2,1)S(1)}, u32[]{:S(2)}, u32[]{:S(2)}) collective-permute-start(bf16[64,2048]{1,0:T(8,128)(2,1)S(1)} %get-tuple-element.68), channel_id=1, source_target_pairs={{0,8},{8,12},{12,4},{4,0},{1,9},{9,13},{13,5},{5,1},{2,10},{10,14}... | collective-permute-start | bytes 786440 | tf_op jit(solution)/shard_map/ppermute | solution.py:503
  83.1 2.8 %collective-permute-done.17 = bf16[64,2048]{1,0:T(8,128)(2,1)S(1)} collective-permute-done((bf16[64,2048]{1,0:T(8,128)(2,1)S(1)}, bf16[64,2048]{1,0:T(8,128)(2,1)S(1)}, u32[]{:S(2)}, u32[]{:S(2)}) %collective-permute-start.17) | collective-permute-done | bytes 262176 | tf_op jit(solution)/shard_map/ppermute | solution.py:503
  86.0 3.7 %collective-permute-start.18 = (bf16[64,2048]{1,0:T(8,128)(2,1)S(1)}, bf16[64,2048]{1,0:T(8,128)(2,1)S(1)}, u32[]{:S(2)}, u32[]{:S(2)}) collective-permute-start(bf16[64,2048]{1,0:T(8,128)(2,1)S(1)} %add_convert_fusion.6), channel_id=1, source_target_pairs={{0,8},{8,12},{12,4},{4,0},{1,9},{9,13},{13,5},{5,1},{2,10},{10,14}... | collective-permute-start | bytes 786440 | tf_op jit(solution)/shard_map/ppermute | solution.py:503
  91.5 3.3 %collective-permute-start.27 = (bf16[64,2048]{1,0:T(8,128)(2,1)S(1)}, bf16[64,2048]{1,0:T(8,128)(2,1)S(1)}, u32[]{:S(2)}, u32[]{:S(2)}) collective-permute-start(bf16[64,2048]{1,0:T(8,128)(2,1)S(1)} %add_convert_fusion.3), channel_id=1, source_target_pairs={{0,8},{8,12},{12,4},{4,0},{1,9},{9,13},{13,5},{5,1},{2,10},{10,14}... | collective-permute-start | bytes 786440 | tf_op jit(solution)/shard_map/ppermute | solution.py:503
  97.4 3.0 %collective-permute-start.25 = (bf16[64,2048]{1,0:T(8,128)(2,1)S(1)}, bf16[64,2048]{1,0:T(8,128)(2,1)S(1)}, u32[]{:S(2)}, u32[]{:S(2)}) collective-permute-start(bf16[64,2048]{1,0:T(8,128)(2,1)S(1)} %add_convert_fusion.5), channel_id=1, source_target_pairs={{0,8},{8,12},{12,4},{4,0},{1,9},{9,13},{13,5},{5,1},{2,10},{10,14}... | collective-permute-start | bytes 786440 | tf_op jit(solution)/shard_map/ppermute | solution.py:503
  108.4 2.6 %collective-permute-done.30.refs_4_ = bf16[32,2048]{1,0:T(8,128)(2,1)S(1)} collective-permute-done((bf16[32,2048]{1,0:T(8,128)(2,1)S(1)}, bf16[32,2048]{1,0:T(8,128)(2,1)S(1)}, u32[]{:S(2)}, u32[]{:S(2)}) %collective-permute-start.30) | collective-permute-done | bytes 131104 | tf_op jit(solution)/shard_map/ppermute | solution.py:508
  111.0 2.3 %collective-permute-done.28.refs_2_ = bf16[32,2048]{1,0:T(8,128)(2,1)S(1)} collective-permute-done((bf16[32,2048]{1,0:T(8,128)(2,1)S(1)}, bf16[32,2048]{1,0:T(8,128)(2,1)S(1)}, u32[]{:S(2)}, u32[]{:S(2)}) %collective-permute-start.28) | collective-permute-done | bytes 131104 | tf_op jit(solution)/shard_map/ppermute | solution.py:508
  (81 shorter events, 39.7 us)
Async XLA Ops:
  3.2 9.5 %collective-permute-start.3 = (bf16[32,2048]{1,0:T(8,128)(2,1)S(1)}, bf16[32,2048]{1,0:T(8,128)(2,1)S(1)}, u32[]{:S(2)}, u32[]{:S(2)}) collective-permute-start(bf16[32,2048]{1,0:T(8,128)(2,1)S(1)} %get-tuple-element.46), channel_id=1, source_target_pairs={{0,2},{2,0},{1,3},{3,1},{4,6},{6,4},{5,7},{7,5},{8,10},{10,8},{9,1... | collective-permute-start | bytes 393224 | tf_op jit(solution)/shard_map/ppermute | solution.py:494
  6.0 10.4 %collective-permute-start.1 = (bf16[64,2048]{1,0:T(8,128)(2,1)S(1)}, bf16[64,2048]{1,0:T(8,128)(2,1)S(1)}, u32[]{:S(2)}, u32[]{:S(2)}) collective-permute-start(bf16[64,2048]{1,0:T(8,128)(2,1)S(1)} %maximum_select_fusion.refs_0_), channel_id=1, source_target_pairs={{0,8},{8,12},{12,4},{4,0},{1,9},{9,13},{13,5},{5,1},{2,10},{10,14}... | collective-permute-start | bytes 786440 | tf_op jit(solution)/shard_map/ppermute | solution.py:503
  12.9 9.2 %collective-permute-start.5 = (bf16[64,2048]{1,0:T(8,128)(2,1)S(1)}, bf16[64,2048]{1,0:T(8,128)(2,1)S(1)}, u32[]{:S(2)}, u32[]{:S(2)}) collective-permute-start(bf16[64,2048]{1,0:T(8,128)(2,1)S(1)} %maximum_select_fusion.1.refs_0_), channel_id=1, source_target_pairs={{0,8},{8,12},{12,4},{4,0},{1,9},{9,13},{13,5},{5,1},{2,10},{10,14}... | collective-permute-start | bytes 786440 | tf_op jit(solution)/shard_map/ppermute | solution.py:503
  16.0 9.2 %collective-permute-start.10 = (bf16[2,8,64,128]{3,2,1,0:T(8,128)(2,1)S(1)}, bf16[2,8,64,128]{3,2,1,0:T(8,128)(2,1)S(1)}, u32[]{:S(2)}, u32[]{:S(2)}) collective-permute-start(bf16[2,8,64,128]{3,2,1,0:T(8,128)(2,1)S(1)} %get-tuple-element.63), channel_id=1, source_target_pairs={{0,1},{1,0},{2,3},{3,2},{4,5},{5,4},{6,7},{7,6},{8,9},{9,8},{10,11... | collective-permute-start | bytes 786440 | tf_op jit(solution)/shard_map/ppermute | solution.py:497
  16.3 12.8 %collective-permute-start.2 = (bf16[64,2048]{1,0:T(8,128)(2,1)S(1)}, bf16[64,2048]{1,0:T(8,128)(2,1)S(1)}, u32[]{:S(2)}, u32[]{:S(2)}) collective-permute-start(bf16[64,2048]{1,0:T(8,128)(2,1)S(1)} %collective-permute-done.1.refs_1_), channel_id=1, source_target_pairs={{0,8},{8,12},{12,4},{4,0},{1,9},{9,13},{13,5},{5,1},{2,10},{10,14}... | collective-permute-start | bytes 786440 | tf_op jit(solution)/shard_map/ppermute | solution.py:503
  22.1 11.0 %collective-permute-start.8 = (bf16[64,2048]{1,0:T(8,128)(2,1)S(1)}, bf16[64,2048]{1,0:T(8,128)(2,1)S(1)}, u32[]{:S(2)}, u32[]{:S(2)}) collective-permute-start(bf16[64,2048]{1,0:T(8,128)(2,1)S(1)} %collective-permute-done.5.refs_1_), channel_id=1, source_target_pairs={{0,8},{8,12},{12,4},{4,0},{1,9},{9,13},{13,5},{5,1},{2,10},{10,14}... | collective-permute-start | bytes 786440 | tf_op jit(solution)/shard_map/ppermute | solution.py:503
  25.3 18.7 %collective-permute-start.11 = (bf16[2,2,8,64,128]{4,3,2,1,0:T(8,128)(2,1)S(1)}, bf16[2,2,8,64,128]{4,3,2,1,0:T(8,128)(2,1)S(1)}, u32[]{:S(2)}, u32[]{:S(2)}) collective-permute-start(bf16[2,2,8,64,128]{4,3,2,1,0:T(8,128)(2,1)S(1)} %pad_maximum_fusion.refs_3_), channel_id=1, source_target_pairs={{0,2},{2,0},{1,3},{3,1},{4,6},{6,4},{5,7},{7,5},{8,10},{10,8},{9,1... | collective-permute-start | bytes 1572872 | tf_op jit(solution)/shard_map/ppermute | solution.py:494
  29.0 16.6 %collective-permute-start.13 = (bf16[128,1280]{1,0:T(8,128)(2,1)S(1)}, bf16[128,1280]{1,0:T(8,128)(2,1)S(1)}, u32[]{:S(2)}, u32[]{:S(2)}) collective-permute-start(bf16[128,1280]{1,0:T(8,128)(2,1)S(1)} %get-tuple-element.55), channel_id=1, source_target_pairs={{0,1},{1,0},{2,3},{3,2},{4,5},{5,4},{6,7},{7,6},{8,9},{9,8},{10,11... | collective-permute-start | bytes 983048 | tf_op jit(solution)/shard_map/ppermute | solution.py:497
  29.1 9.6 %collective-permute-start.6 = (bf16[64,2048]{1,0:T(8,128)(2,1)S(1)}, bf16[64,2048]{1,0:T(8,128)(2,1)S(1)}, u32[]{:S(2)}, u32[]{:S(2)}) collective-permute-start(bf16[64,2048]{1,0:T(8,128)(2,1)S(1)} %collective-permute-done.2.refs_2_), channel_id=1, source_target_pairs={{0,8},{8,12},{12,4},{4,0},{1,9},{9,13},{13,5},{5,1},{2,10},{10,14}... | collective-permute-start | bytes 786440 | tf_op jit(solution)/shard_map/ppermute | solution.py:503
  33.1 10.9 %collective-permute-start.9 = (bf16[64,2048]{1,0:T(8,128)(2,1)S(1)}, bf16[64,2048]{1,0:T(8,128)(2,1)S(1)}, u32[]{:S(2)}, u32[]{:S(2)}) collective-permute-start(bf16[64,2048]{1,0:T(8,128)(2,1)S(1)} %collective-permute-done.8.refs_0_), channel_id=1, source_target_pairs={{0,8},{8,12},{12,4},{4,0},{1,9},{9,13},{13,5},{5,1},{2,10},{10,14}... | collective-permute-start | bytes 786440 | tf_op jit(solution)/shard_map/ppermute | solution.py:503
  42.2 10.6 %collective-permute-start.7 = (bf16[256,1280]{1,0:T(8,128)(2,1)S(1)}, bf16[256,1280]{1,0:T(8,128)(2,1)S(1)}, u32[]{:S(2)}, u32[]{:S(2)}) collective-permute-start(bf16[256,1280]{1,0:T(8,128)(2,1)S(1)} %get-tuple-element.59), channel_id=1, source_target_pairs={{0,1},{1,0},{2,3},{3,2},{4,5},{5,4},{6,7},{7,6},{8,9},{9,8},{10,11... | collective-permute-start | bytes 1966088 | tf_op jit(solution)/shard_map/ppermute | solution.py:497
  45.6 10.6 %collective-permute-start.14 = (bf16[128,1280]{1,0:T(8,128)(2,1)S(1)}, bf16[128,1280]{1,0:T(8,128)(2,1)S(1)}, u32[]{:S(2)}, u32[]{:S(2)}) collective-permute-start(bf16[128,1280]{1,0:T(8,128)(2,1)S(1)} %add_convert_fusion), channel_id=1, source_target_pairs={{0,2},{2,0},{1,3},{3,1},{4,6},{6,4},{5,7},{7,5},{8,10},{10,8},{9,1... | collective-permute-start | bytes 983048 | tf_op jit(solution)/shard_map/ppermute | solution.py:494
  48.7 14.1 %collective-permute-start.15 = (bf16[128,1280]{1,0:T(8,128)(2,1)S(1)}, bf16[128,1280]{1,0:T(8,128)(2,1)S(1)}, u32[]{:S(2)}, u32[]{:S(2)}) collective-permute-start(bf16[128,1280]{1,0:T(8,128)(2,1)S(1)} %add_convert_fusion.1), channel_id=1, source_target_pairs={{0,2},{2,0},{1,3},{3,1},{4,6},{6,4},{5,7},{7,5},{8,10},{10,8},{9,1... | collective-permute-start | bytes 983048 | tf_op jit(solution)/shard_map/ppermute | solution.py:494
  65.6 8.7 %collective-permute-start.22 = (bf16[128,1024]{1,0:T(8,128)(2,1)S(1)}, bf16[128,1024]{1,0:T(8,128)(2,1)S(1)}, u32[]{:S(2)}, u32[]{:S(2)}) collective-permute-start(bf16[128,1024]{1,0:T(8,128)(2,1)S(1)} %attend.2.own_ref), channel_id=1, source_target_pairs={{0,2},{2,0},{1,3},{3,1},{4,6},{6,4},{5,7},{7,5},{8,10},{10,8},{9,1... | collective-permute-start | bytes 786440 | tf_op jit(solution)/shard_map/ppermute | solution.py:494
  74.4 8.7 %collective-permute-start.20 = (bf16[128,1024]{1,0:T(8,128)(2,1)S(1)}, bf16[128,1024]{1,0:T(8,128)(2,1)S(1)}, u32[]{:S(2)}, u32[]{:S(2)}) collective-permute-start(bf16[128,1024]{1,0:T(8,128)(2,1)S(1)} %attend.3.own_ref), channel_id=1, source_target_pairs={{0,2},{2,0},{1,3},{3,1},{4,6},{6,4},{5,7},{7,5},{8,10},{10,8},{9,1... | collective-permute-start | bytes 786440 | tf_op jit(solution)/shard_map/ppermute | solution.py:494
  75.9 10.0 %collective-permute-start.17 = (bf16[64,2048]{1,0:T(8,128)(2,1)S(1)}, bf16[64,2048]{1,0:T(8,128)(2,1)S(1)}, u32[]{:S(2)}, u32[]{:S(2)}) collective-permute-start(bf16[64,2048]{1,0:T(8,128)(2,1)S(1)} %get-tuple-element.68), channel_id=1, source_target_pairs={{0,8},{8,12},{12,4},{4,0},{1,9},{9,13},{13,5},{5,1},{2,10},{10,14}... | collective-permute-start | bytes 786440 | tf_op jit(solution)/shard_map/ppermute | solution.py:503
  79.2 10.4 %collective-permute-start.19 = (bf16[128,1024]{1,0:T(8,128)(2,1)S(1)}, bf16[128,1024]{1,0:T(8,128)(2,1)S(1)}, u32[]{:S(2)}, u32[]{:S(2)}) collective-permute-start(bf16[128,1024]{1,0:T(8,128)(2,1)S(1)} %attend.3.own_ref), channel_id=1, source_target_pairs={{0,1},{1,0},{2,3},{3,2},{4,5},{5,4},{6,7},{7,6},{8,9},{9,8},{10,11... | collective-permute-start | bytes 786440 | tf_op jit(solution)/shard_map/ppermute | solution.py:497
  81.1 10.4 %collective-permute-start.24 = (bf16[64,2048]{1,0:T(8,128)(2,1)S(1)}, bf16[64,2048]{1,0:T(8,128)(2,1)S(1)}, u32[]{:S(2)}, u32[]{:S(2)}) collective-permute-start(bf16[64,2048]{1,0:T(8,128)(2,1)S(1)} %get-tuple-element.77), channel_id=1, source_target_pairs={{0,8},{8,12},{12,4},{4,0},{1,9},{9,13},{13,5},{5,1},{2,10},{10,14}... | collective-permute-start | bytes 786440 | tf_op jit(solution)/shard_map/ppermute | solution.py:503
  85.9 8.9 %collective-permute-start.21 = (bf16[128,1024]{1,0:T(8,128)(2,1)S(1)}, bf16[128,1024]{1,0:T(8,128)(2,1)S(1)}, u32[]{:S(2)}, u32[]{:S(2)}) collective-permute-start(bf16[128,1024]{1,0:T(8,128)(2,1)S(1)} %collective-permute-done.20.own_ref), channel_id=1, source_target_pairs={{0,1},{1,0},{2,3},{3,2},{4,5},{5,4},{6,7},{7,6},{8,9},{9,8},{10,11... | collective-permute-start | bytes 786440 | tf_op jit(solution)/shard_map/ppermute | solution.py:497
  86.0 11.4 %collective-permute-start.18 = (bf16[64,2048]{1,0:T(8,128)(2,1)S(1)}, bf16[64,2048]{1,0:T(8,128)(2,1)S(1)}, u32[]{:S(2)}, u32[]{:S(2)}) collective-permute-start(bf16[64,2048]{1,0:T(8,128)(2,1)S(1)} %add_convert_fusion.6), channel_id=1, source_target_pairs={{0,8},{8,12},{12,4},{4,0},{1,9},{9,13},{13,5},{5,1},{2,10},{10,14}... | collective-permute-start | bytes 786440 | tf_op jit(solution)/shard_map/ppermute | solution.py:503
  91.5 11.0 %collective-permute-start.27 = (bf16[64,2048]{1,0:T(8,128)(2,1)S(1)}, bf16[64,2048]{1,0:T(8,128)(2,1)S(1)}, u32[]{:S(2)}, u32[]{:S(2)}) collective-permute-start(bf16[64,2048]{1,0:T(8,128)(2,1)S(1)} %add_convert_fusion.3), channel_id=1, source_target_pairs={{0,8},{8,12},{12,4},{4,0},{1,9},{9,13},{13,5},{5,1},{2,10},{10,14}... | collective-permute-start | bytes 786440 | tf_op jit(solution)/shard_map/ppermute | solution.py:503
  96.7 11.7 %collective-permute-start.31 = (bf16[32,2048]{1,0:T(8,128)(2,1)S(1)}, bf16[32,2048]{1,0:T(8,128)(2,1)S(1)}, u32[]{:S(2)}, u32[]{:S(2)}) collective-permute-start(bf16[32,2048]{1,0:T(8,128)(2,1)S(1)} %get-tuple-element.87), channel_id=1, source_target_pairs={{0,3},{1,2},{2,1},{3,0},{4,7},{5,6},{6,5},{7,4},{8,11},{9,10},{10,... | collective-permute-start | bytes 393224 | tf_op jit(solution)/shard_map/ppermute | solution.py:500
  96.8 11.6 %collective-permute-start.29 = (bf16[32,2048]{1,0:T(8,128)(2,1)S(1)}, bf16[32,2048]{1,0:T(8,128)(2,1)S(1)}, u32[]{:S(2)}, u32[]{:S(2)}) collective-permute-start(bf16[32,2048]{1,0:T(8,128)(2,1)S(1)} %get-tuple-element.88), channel_id=1, source_target_pairs={{0,2},{2,0},{1,3},{3,1},{4,6},{6,4},{5,7},{7,5},{8,10},{10,8},{9,1... | collective-permute-start | bytes 393224 | tf_op jit(solution)/shard_map/ppermute | solution.py:494
  97.4 10.7 %collective-permute-start.25 = (bf16[64,2048]{1,0:T(8,128)(2,1)S(1)}, bf16[64,2048]{1,0:T(8,128)(2,1)S(1)}, u32[]{:S(2)}, u32[]{:S(2)}) collective-permute-start(bf16[64,2048]{1,0:T(8,128)(2,1)S(1)} %add_convert_fusion.5), channel_id=1, source_target_pairs={{0,8},{8,12},{12,4},{4,0},{1,9},{9,13},{13,5},{5,1},{2,10},{10,14}... | collective-permute-start | bytes 786440 | tf_op jit(solution)/shard_map/ppermute | solution.py:503
  (13 other events, 81.5 us)
